TPU v7x, 256 devices: a whole 4x4x8 slice. The times are simulated.
256 devices in a mesh: dp: 32 (over x_lo, z, core), tm: 8 (over y, x_hi).
Axes of the slice: x: 4 (x_hi: 2, x_lo: 2; x = x_hi * 2 + x_lo), y: 4, z: 8, core: 2. Of those that a mesh axis runs over, the one named last changes fastest.
Arguments:
- clips: bfloat16 [32, 32, 16, 64, 128], P('dp', 'tm'), may hold values from -6 to 6
- cotangent: bfloat16 [32, 16, 8, 32, 256], P('dp', 'tm'), may hold values from -6 to 6
- clip_frames: int32 [32], P('dp'), may hold values from 1 to 32, 768 in all
- w_conv: bfloat16 [3, 3, 3, 128, 128], replicated, may hold values from -0.109375 to 0.109375
- w_down: bfloat16 [3, 3, 3, 128, 256], replicated, may hold values from -0.109375 to 0.109375
Outputs:
- encoded: bfloat16 [32, 16, 8, 32, 256], P('dp', 'tm')
- clip_grad: bfloat16 [32, 32, 16, 64, 128], P('dp', 'tm')
- conv_grad: float32 [3, 3, 3, 128, 128], replicated
- down_grad: float32 [3, 3, 3, 128, 256], replicated
All inputs are finite; a program needn't handle non-finite values. No bound on the sum of `clip_frames` on one device may be relied on, other than what follows from the above.
Results may differ from a plain program's by a relative error of at most 0.013.
Values may be sent and summed in bfloat16 or wider, within the bound.
No kernel may reach another device: no remote copies, remote signals or barrier semaphores. Data moves between devices by JAX's collectives and lax.ppermute only.
A program may use at most 128 MiB of HBM per device.

v0:
```python
import math

import jax
import jax.numpy as jnp
from jax import lax
from jax.sharding import PartitionSpec as P

LAYOUT = ("NDHWC", "DHWIO", "NDHWC")


def shifted(block, axis, distance):
    devices = range(lax.axis_size(axis))
    route = [(i - distance, i) for i in devices if i - distance in devices]
    return lax.ppermute(block, axis, route)


def convolve(lhs, rhs, strides, padding, dilation):
    return lax.conv_general_dilated(
        lhs,
        rhs,
        strides,
        padding,
        lhs_dilation=dilation,
        dimension_numbers=LAYOUT,
        preferred_element_type=jnp.float32,
    )


def flipped(weight):
    return jnp.swapaxes(weight[::-1, ::-1, ::-1], 3, 4)


def kernel_sums(padded, grad, step):
    extent = [step * (grad.shape[d] - 1) + 3 for d in range(3)]
    trimmed = padded[: extent[0], : extent[1], : extent[2]]
    result = lax.conv_general_dilated(
        trimmed[None],
        grad[None],
        (1, 1, 1),
        "VALID",
        rhs_dilation=(step, step, step),
        dimension_numbers=("CDHWN", "IDHWO", "NDHWC"),
        preferred_element_type=jnp.float32,
    )
    return jnp.transpose(result, (1, 2, 3, 0, 4))


def shards(clips, cotangent, clip_frames, w_conv, w_down):
    frames = clips.shape[1]
    rows = clips.shape[2]
    cols = clips.shape[3]
    spatial = [(1, 1), (1, 1)]
    before = shifted(clips[:, frames - 2 :], "tm", 1)
    x_ext = jnp.concatenate([before, clips], axis=1)
    hidden = convolve(x_ext, w_conv, (1, 1, 1), [(0, 0)] + spatial, (1, 1, 1))
    act = jax.nn.silu(hidden).astype(jnp.bfloat16)
    act_before = shifted(act[:, frames - 2 :], "tm", 1)
    act_ext = jnp.concatenate([act_before, act], axis=1)
    encoded = convolve(act_ext, w_down, (2, 2, 2), [(0, 0)] + spatial, (1, 1, 1)).astype(
        jnp.bfloat16
    )
    times = lax.axis_index("tm") * (frames // 2) + jnp.arange(frames // 2, dtype=jnp.int32)
    keep = (2 * times < clip_frames[0])[None, :, None, None, None]
    masked = jnp.where(keep, cotangent, jnp.zeros_like(cotangent))
    scale = 1.0 / math.sqrt(lax.axis_size("dp") * frames * lax.axis_size("tm") * rows * cols)
    act_grad_ext = convolve(masked, flipped(w_down), (1, 1, 1), [(2, 3), (1, 2), (1, 2)], (2, 2, 2))
    returned = shifted(act_grad_ext[:, :2], "tm", -1)
    act_grad = act_grad_ext[:, 2:] + jnp.pad(
        returned, ((0, 0), (frames - 2, 0), (0, 0), (0, 0), (0, 0))
    )
    sig = jax.nn.sigmoid(hidden)
    hidden_grad = (act_grad * sig * (1.0 + hidden * (1.0 - sig))).astype(jnp.bfloat16)
    apad = jnp.pad(act_ext[0], ((0, 0), (1, 1), (1, 1), (0, 0)))
    down_local = kernel_sums(apad, masked[0], 2)
    clip_grad_ext = convolve(hidden_grad, flipped(w_conv), (1, 1, 1), [(2, 2)] + spatial, (1, 1, 1))
    back = shifted(clip_grad_ext[:, :2].astype(jnp.bfloat16), "tm", -1).astype(jnp.float32)
    clip_grad = (
        clip_grad_ext[:, 2:] + jnp.pad(back, ((0, 0), (frames - 2, 0), (0, 0), (0, 0), (0, 0)))
    ).astype(jnp.bfloat16)
    xpad = jnp.pad(x_ext[0], ((0, 0), (1, 1), (1, 1), (0, 0)))
    conv_local = kernel_sums(xpad, hidden_grad[0], 1)
    conv_sum, down_sum = lax.psum((conv_local, down_local), ("dp", "tm"))
    return (encoded, clip_grad, conv_sum * scale, down_sum * scale)


def solution(mesh):
    in_specs = (P("dp", "tm", None, None, None), P("dp", "tm", None, None, None), P("dp"), P(), P())
    out_specs = (P("dp", "tm", None, None, None), P("dp", "tm", None, None, None), P(), P())
    return jax.shard_map(shards, mesh=mesh, in_specs=in_specs, out_specs=out_specs, check_vma=False)
```

profile of v0, /device:TPU:1, one launch (start us, length us, event | category | flops | bytes accessed | tf_op | source)
XLA Modules:
  0.0 398.9 jit_solution(6928499431412351991)
XLA Ops:
  7.2 1.2 slice.47
  8.8 5.5 %collective-permute-start = (bf16[1,2,16,64,128]{4,2,3,1,0:T(8,128)(2,1)S(1)}, bf16[1,2,16,64,128]{4,2,3,1,0:T(8,128)(2,1)S(1)}, u32[]{:S(2)}, u32[]{:S(2)}) collective-permute-start(bf16[1,2,16,64,128]{4,2,3,1,0:T(8,128)(2,1)S(1)} %copy.56), channel_id=1, source_target_pairs={{0,1},{1,2},{2,3},{3,4},{4,5},{5,6},{6,7},{8,9},{9,10},{10,11},{11... | collective-permute-start | bytes 1572872 | tf_op jit(solution)/shard_map/ppermute | solution.py:14
  15.4 3.6 convolution_select_fusion
  19.6 1.9 collective-permute-start.2
  21.5 3.3 collective-permute-done
  27.2 9.5 %add_divide_fusion = (f32[4,16,8,9,128]{4,2,3,1,0:T(8,128)S(1)}, bf16[4,16,8,9,128]{4,2,3,1,0:T(8,128)(2,1)S(1)}, f32[4,16,8,9,128]{4,2,3,1,0:T(8,128)S(1)}) fusion(pred[8,9]{0,1:T(8,128)(4,1)S(1)} %copy-done.12, bf16[3,3,3,128,128]{4,3,2,1,0:T(8,128)(2,1)S(1)} %copy-done.10, bf16[6,16,1,7,2,128]{5,3,4,1,0,2:T(8,128)(2,1)S(1)} %slice.48, ...), kind=kOutput, calls=%fused_computation.20 | convolution fusion | flops 3918790656 | bytes 8896584 | tf_op jit(solution)/shard_map/conv_general_dilated | solution.py:18
  36.9 5.8 %collective-permute-start.1 = (bf16[1,2,16,64,128]{4,2,3,1,0:T(8,128)(2,1)S(1)}, bf16[1,2,16,64,128]{4,2,3,1,0:T(8,128)(2,1)S(1)}, u32[]{:S(2)}, u32[]{:S(2)}) collective-permute-start(bf16[1,2,16,64,128]{4,2,3,1,0:T(8,128)(2,1)S(1)} %slice_bitcast_fusion.7), channel_id=1, source_target_pairs={{0,1},{1,2},{2,3},{3,4},{4,5},{5,6},{6,7},{8,9},{9,10},{10,11},{11... | collective-permute-start | bytes 1572872 | tf_op jit(solution)/shard_map/ppermute | solution.py:14
  42.7 0.9 copy_select_fusion
  43.8 0.8 copy.22
  45.6 2.3 pad_bitcast_fusion
  48.2 4.0 collective-permute-done.1
  52.1 1.4 fusion.43
  53.5 2.1 fusion.28
  56.1 38.4 %fusion.2 = f32[3,3,3,128,128]{4,3,2,1,0:T(8,128)} fusion(bf16[1,6,18,66,128]{4,2,3,1,0:T(8,128)(2,1)} %pad_bitcast_fusion, bf16[1,4,16,64,128]{4,2,3,1,0:T(8,128)(2,1)S(1)} %fusion.24), kind=kOutput, calls=%fused_computation.4 | convolution fusion | flops 3623878656 | bytes 4642816 | tf_op jit(solution)/shard_map/transpose | solution.py:45
  94.5 8.6 %fusion.5 = f32[3,3,3,128,256]{4,3,2,1,0:T(8,128)} fusion(bf16[1,5,17,65,128]{4,2,3,1,0:T(8,128)(2,1)S(1)} %copy-done.5, bf16[1,2,8,32,256]{4,2,3,1,0:T(8,128)(2,1)S(1)} %copy-done.9), kind=kOutput, calls=%fused_computation.8 | convolution fusion | flops 905969664 | bytes 5215488 | tf_op jit(solution)/shard_map/transpose | solution.py:45
  103.1 1.2 copy-done.3
  106.5 13.8 %convolution_select_fusion.1 = f32[6,16,8,9,128]{4,2,3,1,0:T(8,128)S(1)} fusion(bf16[3,3,3,128,128]{4,3,2,1,0:T(8,128)(2,1)S(1)} %copy-done.11, pred[8,9]{0,1:T(8,128)(4,1)S(1)} %copy-done.13, bf16[4,16,1,7,2,128]{5,3,4,1,0,2:T(8,128)(2,1)S(1)} %slice.61, bf16[4,16,1,8,9,128]{5,3,4,1,0,2:T(8,128)(2,1)S(1)} %copy.29), kind=kOutput, calls=%fused_computation.40 | convolution fusion | flops 3912204288 | bytes 5832776 | tf_op jit(solution)/shard_map/conv_general_dilated | solution.py:18
  121.1 1.7 collective-permute-start.3
  124.0 1.4 fusion.38
  126.3 17.2 %collective-permute-done.3 = bf16[1,2,16,64,128]{4,2,3,1,0:T(8,128)(2,1)S(1)} collective-permute-done((bf16[1,2,16,64,128]{4,2,3,1,0:T(8,128)(2,1)S(1)}, bf16[1,2,16,64,128]{4,2,3,1,0:T(8,128)(2,1)S(1)}, u32[]{:S(2)}, u32[]{:S(2)}) %collective-permute-start.3) | collective-permute-done | bytes 524320 | tf_op jit(solution)/shard_map/ppermute | solution.py:14
  143.6 1.2 copy.39
  144.9 241.3 %all-reduce.7.cloned.1.call-done = (f32[3,3,3,128,128]{4,3,2,1,0:T(8,128)}, f32[3,3,3,128,256]{4,3,2,1,0:T(8,128)}) async-done(((f32[3,3,3,128,128]{4,3,2,1,0:T(8,128)}, f32[3,3,3,128,256]{4,3,2,1,0:T(8,128)}), (f32[3,3,3,128,128]{4,3,2,1,0:T(8,128)}, f32[3,3,3,128,256]{4,3,2,1,0:T(8,128)})) %all-reduce.7.cloned.1.call-update) | async-done | bytes 5308432 | tf_op jit(solution)/shard_map/psum | solution.py:82
  386.2 4.3 %broadcast_multiply_fusion = f32[3,3,3,128,256]{4,3,2,1,0:T(8,128)} fusion(f32[3,3,3,128,256]{4,3,2,1,0:T(8,128)} %get-tuple-element.9), kind=kLoop, calls=%fused_computation.41 | loop fusion | flops 884736 | bytes 7077888 | tf_op jit(solution)/shard_map/mul | solution.py:83
  390.5 1.3 broadcast_multiply_fusion.1
  (73 shorter events, 10.6 us)
Async XLA Ops:
  7.2 8.2 %copy-start = (bf16[3,3,3,128,256]{4,3,2,1,0:T(8,128)(2,1)S(1)}, bf16[3,3,3,128,256]{4,3,2,1,0:T(8,128)(2,1)}, u32[]{:S(2)}) copy-start(bf16[3,3,3,128,256]{4,3,2,1,0:T(8,128)(2,1)} %param.9) | copy-start | bytes 5308420
  7.2 8.2 %copy-start.7 = (pred[8,10]{0,1:T(8,128)(4,1)S(1)}, pred[8,10]{0,1:T(8,128)(4,1)}, u32[]{:S(2)}) copy-start(pred[8,10]{0,1:T(8,128)(4,1)} %constant.51) | copy-start | bytes 244
  7.2 7.8 %copy-start.8 = (bf16[1,2,8,32,256]{4,3,2,1,0:T(8,128)(2,1)S(1)}, bf16[1,2,8,32,256]{4,3,2,1,0:T(8,128)(2,1)}, u32[]{:S(2)}) copy-start(bf16[1,2,8,32,256]{4,3,2,1,0:T(8,128)(2,1)} %param.6) | copy-start | bytes 786436
  7.2 379.0 %all-reduce.7.cloned.1.call-start = ((), (), s32[]{:S(2)}) async-start(), calls=%async_computation | async-start | bytes 10616832 | tf_op jit(solution)/shard_map/psum | solution.py:82
  8.8 16.1 %collective-permute-start = (bf16[1,2,16,64,128]{4,2,3,1,0:T(8,128)(2,1)S(1)}, bf16[1,2,16,64,128]{4,2,3,1,0:T(8,128)(2,1)S(1)}, u32[]{:S(2)}, u32[]{:S(2)}) collective-permute-start(bf16[1,2,16,64,128]{4,2,3,1,0:T(8,128)(2,1)S(1)} %copy.56), channel_id=1, source_target_pairs={{0,1},{1,2},{2,3},{3,4},{4,5},{5,6},{6,7},{8,9},{9,10},{10,11},{11... | collective-permute-start | bytes 1572872 | tf_op jit(solution)/shard_map/ppermute | solution.py:14
  19.5 5.4 %copy-start.4 = (bf16[1,4,16,64,128]{4,3,2,1,0:T(8,128)(2,1)S(1)}, bf16[1,4,16,64,128]{4,3,2,1,0:T(8,128)(2,1)}, u32[]{:S(2)}) copy-start(bf16[1,4,16,64,128]{4,3,2,1,0:T(8,128)(2,1)} %param.5) | copy-start | bytes 3145732
  19.6 36.0 %collective-permute-start.2 = (f32[1,2,16,64,128]{4,2,3,1,0:T(8,128)S(1)}, f32[1,2,16,64,128]{4,2,3,1,0:T(8,128)S(1)}, u32[]{:S(2)}, u32[]{:S(2)}) collective-permute-start(f32[1,2,16,64,128]{4,2,3,1,0:T(8,128)S(1)} %slice_bitcast_fusion.4), channel_id=1, source_target_pairs={{1,0},{2,1},{3,2},{4,3},{5,4},{6,5},{7,6},{9,8},{10,9},{11,10},{12... | collective-permute-start | bytes 3145736 | tf_op jit(solution)/shard_map/ppermute | solution.py:14
  26.0 1.2 copy-start.10
  26.0 1.2 copy-start.12
  36.9 15.3 %collective-permute-start.1 = (bf16[1,2,16,64,128]{4,2,3,1,0:T(8,128)(2,1)S(1)}, bf16[1,2,16,64,128]{4,2,3,1,0:T(8,128)(2,1)S(1)}, u32[]{:S(2)}, u32[]{:S(2)}) collective-permute-start(bf16[1,2,16,64,128]{4,2,3,1,0:T(8,128)(2,1)S(1)} %slice_bitcast_fusion.7), channel_id=1, source_target_pairs={{0,1},{1,2},{2,3},{3,4},{4,5},{5,6},{6,7},{8,9},{9,10},{10,11},{11... | collective-permute-start | bytes 1572872 | tf_op jit(solution)/shard_map/ppermute | solution.py:14
  56.1 38.4 %copy-start.2 = (bf16[1,4,16,64,128]{4,2,3,1,0:T(8,128)(2,1)}, bf16[1,4,16,64,128]{4,2,3,1,0:T(8,128)(2,1)S(1)}, u32[]{:S(2)}) copy-start(bf16[1,4,16,64,128]{4,2,3,1,0:T(8,128)(2,1)S(1)} %fusion.24) | copy-start | bytes 3145732
  56.1 38.4 %copy-start.5 = (bf16[1,5,17,65,128]{4,2,3,1,0:T(8,128)(2,1)S(1)}, bf16[1,5,17,65,128]{4,2,3,1,0:T(8,128)(2,1)}, u32[]{:S(2)}) copy-start(bf16[1,5,17,65,128]{4,2,3,1,0:T(8,128)(2,1)} %fusion.28) | copy-start | bytes 4243204
  56.1 38.4 %copy-start.9 = (bf16[1,2,8,32,256]{4,2,3,1,0:T(8,128)(2,1)S(1)}, bf16[1,2,8,32,256]{4,2,3,1,0:T(8,128)(2,1)}, u32[]{:S(2)}) copy-start(bf16[1,2,8,32,256]{4,2,3,1,0:T(8,128)(2,1)} %copy_select_fusion) | copy-start | bytes 786436
  103.1 1.2 copy-start.3
  105.3 1.2 copy-start.11
  105.3 1.2 copy-start.13
  121.0 1.8 copy-start.1
  121.1 22.3 %collective-permute-start.3 = (bf16[1,2,16,64,128]{4,2,3,1,0:T(8,128)(2,1)S(1)}, bf16[1,2,16,64,128]{4,2,3,1,0:T(8,128)(2,1)S(1)}, u32[]{:S(2)}, u32[]{:S(2)}) collective-permute-start(bf16[1,2,16,64,128]{4,2,3,1,0:T(8,128)(2,1)S(1)} %slice_bitcast_fusion.6), channel_id=1, source_target_pairs={{1,0},{2,1},{3,2},{4,3},{5,4},{6,5},{7,6},{9,8},{10,9},{11,10},{12... | collective-permute-start | bytes 1572872 | tf_op jit(solution)/shard_map/ppermute | solution.py:14
  123.1 0.9 copy-start.14
  386.2 4.3 %copy-start.6 = (f32[3,3,3,128,128]{4,3,2,1,0:T(8,128)S(1)}, f32[3,3,3,128,128]{4,3,2,1,0:T(8,128)}, u32[]{:S(2)}) copy-start(f32[3,3,3,128,128]{4,3,2,1,0:T(8,128)} %get-tuple-element.8) | copy-start | bytes 5308420
Sparse Core Ops, SparseCore 0:
  103.3 282.8 all-reduce.6
where the time goes:
time: 404 us; the launch traced here: 399 us
  waiting for transfers between devices  266 us (66%)
  matrix products  75.3 us (19%)
  local copies, waits for them, and re-layouts  18.6 us (5%)
  between operations  15.5 us (4%)
  starting transfers between devices  15 us (4%)
  other arithmetic  8.71 us (2%)
    psum x1, waiting for transfers between devices, shards(): conv_sum, down_sum = lax.psum((conv_local, down_local), ('dp', 'tm'))  241 us
    transpose x2, matrix products, kernel_sums(): return jnp.transpose(result, (1, 2, 3, 0, 4))  47 us
    conv_general_dilated x4, matrix products, convolve(): lax.conv_general_dilated(lhs, rhs, strides, padding, lhs_dilation=dilatio...  28.3 us
    ppermute x4, waiting for transfers between devices, shifted(): return lax.ppermute(block, axis, route)  24.5 us
    ppermute x4, starting transfers between devices, shifted(): return lax.ppermute(block, axis, route)  14.9 us
  transfers between devices with their start and end apart: 5, of which 4 were waited for; matrix products, arithmetic and copies ran while one was open for 11% of the time, Pallas kernels for 0%

commit v1 on v0

v1 whole, which is shorter than its diff:
```python
import math

import jax
import jax.numpy as jnp
from jax import lax
from jax.sharding import Mesh
from jax.sharding import PartitionSpec as P

LAYOUT = ("NDHWC", "DHWIO", "NDHWC")
TM = ("y", "xh")
DP = ("xl", "z", "c")
XY = ("xl", "xh", "y")


def shifted(block, distance):
    devices = range(8)
    route = [(i - distance, i) for i in devices if i - distance in devices]
    return lax.ppermute(block, TM, route)


def convolve(lhs, rhs, strides, padding, dilation):
    return lax.conv_general_dilated(
        lhs,
        rhs,
        strides,
        padding,
        lhs_dilation=dilation,
        dimension_numbers=LAYOUT,
        preferred_element_type=jnp.float32,
    )


def flipped(weight):
    return jnp.swapaxes(weight[::-1, ::-1, ::-1], 3, 4)


def kernel_sums(padded, grad, step):
    extent = [step * (grad.shape[d] - 1) + 3 for d in range(3)]
    trimmed = padded[: extent[0], : extent[1], : extent[2]]
    result = lax.conv_general_dilated(
        trimmed[None],
        grad[None],
        (1, 1, 1),
        "VALID",
        rhs_dilation=(step, step, step),
        dimension_numbers=("CDHWN", "IDHWO", "NDHWC"),
        preferred_element_type=jnp.float32,
    )
    return jnp.transpose(result, (1, 2, 3, 0, 4))


def exchange(value, axes):
    return lax.all_to_all(value, axes, 0, 0, tiled=True)


def add_up(value, parts):
    split = value.reshape((parts, value.shape[0] // parts, 128))
    return jnp.sum(split.astype(jnp.float32), axis=0).astype(jnp.bfloat16)


def gather(value, axes, parts):
    return exchange(jnp.tile(value, (parts, 1)), axes)


def total(rows):
    part = add_up(exchange(rows.astype(jnp.bfloat16), "c"), 2)
    part = add_up(exchange(part, XY), 16)
    part = add_up(gather(part, "z", 8), 8)
    return gather(gather(part, XY, 16), "c", 2)


def shards(clips, cotangent, clip_frames, w_conv, w_down):
    frames = clips.shape[1]
    rows = clips.shape[2]
    cols = clips.shape[3]
    spatial = [(1, 1), (1, 1)]
    before = shifted(clips[:, frames - 2 :], 1)
    x_ext = jnp.concatenate([before, clips], axis=1)
    hidden = convolve(x_ext, w_conv, (1, 1, 1), [(0, 0)] + spatial, (1, 1, 1))
    act = jax.nn.silu(hidden).astype(jnp.bfloat16)
    act_before = shifted(act[:, frames - 2 :], 1)
    act_ext = jnp.concatenate([act_before, act], axis=1)
    encoded = convolve(act_ext, w_down, (2, 2, 2), [(0, 0)] + spatial, (1, 1, 1)).astype(
        jnp.bfloat16
    )
    times = lax.axis_index(TM) * (frames // 2) + jnp.arange(frames // 2, dtype=jnp.int32)
    keep = (2 * times < clip_frames[0])[None, :, None, None, None]
    masked = jnp.where(keep, cotangent, jnp.zeros_like(cotangent))
    scale = 1.0 / math.sqrt(lax.axis_size(DP) * frames * lax.axis_size(TM) * rows * cols)
    act_grad_ext = convolve(masked, flipped(w_down), (1, 1, 1), [(2, 3), (1, 2), (1, 2)], (2, 2, 2))
    returned = shifted(act_grad_ext[:, :2], -1)
    act_grad = act_grad_ext[:, 2:] + jnp.pad(
        returned, ((0, 0), (frames - 2, 0), (0, 0), (0, 0), (0, 0))
    )
    sig = jax.nn.sigmoid(hidden)
    hidden_grad = (act_grad * sig * (1.0 + hidden * (1.0 - sig))).astype(jnp.bfloat16)
    apad = jnp.pad(act_ext[0], ((0, 0), (1, 1), (1, 1), (0, 0)))
    down_local = kernel_sums(apad, masked[0], 2)
    clip_grad_ext = convolve(hidden_grad, flipped(w_conv), (1, 1, 1), [(2, 2)] + spatial, (1, 1, 1))
    back = shifted(clip_grad_ext[:, :2].astype(jnp.bfloat16), -1).astype(jnp.float32)
    clip_grad = (
        clip_grad_ext[:, 2:] + jnp.pad(back, ((0, 0), (frames - 2, 0), (0, 0), (0, 0), (0, 0)))
    ).astype(jnp.bfloat16)
    xpad = jnp.pad(x_ext[0], ((0, 0), (1, 1), (1, 1), (0, 0)))
    conv_local = kernel_sums(xpad, hidden_grad[0], 1)
    down_rows = jnp.concatenate(
        [down_local[..., :128].reshape(-1, 128), down_local[..., 128:].reshape(-1, 128)]
    )
    down_sum = total(jnp.pad(down_rows, ((0, 256), (0, 0))))
    conv_sum = total(jnp.pad(conv_local.reshape(-1, 128), ((0, 128), (0, 0))))
    conv_sum = conv_sum[:3456].reshape(3, 3, 3, 128, 128).astype(jnp.float32)
    down_sum = jnp.concatenate(
        [
            down_sum[:3456].reshape(3, 3, 3, 128, 128),
            down_sum[3456:6912].reshape(3, 3, 3, 128, 128),
        ],
        axis=-1,
    ).astype(jnp.float32)
    return (encoded, clip_grad, conv_sum * scale, down_sum * scale)


def solution(mesh):
    fine = Mesh(mesh.devices.reshape(2, 8, 2, 4, 2), DP + TM)
    spread = P(DP, TM, None, None, None)
    in_specs = (spread, spread, P(DP), P(), P())
    out_specs = (spread, spread, P(), P())
    return jax.shard_map(shards, mesh=fine, in_specs=in_specs, out_specs=out_specs, check_vma=False)
```

time: 404 us -> 269 us (0.67)
  waiting for transfers between devices: 266 us -> 49.9 us
  starting transfers between devices: 15 us -> 71.2 us
  blocking collectives: 0 us -> 14.3 us
  local copies, waits for them, and re-layouts: 18.6 us -> 32.3 us
  between operations: 15.5 us -> 2.01 us
  other arithmetic: 8.71 us -> 20.2 us
    psum x1 -> x0, waiting for transfers between devices: 241 us -> none  [shards(): conv_sum, down_sum = lax.psum((conv_local, down_local), ('dp', 'tm'))]
    all_to_all x0 -> x8, starting transfers between devices: none -> 57.1 us  [exchange(): return lax.all_to_all(value, axes, 0, 0, tiled=True)]
    all_to_all x0 -> x8, waiting for transfers between devices: none -> 45.1 us  [exchange(): return lax.all_to_all(value, axes, 0, 0, tiled=True)]
    ppermute x4, waiting for transfers between devices: 24.5 us -> 4.84 us  [shifted(): return lax.ppermute(block, TM, route)]
    all_to_all x0 -> x2, blocking collectives: none -> 14.3 us  [exchange(): return lax.all_to_all(value, axes, 0, 0, tiled=True)]
    reduce_sum x0 -> x6, other arithmetic: none -> 6.73 us  [add_up(): return jnp.sum(split.astype(jnp.float32), axis=0).astype(jnp.bfloat16)]
    another operation x2 -> x8, local copies, waits for them, and re-layouts: 0.16 us -> 4.82 us  [the longest x6 4.66 us: gather(): return exchange(jnp.tile(value, (parts, 1)), axes)]
    transpose x2, matrix products: 47 us -> 42.6 us  [kernel_sums(): return jnp.transpose(result, (1, 2, 3, 0, 4))]
  transfers between devices with their start and end apart: 5 -> 12, of which waited for: 4 -> 10; matrix products, arithmetic and copies ran while one was open for 11% -> 28% of each run, Pallas kernels for 0% -> 0%
where the time goes in v1:
time: 269 us; the launch traced here: 264 us
  matrix products  73.7 us (27%)
  starting transfers between devices  71.2 us (26%)
  waiting for transfers between devices  49.9 us (19%)
  local copies, waits for them, and re-layouts  32.3 us (12%)
  other arithmetic  20.2 us (8%)
  blocking collectives  14.3 us (5%)
    all_to_all x8, starting transfers between devices, exchange(): return lax.all_to_all(value, axes, 0, 0, tiled=True)  57.1 us
    all_to_all x8, waiting for transfers between devices, exchange(): return lax.all_to_all(value, axes, 0, 0, tiled=True)  45.1 us
    transpose x2, matrix products, kernel_sums(): return jnp.transpose(result, (1, 2, 3, 0, 4))  42.6 us
    conv_general_dilated x4, matrix products, convolve(): lax.conv_general_dilated(lhs, rhs, strides, padding, lhs_dilation=dilatio...  31.1 us
    all_to_all x2, blocking collectives, exchange(): return lax.all_to_all(value, axes, 0, 0, tiled=True)  14.3 us
    ppermute x4, starting transfers between devices, shifted(): return lax.ppermute(block, TM, route)  14.1 us
    conv_general_dilated x14, local copies, waits for them, and re-layouts, convolve(): lax.conv_general_dilated(lhs, rhs, strides, padding, lhs_dilation=dilatio...  7.55 us
    reduce_sum x6, other arithmetic, add_up(): return jnp.sum(split.astype(jnp.float32), axis=0).astype(jnp.bfloat16)  6.73 us
  transfers between devices with their start and end apart: 12, of which 10 were waited for; matrix products, arithmetic and copies ran while one was open for 28% of the time, Pallas kernels for 0%

profile of v1, /device:TPU:1, one launch (start us, length us, event | category | flops | bytes accessed | tf_op | source)
XLA Modules:
  0.0 263.7 jit_solution(6224470415390447738)
XLA Ops:
  2.2 5.5 %collective-permute-start = (bf16[1,2,16,64,128]{4,2,3,1,0:T(8,128)(2,1)S(1)}, bf16[1,2,16,64,128]{4,2,3,1,0:T(8,128)(2,1)S(1)}, u32[]{:S(2)}, u32[]{:S(2)}) collective-permute-start(bf16[1,2,16,64,128]{4,2,3,1,0:T(8,128)(2,1)S(1)} %copy.92), channel_id=1, source_target_pairs={{0,1},{1,2},{2,3},{3,4},{4,5},{5,6},{6,7},{8,9},{9,10},{10,11},{11... | collective-permute-start | bytes 1572872 | tf_op jit(solution)/shard_map/ppermute | solution.py:18
  8.8 3.6 %convolution_select_fusion = f32[6,16,8,10,128]{4,2,3,1,0:T(8,128)S(1)} fusion(bf16[3,3,3,128,256]{4,3,2,1,0:T(8,128)(2,1)S(1)} %copy-done, pred[8,10]{0,1:T(8,128)(4,1)S(1)} %copy-done.7, bf16[2,8,8,6,256]{4,2,3,1,0:T(8,128)(2,1)S(1)} %fusion.88), kind=kOutput, calls=%fused_computation.42 | convolution fusion | flops 1086259200 | bytes 6094928 | tf_op jit(solution)/shard_map/conv_general_dilated | solution.py:22
  20.6 9.5 %add_divide_fusion = (f32[4,16,8,9,128]{4,2,3,1,0:T(8,128)S(1)}, bf16[4,16,8,9,128]{4,2,3,1,0:T(8,128)(2,1)S(1)}, f32[4,16,8,9,128]{4,2,3,1,0:T(8,128)S(1)}) fusion(pred[8,9]{0,1:T(8,128)(4,1)S(1)} %copy-done.12, bf16[3,3,3,128,128]{4,3,2,1,0:T(8,128)(2,1)S(1)} %copy-done.11, bf16[6,16,1,7,2,128]{5,3,4,1,0,2:T(8,128)(2,1)S(1)} %slice.70, ...), kind=kOutput, calls=%fused_computation.24 | convolution fusion | flops 3918790656 | bytes 8896584 | tf_op jit(solution)/shard_map/conv_general_dilated | solution.py:22
  30.3 5.9 %collective-permute-start.1 = (bf16[1,2,16,64,128]{4,2,3,1,0:T(8,128)(2,1)S(1)}, bf16[1,2,16,64,128]{4,2,3,1,0:T(8,128)(2,1)S(1)}, u32[]{:S(2)}, u32[]{:S(2)}) collective-permute-start(bf16[1,2,16,64,128]{4,2,3,1,0:T(8,128)(2,1)S(1)} %slice_bitcast_fusion.7), channel_id=1, source_target_pairs={{0,1},{1,2},{2,3},{3,4},{4,5},{5,6},{6,7},{8,9},{9,10},{10,11},{11... | collective-permute-start | bytes 1572872 | tf_op jit(solution)/shard_map/ppermute | solution.py:18
  47.6 6.7 %fusion.32 = bf16[3,3,3,128,256]{4,3,2,1,0:T(8,128)(2,1)S(1)} fusion(bf16[1,5,17,65,128]{4,2,3,1,0:T(8,128)(2,1)S(1)} %fusion.30, bf16[1,2,8,32,256]{4,2,3,1,0:T(8,128)(2,1)S(1)} %copy_select_fusion), kind=kOutput, calls=%fused_computation.47 | convolution fusion | flops 906854400 | bytes 3446016 | tf_op jit(solution)/shard_map/transpose | solution.py:49
  56.7 3.0 %fusion.26 = bf16[1,4,16,64,128]{4,2,3,1,0:T(8,128)(2,1)S(1)} fusion(f32[4,16,1,72,128]{4,1,3,0,2:T(8,128)} %bitcast.110, f32[4,16,1,72,128]{4,1,3,0,2:T(8,128)} %bitcast.109, f32[4,16,1,80,128]{4,1,3,0,2:T(8,128)S(1)} %bitcast.107, f32[1,2,16,64,128]{4,2,3,1,0:T(8,128)} %collective-permute-done.2), kind=kLoop, calls=%fused_computation.36 | loop fusion | flops 2097152 | bytes 8388608 | tf_op jit(solution)/shard_map/convert_element_type | solution.py:96
  59.7 35.9 %fusion.41 = bf16[3,3,3,128,128]{4,3,2,1,0:T(8,128)(2,1)S(1)} fusion(bf16[1,4,16,64,128]{4,2,3,1,0:T(8,128)(2,1)S(1)} %fusion.26, bf16[1,6,18,66,128]{4,2,3,1,0:T(8,128)(2,1)} %pad_bitcast_fusion), kind=kOutput, calls=%fused_computation.54 | convolution fusion | flops 3624321024 | bytes 3758080 | tf_op jit(solution)/shard_map/transpose | solution.py:49
  95.7 7.3 %all_to_all.78 = bf16[2,1792,128]{2,1,0:T(8,128)(2,1)} all-to-all(bf16[2,1792,128]{2,1,0:T(8,128)(2,1)S(1)} %bitcast.120), channel_id=1, replica_groups=mesh['xl'=2,'z'=8,'c'=2,'y'=4,'xh'=2] {'c'}, dimensions={0} | all-to-all | bytes 1835008 | tf_op jit(solution)/shard_map/all_to_all | solution.py:53
  105.2 13.3 %all-to-all-start.1 = ((bf16[16,112,128]{2,1,0:T(8,128)(2,1)}), bf16[16,112,128]{2,1,0:T(8,128)(2,1)S(1)}, u32[]{:S(2)}, u32[]{:S(2)}) async-start(bf16[16,112,128]{2,1,0:T(8,128)(2,1)} %bitcast.129), calls=%async_computation.1 | async-start | bytes 917504 | tf_op jit(solution)/shard_map/all_to_all | solution.py:53
  121.3 6.8 %all-to-all-done.1 = bf16[16,112,128]{2,1,0:T(8,128)(2,1)S(1)} async-done(((bf16[16,112,128]{2,1,0:T(8,128)(2,1)}), bf16[16,112,128]{2,1,0:T(8,128)(2,1)S(1)}, u32[]{:S(2)}, u32[]{:S(2)}) %all-to-all-start.1) | async-done | bytes 458784 | tf_op jit(solution)/shard_map/all_to_all | solution.py:53
  128.1 6.5 %all-to-all-start.5 = ((bf16[2,3584,128]{2,1,0:T(8,128)(2,1)}), bf16[2,3584,128]{2,1,0:T(8,128)(2,1)}, u32[]{:S(2)}, u32[]{:S(2)}) async-start(bf16[2,3584,128]{2,1,0:T(8,128)(2,1)} %bitcast.112), calls=%async_computation.5 | async-start | bytes 3670016 | tf_op jit(solution)/shard_map/all_to_all | solution.py:53
  137.8 8.2 %all-to-all-start.2 = ((bf16[8,112,128]{2,1,0:T(8,128)(2,1)}), bf16[8,112,128]{2,1,0:T(8,128)(2,1)S(1)}, u32[]{:S(2)}, u32[]{:S(2)}) async-start(bf16[8,112,128]{2,1,0:T(8,128)(2,1)} %tile.16), calls=%async_computation.2 | async-start | bytes 458752 | tf_op jit(solution)/shard_map/all_to_all | solution.py:53
  146.0 3.0 %reduce_sum.75 = bf16[3584,128]{1,0:T(8,128)(2,1)} reduce(bf16[2,3584,128]{2,1,0:T(8,128)(2,1)} %all-to-all-done.5, bf16[]{:T(256)} %constant.29.clone.1), dimensions={0}, to_apply=%region_3.4 | reduce | flops 458752 | bytes 2752514 | tf_op jit(solution)/shard_map/reduce_sum | solution.py:58
  149.0 7.1 %all-to-all-done.2 = bf16[8,112,128]{2,1,0:T(8,128)(2,1)S(1)} async-done(((bf16[8,112,128]{2,1,0:T(8,128)(2,1)}), bf16[8,112,128]{2,1,0:T(8,128)(2,1)S(1)}, u32[]{:S(2)}, u32[]{:S(2)}) %all-to-all-start.2) | async-done | bytes 229408 | tf_op jit(solution)/shard_map/all_to_all | solution.py:53
  156.2 4.3 %all-to-all-start.6 = ((bf16[16,224,128]{2,1,0:T(8,128)(2,1)}), bf16[16,224,128]{2,1,0:T(8,128)(2,1)}, u32[]{:S(2)}, u32[]{:S(2)}) async-start(bf16[16,224,128]{2,1,0:T(8,128)(2,1)} %bitcast.119), calls=%async_computation.6 | async-start | bytes 1835008 | tf_op jit(solution)/shard_map/all_to_all | solution.py:53
  162.8 10.3 %all-to-all-done.6 = bf16[16,224,128]{2,1,0:T(8,128)(2,1)} async-done(((bf16[16,224,128]{2,1,0:T(8,128)(2,1)}), bf16[16,224,128]{2,1,0:T(8,128)(2,1)}, u32[]{:S(2)}, u32[]{:S(2)}) %all-to-all-start.6) | async-done | bytes 917536 | tf_op jit(solution)/shard_map/all_to_all | solution.py:53
  174.0 5.7 %all-to-all-start.3 = ((bf16[16,112,128]{2,1,0:T(8,128)(2,1)}), bf16[16,112,128]{2,1,0:T(8,128)(2,1)S(1)}, u32[]{:S(2)}, u32[]{:S(2)}) async-start(bf16[16,112,128]{2,1,0:T(8,128)(2,1)} %tile.17), calls=%async_computation.3 | async-start | bytes 917504 | tf_op jit(solution)/shard_map/all_to_all | solution.py:53
  179.7 15.0 %convolution_select_fusion.1 = f32[6,16,8,9,128]{4,2,3,1,0:T(8,128)S(1)} fusion(bf16[3,3,3,128,128]{4,3,2,1,0:T(8,128)(2,1)} %param.8, pred[8,9]{0,1:T(8,128)(4,1)S(1)} %copy-done.13, bf16[4,16,1,7,2,128]{5,3,4,1,0,2:T(8,128)(2,1)} %slice.83, bf16[4,16,1,8,9,128]{5,3,4,1,0,2:T(8,128)(2,1)S(1)} %copy.59), kind=kOutput, calls=%fused_computation.44 | convolution fusion | flops 3912204288 | bytes 5832776 | tf_op jit(solution)/shard_map/conv_general_dilated | solution.py:22
  203.6 3.5 %all-to-all-start.7 = ((bf16[8,224,128]{2,1,0:T(8,128)(2,1)}), bf16[8,224,128]{2,1,0:T(8,128)(2,1)S(1)}, u32[]{:S(2)}, u32[]{:S(2)}) async-start(bf16[8,224,128]{2,1,0:T(8,128)(2,1)} %tile.20), calls=%async_computation.7 | async-start | bytes 917504 | tf_op jit(solution)/shard_map/all_to_all | solution.py:53
  215.1 5.4 %all-to-all-done.7 = bf16[8,224,128]{2,1,0:T(8,128)(2,1)S(1)} async-done(((bf16[8,224,128]{2,1,0:T(8,128)(2,1)}), bf16[8,224,128]{2,1,0:T(8,128)(2,1)S(1)}, u32[]{:S(2)}, u32[]{:S(2)}) %all-to-all-start.7) | async-done | bytes 458784 | tf_op jit(solution)/shard_map/all_to_all | solution.py:53
  221.6 7.0 %all-to-all-start.4 = ((bf16[2,1792,128]{2,1,0:T(8,128)(2,1)}), bf16[2,1792,128]{2,1,0:T(8,128)(2,1)S(1)}, u32[]{:S(2)}, u32[]{:S(2)}) async-start(bf16[2,1792,128]{2,1,0:T(8,128)(2,1)} %tile.19), calls=%async_computation.4 | async-start | bytes 1835008 | tf_op jit(solution)/shard_map/all_to_all | solution.py:53
  231.5 8.6 %all-to-all-start.8 = ((bf16[16,224,128]{2,1,0:T(8,128)(2,1)}), bf16[16,224,128]{2,1,0:T(8,128)(2,1)S(1)}, u32[]{:S(2)}, u32[]{:S(2)}) async-start(bf16[16,224,128]{2,1,0:T(8,128)(2,1)} %tile.21), calls=%async_computation.8 | async-start | bytes 1835008 | tf_op jit(solution)/shard_map/all_to_all | solution.py:53
  242.6 11.4 %all-to-all-done.8 = bf16[16,224,128]{2,1,0:T(8,128)(2,1)S(1)} async-done(((bf16[16,224,128]{2,1,0:T(8,128)(2,1)}), bf16[16,224,128]{2,1,0:T(8,128)(2,1)S(1)}, u32[]{:S(2)}, u32[]{:S(2)}) %all-to-all-start.8) | async-done | bytes 917536 | tf_op jit(solution)/shard_map/all_to_all | solution.py:53
  254.1 7.0 %all_to_all.79 = bf16[2,3584,128]{2,1,0:T(8,128)(2,1)S(1)} all-to-all(bf16[2,3584,128]{2,1,0:T(8,128)(2,1)S(1)} %tile.23), channel_id=1, replica_groups=mesh['xl'=2,'z'=8,'c'=2,'y'=4,'xh'=2] {'c'}, dimensions={0} | all-to-all | bytes 3670016 | tf_op jit(solution)/shard_map/all_to_all | solution.py:53
  (104 shorter events, 61.0 us)
Async XLA Ops:
  0.6 8.1 %copy-start = (bf16[3,3,3,128,256]{4,3,2,1,0:T(8,128)(2,1)S(1)}, bf16[3,3,3,128,256]{4,3,2,1,0:T(8,128)(2,1)}, u32[]{:S(2)}) copy-start(bf16[3,3,3,128,256]{4,3,2,1,0:T(8,128)(2,1)} %param.9) | copy-start | bytes 5308420
  0.6 7.8 %copy-start.8 = (bf16[1,2,8,32,256]{4,3,2,1,0:T(8,128)(2,1)S(1)}, bf16[1,2,8,32,256]{4,3,2,1,0:T(8,128)(2,1)}, u32[]{:S(2)}) copy-start(bf16[1,2,8,32,256]{4,3,2,1,0:T(8,128)(2,1)} %param.6) | copy-start | bytes 786436
  1.9 6.9 %copy-start.7 = (pred[8,10]{0,1:T(8,128)(4,1)S(1)}, pred[8,10]{0,1:T(8,128)(4,1)}, u32[]{:S(2)}) copy-start(pred[8,10]{0,1:T(8,128)(4,1)} %constant.66) | copy-start | bytes 244
  2.2 16.1 %collective-permute-start = (bf16[1,2,16,64,128]{4,2,3,1,0:T(8,128)(2,1)S(1)}, bf16[1,2,16,64,128]{4,2,3,1,0:T(8,128)(2,1)S(1)}, u32[]{:S(2)}, u32[]{:S(2)}) collective-permute-start(bf16[1,2,16,64,128]{4,2,3,1,0:T(8,128)(2,1)S(1)} %copy.92), channel_id=1, source_target_pairs={{0,1},{1,2},{2,3},{3,4},{4,5},{5,6},{6,7},{8,9},{9,10},{10,11},{11... | collective-permute-start | bytes 1572872 | tf_op jit(solution)/shard_map/ppermute | solution.py:18
  12.9 5.4 %copy-start.6 = (bf16[1,4,16,64,128]{4,3,2,1,0:T(8,128)(2,1)S(1)}, bf16[1,4,16,64,128]{4,3,2,1,0:T(8,128)(2,1)}, u32[]{:S(2)}) copy-start(bf16[1,4,16,64,128]{4,3,2,1,0:T(8,128)(2,1)} %param.5) | copy-start | bytes 3145732
  14.0 42.2 %collective-permute-start.2 = (f32[1,2,16,64,128]{4,2,3,1,0:T(8,128)}, f32[1,2,16,64,128]{4,2,3,1,0:T(8,128)}, u32[]{:S(2)}, u32[]{:S(2)}) collective-permute-start(f32[1,2,16,64,128]{4,2,3,1,0:T(8,128)} %slice_bitcast_fusion.4), channel_id=1, source_target_pairs={{1,0},{2,1},{3,2},{4,3},{5,4},{6,5},{7,6},{9,8},{10,9},{11,10},{12... | collective-permute-start | bytes 3145736 | tf_op jit(solution)/shard_map/ppermute | solution.py:18
  30.3 15.3 %collective-permute-start.1 = (bf16[1,2,16,64,128]{4,2,3,1,0:T(8,128)(2,1)S(1)}, bf16[1,2,16,64,128]{4,2,3,1,0:T(8,128)(2,1)S(1)}, u32[]{:S(2)}, u32[]{:S(2)}) collective-permute-start(bf16[1,2,16,64,128]{4,2,3,1,0:T(8,128)(2,1)S(1)} %slice_bitcast_fusion.7), channel_id=1, source_target_pairs={{0,1},{1,2},{2,3},{3,4},{4,5},{5,6},{6,7},{8,9},{9,10},{10,11},{11... | collective-permute-start | bytes 1572872 | tf_op jit(solution)/shard_map/ppermute | solution.py:18
  54.3 2.4 copy-start.1
  105.2 22.9 %all-to-all-start.1 = ((bf16[16,112,128]{2,1,0:T(8,128)(2,1)}), bf16[16,112,128]{2,1,0:T(8,128)(2,1)S(1)}, u32[]{:S(2)}, u32[]{:S(2)}) async-start(bf16[16,112,128]{2,1,0:T(8,128)(2,1)} %bitcast.129), calls=%async_computation.1 | async-start | bytes 917504 | tf_op jit(solution)/shard_map/all_to_all | solution.py:53
  128.1 9.0 %all-to-all-start.5 = ((bf16[2,3584,128]{2,1,0:T(8,128)(2,1)}), bf16[2,3584,128]{2,1,0:T(8,128)(2,1)}, u32[]{:S(2)}, u32[]{:S(2)}) async-start(bf16[2,3584,128]{2,1,0:T(8,128)(2,1)} %bitcast.112), calls=%async_computation.5 | async-start | bytes 3670016 | tf_op jit(solution)/shard_map/all_to_all | solution.py:53
  137.8 18.3 %all-to-all-start.2 = ((bf16[8,112,128]{2,1,0:T(8,128)(2,1)}), bf16[8,112,128]{2,1,0:T(8,128)(2,1)S(1)}, u32[]{:S(2)}, u32[]{:S(2)}) async-start(bf16[8,112,128]{2,1,0:T(8,128)(2,1)} %tile.16), calls=%async_computation.2 | async-start | bytes 458752 | tf_op jit(solution)/shard_map/all_to_all | solution.py:53
  156.2 5.3 %copy-start.9 = (bf16[8,112,128]{2,1,0:T(8,128)(2,1)}, bf16[8,112,128]{2,1,0:T(8,128)(2,1)S(1)}, u32[]{:S(2)}) copy-start(bf16[8,112,128]{2,1,0:T(8,128)(2,1)S(1)} %all-to-all-done.2) | copy-start | bytes 688132
  156.2 17.0 %all-to-all-start.6 = ((bf16[16,224,128]{2,1,0:T(8,128)(2,1)}), bf16[16,224,128]{2,1,0:T(8,128)(2,1)}, u32[]{:S(2)}, u32[]{:S(2)}) async-start(bf16[16,224,128]{2,1,0:T(8,128)(2,1)} %bitcast.119), calls=%async_computation.6 | async-start | bytes 1835008 | tf_op jit(solution)/shard_map/all_to_all | solution.py:53
  161.7 18.0 %copy-start.13 = (pred[8,9]{0,1:T(8,128)(4,1)S(1)}, pred[8,9]{0,1:T(8,128)(4,1)}, u32[]{:S(2)}) copy-start(pred[8,9]{0,1:T(8,128)(4,1)} %constant.64) | copy-start | bytes 220
  174.0 28.8 %all-to-all-start.3 = ((bf16[16,112,128]{2,1,0:T(8,128)(2,1)}), bf16[16,112,128]{2,1,0:T(8,128)(2,1)S(1)}, u32[]{:S(2)}, u32[]{:S(2)}) async-start(bf16[16,112,128]{2,1,0:T(8,128)(2,1)} %tile.17), calls=%async_computation.3 | async-start | bytes 917504 | tf_op jit(solution)/shard_map/all_to_all | solution.py:53
  196.8 2.2 copy-start.3
  197.7 14.9 %collective-permute-start.3 = (bf16[1,2,16,64,128]{4,2,3,1,0:T(8,128)(2,1)}, bf16[1,2,16,64,128]{4,2,3,1,0:T(8,128)(2,1)}, u32[]{:S(2)}, u32[]{:S(2)}) collective-permute-start(bf16[1,2,16,64,128]{4,2,3,1,0:T(8,128)(2,1)} %slice_bitcast_fusion.6), channel_id=1, source_target_pairs={{1,0},{2,1},{3,2},{4,3},{5,4},{6,5},{7,6},{9,8},{10,9},{11,10},{12... | collective-permute-start | bytes 1572872 | tf_op jit(solution)/shard_map/ppermute | solution.py:18
  200.1 1.3 copy-start.5
  201.4 5.7 %copy-start.14 = (pred[8,5]{0,1:T(8,128)(4,1)S(1)}, pred[8,5]{0,1:T(8,128)(4,1)}, u32[]{:S(2)}) copy-start(pred[8,5]{0,1:T(8,128)(4,1)} %constant.63) | copy-start | bytes 124
  203.6 17.0 %all-to-all-start.7 = ((bf16[8,224,128]{2,1,0:T(8,128)(2,1)}), bf16[8,224,128]{2,1,0:T(8,128)(2,1)S(1)}, u32[]{:S(2)}, u32[]{:S(2)}) async-start(bf16[8,224,128]{2,1,0:T(8,128)(2,1)} %tile.20), calls=%async_computation.7 | async-start | bytes 917504 | tf_op jit(solution)/shard_map/all_to_all | solution.py:53
  207.1 5.5 %copy-start.2 = (f32[4,16,8,9,128]{4,1,3,2,0:T(8,128)S(1)}, f32[4,16,8,9,128]{4,1,3,2,0:T(8,128)}, u32[]{:S(2)}) copy-start(f32[4,16,8,9,128]{4,1,3,2,0:T(8,128)} %copy.60) | copy-start | bytes 7077892
  221.6 8.7 %all-to-all-start.4 = ((bf16[2,1792,128]{2,1,0:T(8,128)(2,1)}), bf16[2,1792,128]{2,1,0:T(8,128)(2,1)S(1)}, u32[]{:S(2)}, u32[]{:S(2)}) async-start(bf16[2,1792,128]{2,1,0:T(8,128)(2,1)} %tile.19), calls=%async_computation.4 | async-start | bytes 1835008 | tf_op jit(solution)/shard_map/all_to_all | solution.py:53
  230.2 1.2 copy-start.4
  231.5 22.5 %all-to-all-start.8 = ((bf16[16,224,128]{2,1,0:T(8,128)(2,1)}), bf16[16,224,128]{2,1,0:T(8,128)(2,1)S(1)}, u32[]{:S(2)}, u32[]{:S(2)}) async-start(bf16[16,224,128]{2,1,0:T(8,128)(2,1)} %tile.21), calls=%async_computation.8 | async-start | bytes 1835008 | tf_op jit(solution)/shard_map/all_to_all | solution.py:53
  (3 other events, 3.4 us)

commit v2 on v1

v2 whole, which is shorter than its diff:
```python
import functools
import math

import jax
import jax.numpy as jnp
from jax import lax
from jax.experimental import pallas as pl
from jax.experimental.pallas import tpu as pltpu
from jax.sharding import Mesh
from jax.sharding import PartitionSpec as P

TM = ("y", "xh")
DP = ("xl", "z", "c")
XY = ("xl", "xh", "y")

BF = jnp.bfloat16
F32 = jnp.float32
VMEM = pl.BlockSpec(memory_space=pltpu.VMEM)
SMEM = pl.BlockSpec(memory_space=pltpu.SMEM)
ANY = pl.BlockSpec(memory_space=pl.ANY)
HALF = 42 * 128


def params(mib):
    return pltpu.CompilerParams(vmem_limit_bytes=mib * 1024 * 1024)


def cost(flops, moved):
    return pl.CostEstimate(flops=flops, bytes_accessed=moved, transcendentals=0)


def dot(a, b):
    return jnp.dot(a, b, preferred_element_type=F32)


def turned(v):
    return v.astype(F32).T.astype(BF)


def column(shape):
    return lax.broadcasted_iota(jnp.int32, shape, 1)


def from_left(v):
    return jnp.where(column(v.shape) == 0, 0.0, pltpu.roll(v, 1, 1))


def from_right(v):
    last = v.shape[1] - 1
    return jnp.where(column(v.shape) == last, 0.0, pltpu.roll(v, last, 1))


def spread(dst, frame, even, odd):
    dst[frame, 1:17, :, 0:128] = even.astype(BF)
    dst[frame, 1:17, :, 128:256] = odd.astype(BF)
    dst[frame, 1:17, :, 256:384] = from_left(odd).astype(BF)
    dst[frame, 1:17, :, 384:512] = from_right(even).astype(BF)


def split_columns(wide, v):
    wide[...] = v.astype(F32)
    return wide[:, pl.ds(0, 32, stride=2), :], wide[:, pl.ds(1, 32, stride=2), :]


def clear_edges(dst, frames):
    z = jnp.zeros((frames, 1, 32, 512), BF)
    dst[:, 0:1] = z
    dst[:, 17:18] = z


def conv_frame(src, f, w_ref):
    acc = None
    for k in range(3):
        for a in range(3):
            lhs = src[f + k, a : a + 16].reshape(512, 512)
            term = dot(lhs, w_ref[3 * k + a])
            acc = term if acc is None else acc + term
    return acc


def pair_weights(dst, tap, w):
    z = jnp.zeros((128, 128), BF)
    rows = ((w[1], w[0]), (w[2], w[1]), (w[0], z), (z, w[2]))
    for r, (even, odd) in enumerate(rows):
        dst[tap, 128 * r : 128 * r + 128, 0:128] = even
        dst[tap, 128 * r : 128 * r + 128, 128:256] = odd


def kernel_weights(wconv_ref, wdown_ref, wc_ref, wa_ref):
    z = jnp.zeros((256, 128), BF)
    for tap in range(9):
        pair_weights(wc_ref, tap, [wconv_ref[3 * tap + b] for b in range(3)])
        w = [turned(wdown_ref[tap, 128 * b : 128 * b + 128]) for b in range(3)]
        wa_ref[tap, 0:256, 0:128] = w[1]
        wa_ref[tap, 0:256, 128:256] = w[2]
        wa_ref[tap, 256:512, 0:128] = z
        wa_ref[tap, 256:512, 128:256] = w[0]


def call_weights(w_conv, w_down):
    return pl.pallas_call(
        kernel_weights,
        out_shape=(jax.ShapeDtypeStruct((9, 512, 256), BF),) * 2,
        in_specs=[VMEM, VMEM],
        out_specs=(VMEM, VMEM),
        compiler_params=params(16),
        cost_estimate=cost(10**6, 8 * 10**6),
    )(w_conv, w_down)


TERMS = {0: ((0, 2), (1, 0)), 1: ((1, 1),), 2: ((1, 2), (2, 0)), 3: ((2, 1),)}


def kernel_grads(core_ref, x_ref, before_ref, m_ref, next_ref, wc_ref, wa_ref, wd_ref,
                 hg_ref, own_ref, other_ref, enc_ref, part_ref,
                 wide, xs, ms, mt, acs, hgt, dact, sums, sems):
    core = core_ref[0]
    clear_edges(xs, 6)
    for f in range(6):
        frame = before_ref[f] if f < 2 else x_ref[f - 2]
        spread(xs, f, *split_columns(wide.at[f % 2], frame))
    ms[:, 8:9] = jnp.zeros((3, 1, 32, 512), BF)
    for t in range(3):
        m = next_ref[0] if t == 2 else m_ref[t]
        ms[t, 0:8, :, 0:256] = m
        ms[t, 0:8, :, 256:512] = from_right(m.astype(F32)).astype(BF)
        mt[:, 256 * t : 256 * t + 256] = turned(m.reshape(256, 256))
    acs[:, 0:1, 0:1] = jnp.zeros((4, 1, 1, 32, 384), BF)
    acs[:, 8:9, 1:2] = jnp.zeros((4, 1, 1, 32, 384), BF)
    sums[1, HALF - 384 :] = jnp.zeros((384, 128), BF)

    for f in range(4):
        even = odd = None
        for t, k in TERMS[f]:
            here = ms[t, 0:8].reshape(256, 512)
            below = ms[t, 1:9].reshape(256, 512)
            e = dot(here, wa_ref[3 * k + 1])
            o = dot(here, wa_ref[3 * k + 2]) + dot(below, wa_ref[3 * k])
            even = e if even is None else even + e
            odd = o if odd is None else odd + o
        dact[f, :, 0] = even.reshape(8, 32, 256)
        dact[f, :, 1] = odd.reshape(8, 32, 256)

    for f in range(4):
        hidden = conv_frame(xs, f, wc_ref)
        sig = 1.0 / (1.0 + jnp.exp(-hidden))
        act = (hidden * sig).reshape(8, 2, 32, 256)
        left = from_left(act[..., 128:256].reshape(16, 32, 128)).reshape(8, 2, 32, 128)
        actb = act.astype(BF)
        leftb = left.astype(BF)
        acs[f, 0:8, 1, :, 128:384] = actb[:, 0]
        acs[f, 1:9, 0, :, 128:384] = actb[:, 1]
        acs[f, 0:8, 1, :, 0:128] = leftb[:, 0]
        acs[f, 1:9, 0, :, 0:128] = leftb[:, 1]
        grad = dact[f].reshape(512, 256) * sig * (1.0 + hidden * (1.0 - sig))
        hg_ref[f] = grad.astype(BF).reshape(16, 32, 256)
        hgt[:, 512 * f : 512 * f + 512] = grad.T.astype(BF)

    def put(block, v):
        half, at = divmod(128 * block, HALF)
        sums[half, at : at + 128] = v

    def tap(f, a):
        rows = (acs[f, 0:8, 0], acs[f, 0:8, 1], acs[f, 1:9, 0])[a]
        return rows.reshape(256, 384)

    for k in range(3):
        m_t = mt[:, 0:512] if k == 2 else mt[:, 256:768]
        parity = 1 if k == 1 else 0
        for a in range(3):
            right = jnp.concatenate([tap(parity, a), tap(parity + 2, a)], axis=0)
            g = dot(m_t, right)
            for b in range(3):
                block = g[:, 128 * b : 128 * b + 128].T.astype(BF)
                put(27 + 9 * k + 3 * a + b, block[:, 0:128])
                put(54 + 9 * k + 3 * a + b, block[:, 128:256])

    for k in range(3):
        for a in range(3):
            right = xs[k : k + 4, a : a + 16].reshape(2048, 512)
            g = dot(hgt[...], right)
            for b in range(3):
                u, v = (2, 0, 1)[b], (0, 1, 3)[b]
                both = g[0:128, 128 * u : 128 * u + 128] + g[128:256, 128 * v : 128 * v + 128]
                put(9 * k + 3 * a + b, both.T.astype(BF))

    send = pltpu.make_async_copy(sums.at[1 - core], other_ref, sems.at[0])
    keep = pltpu.make_async_copy(sums.at[core], own_ref, sems.at[1])
    send.start()
    keep.start()
    for t in range(3):
        acc = None
        for k in range(3):
            f = 2 * t + k - 2
            if 0 <= f < 4:
                for a in range(3):
                    term = dot(tap(f, a), wd_ref[3 * k + a])
                    acc = term if acc is None else acc + term
        if t == 2:
            part_ref[0] = acc.reshape(8, 32, 256)
        else:
            enc_ref[t] = acc.reshape(8, 32, 256)
    send.wait()
    keep.wait()


def call_grads(core, x, before, m, after, wc, wa, wd):
    return pl.pallas_call(
        kernel_grads,
        out_shape=(
            jax.ShapeDtypeStruct((4, 16, 32, 256), BF),
            jax.ShapeDtypeStruct((HALF, 128), BF),
            jax.ShapeDtypeStruct((HALF, 128), BF),
            jax.ShapeDtypeStruct((2, 8, 32, 256), F32),
            jax.ShapeDtypeStruct((1, 8, 32, 256), F32),
        ),
        in_specs=[SMEM] + [VMEM] * 7,
        out_specs=(VMEM, ANY, ANY, VMEM, VMEM),
        scratch_shapes=[
            pltpu.VMEM((2, 16, 64, 128), F32),
            pltpu.VMEM((6, 18, 32, 512), BF),
            pltpu.VMEM((3, 9, 32, 512), BF),
            pltpu.VMEM((256, 768), BF),
            pltpu.VMEM((4, 9, 2, 32, 384), BF),
            pltpu.VMEM((256, 2048), BF),
            pltpu.VMEM((4, 8, 2, 32, 256), F32),
            pltpu.VMEM((2, HALF, 128), BF),
            pltpu.SemaphoreType.DMA((2,)),
        ],
        compiler_params=params(40),
        cost_estimate=cost(12 * 10**9, 10**7),
    )(core, x, before, m, after, wc, wa, wd)


def kernel_clip(h_ref, after_ref, w_ref, out_ref, hs, wt, wide):
    clear_edges(hs, 6)
    for tap in range(9):
        pair_weights(wt, tap, [turned(w_ref[3 * (8 - tap) + 2 - b]) for b in range(3)])
    for f in range(6):
        v = (h_ref[f] if f < 4 else after_ref[f - 4]).astype(F32)
        spread(hs, f, v[:, :, 0:128], v[:, :, 128:256])
    for f in range(4):
        v = conv_frame(hs, f, wt).reshape(16, 32, 256)
        wide[f % 2, :, pl.ds(0, 32, stride=2), :] = v[:, :, 0:128]
        wide[f % 2, :, pl.ds(1, 32, stride=2), :] = v[:, :, 128:256]
        out_ref[f] = wide[f % 2].astype(BF)


def call_clip(h, after, w):
    return pl.pallas_call(
        kernel_clip,
        out_shape=jax.ShapeDtypeStruct((4, 16, 64, 128), BF),
        in_specs=[VMEM] * 3,
        out_specs=VMEM,
        scratch_shapes=[
            pltpu.VMEM((6, 18, 32, 512), BF),
            pltpu.VMEM((9, 512, 256), BF),
            pltpu.VMEM((2, 16, 64, 128), F32),
        ],
        compiler_params=params(32),
        cost_estimate=cost(5 * 10**9, 5 * 10**6),
    )(h, after, w)


def kernel_out(scale, core_ref, own_ref, other_ref, conv_ref, down_ref):
    def write(halves):
        for block in range(81):
            half, at = divmod(128 * block, HALF)
            v = halves[half][at : at + 128].astype(F32) * scale
            which, tap = divmod(block, 27)
            if which == 0:
                conv_ref[tap] = v
            else:
                down_ref[tap, :, 128 * (which - 1) : 128 * which] = v

    @pl.when(core_ref[0] == 0)
    def _():
        write((own_ref, other_ref))

    @pl.when(core_ref[0] == 1)
    def _():
        write((other_ref, own_ref))


def call_out(core, own, other, scale):
    return pl.pallas_call(
        functools.partial(kernel_out, scale),
        out_shape=(
            jax.ShapeDtypeStruct((27, 128, 128), F32),
            jax.ShapeDtypeStruct((27, 128, 256), F32),
        ),
        in_specs=[SMEM, VMEM, VMEM],
        out_specs=(VMEM, VMEM),
        compiler_params=params(32),
        cost_estimate=cost(10**6, 8 * 10**6),
    )(core, own, other)


def shifted(block, distance):
    devices = range(8)
    route = [(i - distance, i) for i in devices if i - distance in devices]
    return lax.ppermute(block, TM, route)


def swapped(block):
    return lax.ppermute(block, "c", [(0, 1), (1, 0)])


def exchange(value, axes):
    return lax.all_to_all(value, axes, 0, 0, tiled=True)


def add_up(value, parts):
    split = value.reshape((parts, value.shape[0] // parts, 128))
    return jnp.sum(split.astype(F32), axis=0).astype(BF)


def gather(value, axes, parts):
    return exchange(jnp.tile(value, (parts, 1)), axes)


def shards(clips, cotangent, clip_frames, w_conv, w_down):
    frames, rows, cols = clips.shape[1:4]
    core = lax.axis_index("c").astype(jnp.int32).reshape(1)
    last = clips[0, 2:]
    before = shifted(last, 1)
    cotangent, _ = lax.optimization_barrier((cotangent, last))
    times = lax.axis_index(TM) * 2 + jnp.arange(2, dtype=jnp.int32)
    keep = (2 * times < clip_frames[0])[:, None, None, None]
    masked = jnp.where(keep, cotangent[0], jnp.zeros_like(cotangent[0]))
    masked_after = shifted(masked[:1], -1)
    taps_conv = w_conv.reshape(27, 128, 128)
    taps_down = w_down.reshape(9, 384, 256)
    wc, wa = call_weights(taps_conv, taps_down)
    hg, own, other, enc, part = call_grads(
        core, clips[0], before, masked, masked_after, wc, wa, taps_down
    )
    own = (own.astype(F32) + swapped(other).astype(F32)).astype(BF)
    own = add_up(exchange(own, XY), 16)
    own, ends, part = lax.optimization_barrier((own, hg[:2], part))
    after = shifted(ends, -1)
    part = shifted(part, 1)
    own = add_up(gather(own, "z", 8), 8)
    own, after, part = lax.optimization_barrier((own, after, part))
    own = gather(own, XY, 16)
    clip_grad = call_clip(hg, after, taps_conv)[None]
    own, clip_grad = lax.optimization_barrier((own, clip_grad))
    encoded = jnp.concatenate([enc[:1] + part, enc[1:]]).astype(BF)[None]
    scale = 1.0 / math.sqrt(lax.axis_size(DP) * frames * lax.axis_size(TM) * rows * cols)
    conv_grad, down_grad = call_out(core, own, swapped(own), scale)
    return (encoded, clip_grad, conv_grad.reshape(w_conv.shape), down_grad.reshape(w_down.shape))


def solution(mesh):
    fine = Mesh(mesh.devices.reshape(2, 8, 2, 4, 2), DP + TM)
    spread_out = P(DP, TM, None, None, None)
    in_specs = (spread_out, spread_out, P(DP), P(), P())
    out_specs = (spread_out, spread_out, P(), P())
    return jax.shard_map(shards, mesh=fine, in_specs=in_specs, out_specs=out_specs, check_vma=False)
```

time: 269 us -> 135 us (0.50); the launches traced: 264 us -> 135 us
  matrix products: 73.7 us -> 0 us
  starting transfers between devices: 71.2 us -> 43.1 us
  local copies, waits for them, and re-layouts: 32.3 us -> 5.88 us
  Pallas kernels: 0 us -> 25 us
  other arithmetic: 20.2 us -> 5.82 us
  blocking collectives: 14.3 us -> 0 us
  waiting for transfers between devices: 49.9 us -> 53.5 us
    transpose x2 -> x0, matrix products: 42.6 us -> none  [kernel_sums(): return jnp.transpose(result, (1, 2, 3, 0, 4))]
    all_to_all x8 -> x3, starting transfers between devices: 57.1 us -> 23.3 us  [exchange(): return lax.all_to_all(value, axes, 0, 0, tiled=True)]
    conv_general_dilated x4 -> x0, matrix products: 31.1 us -> none  [convolve(): lax.conv_general_dilated(lhs, rhs, strides, padding, lhs_dilation=dilatio...]
    pallas_call x0 -> x4, Pallas kernels: none -> 25 us  [the longest x1 15.1 us: call_grads(): pl.pallas_call(kernel_grads, out_shape=(jax.ShapeDtypeStruct((4, 16, 32,...]
    all_to_all x2 -> x0, blocking collectives: 14.3 us -> none  [exchange(): return lax.all_to_all(value, axes, 0, 0, tiled=True)]
    conv_general_dilated x14 -> x0, local copies, waits for them, and re-layouts: 7.55 us -> none  [convolve(): lax.conv_general_dilated(lhs, rhs, strides, padding, lhs_dilation=dilatio...]
    ppermute x0 -> x2, starting transfers between devices: none -> 6.25 us  [swapped(): return lax.ppermute(block, 'c', [(0, 1), (1, 0)])]
    all_to_all x8 -> x3, waiting for transfers between devices: 45.1 us -> 39.5 us  [exchange(): return lax.all_to_all(value, axes, 0, 0, tiled=True)]
  transfers between devices with their start and end apart: 12 -> 9, of which waited for: 10 -> 6; matrix products, arithmetic and copies ran while one was open for 28% -> 2% of each run, Pallas kernels for 0% -> 5%
where the time goes in v2:
time: 135 us
  waiting for transfers between devices  53.5 us (40%)
  starting transfers between devices  43.1 us (32%)
  Pallas kernels  25 us (19%)
  local copies, waits for them, and re-layouts  5.88 us (4%)
  other arithmetic  5.82 us (4%)
  between operations  1.5 us (1%)
    all_to_all x3, waiting for transfers between devices, exchange(): return lax.all_to_all(value, axes, 0, 0, tiled=True)  39.5 us
    all_to_all x3, starting transfers between devices, exchange(): return lax.all_to_all(value, axes, 0, 0, tiled=True)  23.3 us
    pallas_call x1, Pallas kernels, call_grads(): pl.pallas_call(kernel_grads, out_shape=(jax.ShapeDtypeStruct((4, 16, 32,...  15.1 us
    ppermute x4, starting transfers between devices, shifted(): return lax.ppermute(block, TM, route)  13.6 us
    ppermute x4, waiting for transfers between devices, shifted(): return lax.ppermute(block, TM, route)  10.2 us
    ppermute x2, starting transfers between devices, swapped(): return lax.ppermute(block, 'c', [(0, 1), (1, 0)])  6.25 us
    pallas_call x1, Pallas kernels, call_clip(): pl.pallas_call(kernel_clip, out_shape=jax.ShapeDtypeStruct((4, 16, 64, 12...  6.21 us
    ppermute x2, waiting for transfers between devices, swapped(): return lax.ppermute(block, 'c', [(0, 1), (1, 0)])  3.78 us
  transfers between devices with their start and end apart: 9, of which 6 were waited for; matrix products, arithmetic and copies ran while one was open for 2% of the time, Pallas kernels for 5%

profile of v2, /device:TPU:1, one launch (start us, length us, event | category | flops | bytes accessed | tf_op | source)
XLA Modules:
  0.0 134.8 jit_solution(16886959155869623457)
XLA Ops:
  0.6 1.2 slice_bitcast_fusion
  1.9 5.5 %collective-permute-start = (bf16[2,16,64,128]{3,2,1,0:T(8,128)(2,1)S(1)}, bf16[2,16,64,128]{3,2,1,0:T(8,128)(2,1)S(1)}, u32[]{:S(2)}, u32[]{:S(2)}) collective-permute-start(bf16[2,16,64,128]{3,2,1,0:T(8,128)(2,1)S(1)} %slice_bitcast_fusion), channel_id=1, source_target_pairs={{0,1},{1,2},{2,3},{3,4},{4,5},{5,6},{6,7},{8,9},{9,10},{10,11},{11... | collective-permute-start | bytes 1572872 | tf_op jit(solution)/shard_map/ppermute | solution.py:302
  8.0 1.0 bitcast_select_fusion.m_ref
  9.1 1.3 collective-permute-start.1
  10.4 1.2 copy-done.1
  12.5 10.2 %collective-permute-done.1.next_ref = bf16[1,8,32,256]{3,2,1,0:T(8,128)(2,1)S(1)} collective-permute-done((bf16[1,8,32,256]{3,2,1,0:T(8,128)(2,1)S(1)}, bf16[1,8,32,256]{3,2,1,0:T(8,128)(2,1)S(1)}, u32[]{:S(2)}, u32[]{:S(2)}) %collective-permute-start.1) | collective-permute-done | bytes 131104 | tf_op jit(solution)/shard_map/ppermute | solution.py:302
  22.7 15.1 %shard_map.85 = (bf16[4,16,32,256]{3,2,1,0:T(8,128)(2,1)S(1)}, bf16[5376,128]{1,0:T(8,128)(2,1)S(1)}, bf16[5376,128]{1,0:T(8,128)(2,1)S(1)}, f32[2,8,32,256]{3,2,1,0:T(8,128)S(1)}, f32[1,8,32,256]{3,2,1,0:T(8,128)S(1)}) custom-call(s32[1]{0:T(128)} %bitcast.core_ref, bf16[4,16,64,128]{3,2,1,0:T(8,128)(2,1)S(1)} %bitcast.25, ...), custom_call_target="tpu_custom_call" | custom-call | flops 12000000000 | bytes 10000000 | tf_op jit(solution)/shard_map/pallas_call | solution.py:208
  37.9 1.6 %collective-permute-start.2 = (bf16[5376,128]{1,0:T(8,128)(2,1)S(1)}, bf16[5376,128]{1,0:T(8,128)(2,1)S(1)}, u32[]{:S(2)}, u32[]{:S(2)}) collective-permute-start(bf16[5376,128]{1,0:T(8,128)(2,1)S(1)} %get-tuple-element.27), channel_id=1, source_target_pairs={{0,8},{8,0},{1,9},{9,1},{2,10},{10,2},{3,11},{11,3},{4,12},{12,4},... | collective-permute-start | bytes 4128776 | tf_op jit(solution)/shard_map/ppermute | solution.py:306
  39.5 2.8 %collective-permute-done.2 = bf16[5376,128]{1,0:T(8,128)(2,1)S(1)} collective-permute-done((bf16[5376,128]{1,0:T(8,128)(2,1)S(1)}, bf16[5376,128]{1,0:T(8,128)(2,1)S(1)}, u32[]{:S(2)}, u32[]{:S(2)}) %collective-permute-start.2) | collective-permute-done | bytes 1376288 | tf_op jit(solution)/shard_map/ppermute | solution.py:306
  42.3 1.4 %add_convert_fusion = bf16[5376,128]{1,0:T(8,128)(2,1)} fusion(bf16[5376,128]{1,0:T(8,128)(2,1)S(1)} %collective-permute-done.2, bf16[5376,128]{1,0:T(8,128)(2,1)S(1)} %get-tuple-element.26), kind=kLoop, calls=%fused_computation | loop fusion | flops 2752512 | bytes 4128768 | tf_op jit(solution)/shard_map/convert_element_type | solution.py:338
  43.7 6.7 %all-to-all-start = ((bf16[16,336,128]{2,1,0:T(8,128)(2,1)}), bf16[16,336,128]{2,1,0:T(8,128)(2,1)}, u32[]{:S(2)}, u32[]{:S(2)}) async-start(bf16[16,336,128]{2,1,0:T(8,128)(2,1)} %bitcast.7), calls=%async_computation | async-start | bytes 2752512 | tf_op jit(solution)/shard_map/all_to_all | solution.py:310
  50.4 18.4 %all-to-all-done = bf16[16,336,128]{2,1,0:T(8,128)(2,1)} async-done(((bf16[16,336,128]{2,1,0:T(8,128)(2,1)}), bf16[16,336,128]{2,1,0:T(8,128)(2,1)}, u32[]{:S(2)}, u32[]{:S(2)}) %all-to-all-start) | async-done | bytes 1376288 | tf_op jit(solution)/shard_map/all_to_all | solution.py:310
  68.8 1.5 %reduce_sum.24 = bf16[336,128]{1,0:T(8,128)(2,1)S(1)} reduce(bf16[16,336,128]{2,1,0:T(8,128)(2,1)} %all-to-all-done, bf16[]{:T(256)} %constant.18.clone.1), dimensions={0}, to_apply=%region_0.1 | reduce | flops 645120 | bytes 1462274 | tf_op jit(solution)/shard_map/reduce_sum | solution.py:315
  71.2 8.2 %all-to-all-start.1 = ((bf16[8,336,128]{2,1,0:T(8,128)(2,1)}), bf16[8,336,128]{2,1,0:T(8,128)(2,1)S(1)}, u32[]{:S(2)}, u32[]{:S(2)}) async-start(bf16[8,336,128]{2,1,0:T(8,128)(2,1)} %tile.4), calls=%async_computation.1 | async-start | bytes 1376256 | tf_op jit(solution)/shard_map/all_to_all | solution.py:310
  79.4 1.3 collective-permute-start.3
  80.7 5.5 %collective-permute-start.4 = (f32[1,8,32,256]{3,2,1,0:T(8,128)S(1)}, f32[1,8,32,256]{3,2,1,0:T(8,128)S(1)}, u32[]{:S(2)}, u32[]{:S(2)}) collective-permute-start(f32[1,8,32,256]{3,2,1,0:T(8,128)S(1)} %copy-done.8), channel_id=1, source_target_pairs={{0,1},{1,2},{2,3},{3,4},{4,5},{5,6},{6,7},{8,9},{9,10},{10,11},{11... | collective-permute-start | bytes 786440 | tf_op jit(solution)/shard_map/ppermute | solution.py:302
  86.2 12.1 %all-to-all-done.1 = bf16[8,336,128]{2,1,0:T(8,128)(2,1)S(1)} async-done(((bf16[8,336,128]{2,1,0:T(8,128)(2,1)}), bf16[8,336,128]{2,1,0:T(8,128)(2,1)S(1)}, u32[]{:S(2)}, u32[]{:S(2)}) %all-to-all-start.1) | async-done | bytes 688160 | tf_op jit(solution)/shard_map/all_to_all | solution.py:310
  98.4 1.3 tile.5
  99.7 8.4 %all-to-all-start.2 = ((bf16[16,336,128]{2,1,0:T(8,128)(2,1)}), bf16[16,336,128]{2,1,0:T(8,128)(2,1)S(1)}, u32[]{:S(2)}, u32[]{:S(2)}) async-start(bf16[16,336,128]{2,1,0:T(8,128)(2,1)} %tile.5), calls=%async_computation.2 | async-start | bytes 2752512 | tf_op jit(solution)/shard_map/all_to_all | solution.py:310
  108.1 1.2 copy-done.6
  109.4 6.2 %shard_map.86 = bf16[4,16,64,128]{3,2,1,0:T(8,128)(2,1)} custom-call(bf16[4,16,32,256]{3,2,1,0:T(8,128)(2,1)S(1)} %copy-done.6, bf16[2,16,32,256]{3,2,1,0:T(8,128)(2,1)S(1)} %collective-permute-done.3.after_ref, bf16[27,128,128]{2,1,0:T(8,128)(2,1)S(1)} %bitcast.24), custom_call_target="tpu_custom_call" | custom-call | flops 5000000000 | bytes 5000000 | tf_op jit(solution)/shard_map/pallas_call | solution.py:250
  115.6 9.1 %all-to-all-done.2 = bf16[16,336,128]{2,1,0:T(8,128)(2,1)S(1)} async-done(((bf16[16,336,128]{2,1,0:T(8,128)(2,1)}), bf16[16,336,128]{2,1,0:T(8,128)(2,1)S(1)}, u32[]{:S(2)}, u32[]{:S(2)}) %all-to-all-start.2) | async-done | bytes 1376288 | tf_op jit(solution)/shard_map/all_to_all | solution.py:310
  124.7 4.6 %collective-permute-start.5 = (bf16[5376,128]{1,0:T(8,128)(2,1)S(1)}, bf16[5376,128]{1,0:T(8,128)(2,1)S(1)}, u32[]{:S(2)}, u32[]{:S(2)}) collective-permute-start(bf16[5376,128]{1,0:T(8,128)(2,1)S(1)} %bitcast.19), channel_id=1, source_target_pairs={{0,8},{8,0},{1,9},{9,1},{2,10},{10,2},{3,11},{11,3},{4,12},{12,4},... | collective-permute-start | bytes 4128776 | tf_op jit(solution)/shard_map/ppermute | solution.py:306
  132.0 2.7 %shard_map.87 = (f32[27,128,128]{2,1,0:T(8,128)}, f32[27,128,256]{2,1,0:T(8,128)}) custom-call(s32[1]{0:T(128)} %bitcast.core_ref, bf16[5376,128]{1,0:T(8,128)(2,1)S(1)} %bitcast.20, bf16[5376,128]{1,0:T(8,128)(2,1)S(1)} %collective-permute-done.5.other_ref), custom_call_target="tpu_custom_call" | custom-call | flops 1000000 | bytes 8000000 | tf_op jit(solution)/shard_map/pallas_call | solution.py:286
  (31 shorter events, 4.8 us)
Async XLA Ops:
  0.6 9.8 %copy-start = (bf16[3,3,3,128,256]{4,3,2,1,0:T(8,128)(2,1)S(1)}, bf16[3,3,3,128,256]{4,3,2,1,0:T(8,128)(2,1)}, u32[]{:S(2)}) copy-start(bf16[3,3,3,128,256]{4,3,2,1,0:T(8,128)(2,1)} %param.9) | copy-start | bytes 5308420
  1.9 20.8 %collective-permute-start = (bf16[2,16,64,128]{3,2,1,0:T(8,128)(2,1)S(1)}, bf16[2,16,64,128]{3,2,1,0:T(8,128)(2,1)S(1)}, u32[]{:S(2)}, u32[]{:S(2)}) collective-permute-start(bf16[2,16,64,128]{3,2,1,0:T(8,128)(2,1)S(1)} %slice_bitcast_fusion), channel_id=1, source_target_pairs={{0,1},{1,2},{2,3},{3,4},{4,5},{5,6},{6,7},{8,9},{9,10},{10,11},{11... | collective-permute-start | bytes 1572872 | tf_op jit(solution)/shard_map/ppermute | solution.py:302
  9.1 13.6 %collective-permute-start.1 = (bf16[1,8,32,256]{3,2,1,0:T(8,128)(2,1)S(1)}, bf16[1,8,32,256]{3,2,1,0:T(8,128)(2,1)S(1)}, u32[]{:S(2)}, u32[]{:S(2)}) collective-permute-start(bf16[1,8,32,256]{3,2,1,0:T(8,128)(2,1)S(1)} %slice.21), channel_id=1, source_target_pairs={{1,0},{2,1},{3,2},{4,3},{5,4},{6,5},{7,6},{9,8},{10,9},{11,10},{12... | collective-permute-start | bytes 393224 | tf_op jit(solution)/shard_map/ppermute | solution.py:302
  10.4 1.2 copy-start.1
  11.6 11.1 %copy-start.3 = (bf16[1,4,16,64,128]{4,3,2,1,0:T(8,128)(2,1)S(1)}, bf16[1,4,16,64,128]{4,3,2,1,0:T(8,128)(2,1)}, u32[]{:S(2)}) copy-start(bf16[1,4,16,64,128]{4,3,2,1,0:T(8,128)(2,1)} %param.5) | copy-start | bytes 3145732
  37.8 5.8 %copy-start.4 = (bf16[4,16,32,256]{3,2,1,0:T(8,128)(2,1)}, bf16[4,16,32,256]{3,2,1,0:T(8,128)(2,1)S(1)}, u32[]{:S(2)}) copy-start(bf16[4,16,32,256]{3,2,1,0:T(8,128)(2,1)S(1)} %get-tuple-element.28.h_ref) | copy-start | bytes 3145732
  37.9 5.8 %copy-start.7 = (f32[1,8,32,256]{3,2,1,0:T(8,128)}, f32[1,8,32,256]{3,2,1,0:T(8,128)S(1)}, u32[]{:S(2)}) copy-start(f32[1,8,32,256]{3,2,1,0:T(8,128)S(1)} %get-tuple-element.32) | copy-start | bytes 786436
  37.9 4.4 %collective-permute-start.2 = (bf16[5376,128]{1,0:T(8,128)(2,1)S(1)}, bf16[5376,128]{1,0:T(8,128)(2,1)S(1)}, u32[]{:S(2)}, u32[]{:S(2)}) collective-permute-start(bf16[5376,128]{1,0:T(8,128)(2,1)S(1)} %get-tuple-element.27), channel_id=1, source_target_pairs={{0,8},{8,0},{1,9},{9,1},{2,10},{10,2},{3,11},{11,3},{4,12},{12,4},... | collective-permute-start | bytes 4128776 | tf_op jit(solution)/shard_map/ppermute | solution.py:306
  43.7 6.7 %copy-start.5 = (bf16[4,16,32,256]{3,2,1,0:T(8,128)(2,1)S(1)}, bf16[4,16,32,256]{3,2,1,0:T(8,128)(2,1)}, u32[]{:S(2)}) copy-start(bf16[4,16,32,256]{3,2,1,0:T(8,128)(2,1)} %copy-done.4) | copy-start | bytes 3145732
  43.7 25.1 %all-to-all-start = ((bf16[16,336,128]{2,1,0:T(8,128)(2,1)}), bf16[16,336,128]{2,1,0:T(8,128)(2,1)}, u32[]{:S(2)}, u32[]{:S(2)}) async-start(bf16[16,336,128]{2,1,0:T(8,128)(2,1)} %bitcast.7), calls=%async_computation | async-start | bytes 2752512 | tf_op jit(solution)/shard_map/all_to_all | solution.py:310
  70.3 10.4 %copy-start.8 = (f32[1,8,32,256]{3,2,1,0:T(8,128)S(1)}, f32[1,8,32,256]{3,2,1,0:T(8,128)}, u32[]{:S(2)}) copy-start(f32[1,8,32,256]{3,2,1,0:T(8,128)} %copy-done.7) | copy-start | bytes 786436
  71.2 27.0 %all-to-all-start.1 = ((bf16[8,336,128]{2,1,0:T(8,128)(2,1)}), bf16[8,336,128]{2,1,0:T(8,128)(2,1)S(1)}, u32[]{:S(2)}, u32[]{:S(2)}) async-start(bf16[8,336,128]{2,1,0:T(8,128)(2,1)} %tile.4), calls=%async_computation.1 | async-start | bytes 1376256 | tf_op jit(solution)/shard_map/all_to_all | solution.py:310
  79.4 19.0 %collective-permute-start.3 = (bf16[2,16,32,256]{3,2,1,0:T(8,128)(2,1)S(1)}, bf16[2,16,32,256]{3,2,1,0:T(8,128)(2,1)S(1)}, u32[]{:S(2)}, u32[]{:S(2)}) collective-permute-start(bf16[2,16,32,256]{3,2,1,0:T(8,128)(2,1)S(1)} %slice.19), channel_id=1, source_target_pairs={{1,0},{2,1},{3,2},{4,3},{5,4},{6,5},{7,6},{9,8},{10,9},{11,10},{12... | collective-permute-start | bytes 1572872 | tf_op jit(solution)/shard_map/ppermute | solution.py:302
  80.7 17.7 %collective-permute-start.4 = (f32[1,8,32,256]{3,2,1,0:T(8,128)S(1)}, f32[1,8,32,256]{3,2,1,0:T(8,128)S(1)}, u32[]{:S(2)}, u32[]{:S(2)}) collective-permute-start(f32[1,8,32,256]{3,2,1,0:T(8,128)S(1)} %copy-done.8), channel_id=1, source_target_pairs={{0,1},{1,2},{2,3},{3,4},{4,5},{5,6},{6,7},{8,9},{9,10},{10,11},{11... | collective-permute-start | bytes 786440 | tf_op jit(solution)/shard_map/ppermute | solution.py:302
  98.4 1.3 copy-start.9
  99.7 8.4 %copy-start.2 = (bf16[3,3,3,128,128]{4,3,2,1,0:T(8,128)(2,1)S(1)}, bf16[3,3,3,128,128]{4,3,2,1,0:T(8,128)(2,1)}, u32[]{:S(2)}) copy-start(bf16[3,3,3,128,128]{4,3,2,1,0:T(8,128)(2,1)} %param.8) | copy-start | bytes 2654212
  99.7 25.0 %all-to-all-start.2 = ((bf16[16,336,128]{2,1,0:T(8,128)(2,1)}), bf16[16,336,128]{2,1,0:T(8,128)(2,1)S(1)}, u32[]{:S(2)}, u32[]{:S(2)}) async-start(bf16[16,336,128]{2,1,0:T(8,128)(2,1)} %tile.5), calls=%async_computation.2 | async-start | bytes 2752512 | tf_op jit(solution)/shard_map/all_to_all | solution.py:310
  108.1 1.2 copy-start.6
  124.7 7.4 %collective-permute-start.5 = (bf16[5376,128]{1,0:T(8,128)(2,1)S(1)}, bf16[5376,128]{1,0:T(8,128)(2,1)S(1)}, u32[]{:S(2)}, u32[]{:S(2)}) collective-permute-start(bf16[5376,128]{1,0:T(8,128)(2,1)S(1)} %bitcast.19), channel_id=1, source_target_pairs={{0,8},{8,0},{1,9},{9,1},{2,10},{10,2},{3,11},{11,3},{4,12},{12,4},... | collective-permute-start | bytes 4128776 | tf_op jit(solution)/shard_map/ppermute | solution.py:306

commit v3 on v2

--- a/solution.py
+++ b/solution.py
@@ -10,15 +10,17 @@
 from jax.sharding import PartitionSpec as P
 
 TM = ("y", "xh")
-DP = ("xl", "z", "c")
-XY = ("xl", "xh", "y")
+DP = ("xl", "zh", "zl", "c")
+NEAR = ("xl", "xh", "y", "zl")
 
 BF = jnp.bfloat16
 F32 = jnp.float32
 VMEM = pl.BlockSpec(memory_space=pltpu.VMEM)
 SMEM = pl.BlockSpec(memory_space=pltpu.SMEM)
 ANY = pl.BlockSpec(memory_space=pl.ANY)
+HBM = pl.BlockSpec(memory_space=pltpu.HBM)
 HALF = 42 * 128
+EARLY = 7
 
 
 def params(mib):
@@ -86,7 +88,7 @@
         dst[tap, 128 * r : 128 * r + 128, 128:256] = odd
 
 
-def kernel_weights(wconv_ref, wdown_ref, wc_ref, wa_ref):
+def kernel_weights(x_ref, wconv_ref, wdown_ref, wc_ref, wa_ref, late_ref, wide, xs):
     z = jnp.zeros((256, 128), BF)
     for tap in range(9):
         pair_weights(wc_ref, tap, [wconv_ref[3 * tap + b] for b in range(3)])
@@ -95,23 +97,33 @@
         wa_ref[tap, 0:256, 128:256] = w[2]
         wa_ref[tap, 256:512, 0:128] = z
         wa_ref[tap, 256:512, 128:256] = w[0]
-
-
-def call_weights(w_conv, w_down):
+    clear_edges(xs, 4)
+    for f in range(4):
+        spread(xs, f, *split_columns(wide.at[f % 2], x_ref[f]))
+    for f in range(2):
+        late_ref[f] = conv_frame(xs, f, wc_ref)
+
+
+def call_weights(x, w_conv, w_down):
     return pl.pallas_call(
         kernel_weights,
-        out_shape=(jax.ShapeDtypeStruct((9, 512, 256), BF),) * 2,
-        in_specs=[VMEM, VMEM],
-        out_specs=(VMEM, VMEM),
+        out_shape=(jax.ShapeDtypeStruct((9, 512, 256), BF),) * 2
+        + (jax.ShapeDtypeStruct((2, 512, 256), F32),),
+        in_specs=[VMEM] * 3,
+        out_specs=(VMEM,) * 3,
+        scratch_shapes=[
+            pltpu.VMEM((2, 16, 64, 128), F32),
+            pltpu.VMEM((4, 18, 32, 512), BF),
+        ],
         compiler_params=params(16),
         cost_estimate=cost(10**6, 8 * 10**6),
-    )(w_conv, w_down)
+    )(x, w_conv, w_down)
 
 
 TERMS = {0: ((0, 2), (1, 0)), 1: ((1, 1),), 2: ((1, 2), (2, 0)), 3: ((2, 1),)}
 
 
-def kernel_grads(core_ref, x_ref, before_ref, m_ref, next_ref, wc_ref, wa_ref, wd_ref,
+def kernel_grads(core_ref, x_ref, before_ref, m_ref, next_ref, wc_ref, wa_ref, late_ref, wd_ref,
                  hg_ref, own_ref, other_ref, enc_ref, part_ref,
                  wide, xs, ms, mt, acs, hgt, dact, sums, sems):
     core = core_ref[0]
@@ -127,7 +139,8 @@
         mt[:, 256 * t : 256 * t + 256] = turned(m.reshape(256, 256))
     acs[:, 0:1, 0:1] = jnp.zeros((4, 1, 1, 32, 384), BF)
     acs[:, 8:9, 1:2] = jnp.zeros((4, 1, 1, 32, 384), BF)
-    sums[1, HALF - 384 :] = jnp.zeros((384, 128), BF)
+    sums[0, HALF - 128 :] = jnp.zeros((128, 128), BF)
+    sums[1, HALF - 256 :] = jnp.zeros((256, 128), BF)
 
     for f in range(4):
         even = odd = None
@@ -142,7 +155,7 @@
         dact[f, :, 1] = odd.reshape(8, 32, 256)
 
     for f in range(4):
-        hidden = conv_frame(xs, f, wc_ref)
+        hidden = conv_frame(xs, f, wc_ref) if f < 2 else late_ref[f - 2]
         sig = 1.0 / (1.0 + jnp.exp(-hidden))
         act = (hidden * sig).reshape(8, 2, 32, 256)
         left = from_left(act[..., 128:256].reshape(16, 32, 128)).reshape(8, 2, 32, 128)
@@ -156,9 +169,8 @@
         hg_ref[f] = grad.astype(BF).reshape(16, 32, 256)
         hgt[:, 512 * f : 512 * f + 512] = grad.T.astype(BF)
 
-    def put(block, v):
-        half, at = divmod(128 * block, HALF)
-        sums[half, at : at + 128] = v
+    def put(half, block, v):
+        sums[half, 128 * block : 128 * block + 128] = v
 
     def tap(f, a):
         rows = (acs[f, 0:8, 0], acs[f, 0:8, 1], acs[f, 1:9, 0])[a]
@@ -172,8 +184,10 @@
             g = dot(m_t, right)
             for b in range(3):
                 block = g[:, 128 * b : 128 * b + 128].T.astype(BF)
-                put(27 + 9 * k + 3 * a + b, block[:, 0:128])
-                put(54 + 9 * k + 3 * a + b, block[:, 128:256])
+                at = 9 * k + 3 * a + b
+                half, first = (0, 27 + 2 * at) if at < EARLY else (1, 2 * (at - EARLY))
+                put(half, first, block[:, 0:128])
+                put(half, first + 1, block[:, 128:256])
 
     for k in range(3):
         for a in range(3):
@@ -182,7 +196,7 @@
             for b in range(3):
                 u, v = (2, 0, 1)[b], (0, 1, 3)[b]
                 both = g[0:128, 128 * u : 128 * u + 128] + g[128:256, 128 * v : 128 * v + 128]
-                put(9 * k + 3 * a + b, both.T.astype(BF))
+                put(0, 9 * k + 3 * a + b, both.T.astype(BF))
 
     send = pltpu.make_async_copy(sums.at[1 - core], other_ref, sems.at[0])
     keep = pltpu.make_async_copy(sums.at[core], own_ref, sems.at[1])
@@ -197,14 +211,14 @@
                     term = dot(tap(f, a), wd_ref[3 * k + a])
                     acc = term if acc is None else acc + term
         if t == 2:
-            part_ref[0] = acc.reshape(8, 32, 256)
+            part_ref[0] = acc.astype(BF).reshape(8, 32, 256)
         else:
             enc_ref[t] = acc.reshape(8, 32, 256)
     send.wait()
     keep.wait()
 
 
-def call_grads(core, x, before, m, after, wc, wa, wd):
+def call_grads(core, x, before, m, after, wc, wa, late, wd):
     return pl.pallas_call(
         kernel_grads,
         out_shape=(
@@ -212,9 +226,9 @@
             jax.ShapeDtypeStruct((HALF, 128), BF),
             jax.ShapeDtypeStruct((HALF, 128), BF),
             jax.ShapeDtypeStruct((2, 8, 32, 256), F32),
-            jax.ShapeDtypeStruct((1, 8, 32, 256), F32),
+            jax.ShapeDtypeStruct((1, 8, 32, 256), BF),
         ),
-        in_specs=[SMEM] + [VMEM] * 7,
+        in_specs=[SMEM] + [VMEM] * 8,
         out_specs=(VMEM, ANY, ANY, VMEM, VMEM),
         scratch_shapes=[
             pltpu.VMEM((2, 16, 64, 128), F32),
@@ -229,10 +243,12 @@
         ],
         compiler_params=params(40),
         cost_estimate=cost(12 * 10**9, 10**7),
-    )(core, x, before, m, after, wc, wa, wd)
-
-
-def kernel_clip(h_ref, after_ref, w_ref, out_ref, hs, wt, wide):
+    )(core, x, before, m, after, wc, wa, late, wd)
+
+
+def kernel_clip(h_ref, after_ref, w_ref, own_ref, part_ref, out_ref, enc_ref, hs, wt, wide):
+    enc_ref[0] = (own_ref[0] + part_ref[0].astype(F32)).astype(BF)
+    enc_ref[1] = own_ref[1].astype(BF)
     clear_edges(hs, 6)
     for tap in range(9):
         pair_weights(wt, tap, [turned(w_ref[3 * (8 - tap) + 2 - b]) for b in range(3)])
@@ -246,12 +262,15 @@
         out_ref[f] = wide[f % 2].astype(BF)
 
 
-def call_clip(h, after, w):
+def call_clip(h, after, w, enc, part):
     return pl.pallas_call(
         kernel_clip,
-        out_shape=jax.ShapeDtypeStruct((4, 16, 64, 128), BF),
-        in_specs=[VMEM] * 3,
-        out_specs=VMEM,
+        out_shape=(
+            jax.ShapeDtypeStruct((4, 16, 64, 128), BF),
+            jax.ShapeDtypeStruct((2, 8, 32, 256), BF),
+        ),
+        in_specs=[VMEM] * 5,
+        out_specs=(VMEM, VMEM),
         scratch_shapes=[
             pltpu.VMEM((6, 18, 32, 512), BF),
             pltpu.VMEM((9, 512, 256), BF),
@@ -259,41 +278,88 @@
         ],
         compiler_params=params(32),
         cost_estimate=cost(5 * 10**9, 5 * 10**6),
-    )(h, after, w)
-
-
-def kernel_out(scale, core_ref, own_ref, other_ref, conv_ref, down_ref):
-    def write(halves):
-        for block in range(81):
-            half, at = divmod(128 * block, HALF)
-            v = halves[half][at : at + 128].astype(F32) * scale
-            which, tap = divmod(block, 27)
-            if which == 0:
-                conv_ref[tap] = v
-            else:
-                down_ref[tap, :, 128 * (which - 1) : 128 * which] = v
-
-    @pl.when(core_ref[0] == 0)
+    )(h, after, w, enc, part)
+
+
+def write_half(half, scale, src, conv_ref, down_ref, conv, down, sems):
+    def block(at):
+        return src[128 * at : 128 * at + 128].astype(F32) * scale
+
+    @pl.when(half == 0)
     def _():
-        write((own_ref, other_ref))
-
-    @pl.when(core_ref[0] == 1)
+        for at in range(27):
+            conv[at] = block(at)
+        to_conv = pltpu.make_async_copy(conv, conv_ref, sems.at[0])
+        to_conv.start()
+        for at in range(EARLY):
+            down[at, :, 0:128] = block(27 + 2 * at)
+            down[at, :, 128:256] = block(28 + 2 * at)
+        to_down = pltpu.make_async_copy(down.at[0:EARLY], down_ref.at[0:EARLY], sems.at[1])
+        to_down.start()
+        to_conv.wait()
+        to_down.wait()
+
+    @pl.when(half == 1)
     def _():
-        write((other_ref, own_ref))
-
-
-def call_out(core, own, other, scale):
+        pieces = ((0, 7), (7, 14), (14, 27 - EARLY))
+        copies = []
+        for i, (first, last) in enumerate(pieces):
+            for at in range(first, last):
+                down[at, :, 0:128] = block(2 * at)
+                down[at, :, 128:256] = block(2 * at + 1)
+            target = down_ref.at[EARLY + first : EARLY + last]
+            copies.append(pltpu.make_async_copy(down.at[first:last], target, sems.at[i]))
+            copies[-1].start()
+        for copy in copies:
+            copy.wait()
+
+
+def kernel_own(scale, core_ref, src, conv_ref, down_ref, conv, down, sems):
+    write_half(core_ref[0], scale, src, conv_ref, down_ref, conv, down, sems)
+
+
+def kernel_other(scale, core_ref, src, conv_in, down_in, conv_ref, down_ref, conv, down, sems):
+    write_half(1 - core_ref[0], scale, src, conv_ref, down_ref, conv, down, sems)
+
+
+def call_out(kernel, core, half, scale, begun=()):
     return pl.pallas_call(
-        functools.partial(kernel_out, scale),
-        out_shape=(
-            jax.ShapeDtypeStruct((27, 128, 128), F32),
-            jax.ShapeDtypeStruct((27, 128, 256), F32),
-        ),
-        in_specs=[SMEM, VMEM, VMEM],
-        out_specs=(VMEM, VMEM),
-        compiler_params=params(32),
-        cost_estimate=cost(10**6, 8 * 10**6),
-    )(core, own, other)
+        functools.partial(kernel, scale),
+        out_shape=(pltpu.HBM((27, 128, 128), F32), pltpu.HBM((27, 128, 256), F32)),
+        in_specs=[SMEM, VMEM] + [HBM] * len(begun),
+        out_specs=(HBM, HBM),
+        input_output_aliases={2: 0, 3: 1} if begun else {},
+        scratch_shapes=[
+            pltpu.VMEM((27, 128, 128), F32),
+            pltpu.VMEM((27 - EARLY, 128, 256), F32),
+            pltpu.SemaphoreType.DMA((3,)),
+        ],
+        compiler_params=params(16),
+        cost_estimate=cost(10**6, 4 * 10**6),
+    )(core, half, *begun)
+
+
+CHUNK = HALF // 32
+
+
+def kernel_fold(in_ref, out_ref):
+    total = in_ref[0].astype(F32)
+    for i in range(1, in_ref.shape[0]):
+        total += in_ref[i].astype(F32)
+    total = total.astype(BF)
+    for i in range(out_ref.shape[0]):
+        out_ref[i] = total
+
+
+def call_fold(v, copies):
+    return pl.pallas_call(
+        kernel_fold,
+        out_shape=jax.ShapeDtypeStruct((copies, CHUNK, 128), BF),
+        in_specs=[VMEM],
+        out_specs=VMEM,
+        compiler_params=params(8),
+        cost_estimate=cost(10**6, 10**6),
+    )(v)
 
 
 def shifted(block, distance):
@@ -308,15 +374,6 @@
 
 def exchange(value, axes):
     return lax.all_to_all(value, axes, 0, 0, tiled=True)
-
-
-def add_up(value, parts):
-    split = value.reshape((parts, value.shape[0] // parts, 128))
-    return jnp.sum(split.astype(F32), axis=0).astype(BF)
-
-
-def gather(value, axes, parts):
-    return exchange(jnp.tile(value, (parts, 1)), axes)
 
 
 def shards(clips, cotangent, clip_frames, w_conv, w_down):
@@ -331,29 +388,32 @@
     masked_after = shifted(masked[:1], -1)
     taps_conv = w_conv.reshape(27, 128, 128)
     taps_down = w_down.reshape(9, 384, 256)
-    wc, wa = call_weights(taps_conv, taps_down)
+    wc, wa, late = call_weights(clips[0], taps_conv, taps_down)
     hg, own, other, enc, part = call_grads(
-        core, clips[0], before, masked, masked_after, wc, wa, taps_down
+        core, clips[0], before, masked, masked_after, wc, wa, late, taps_down
     )
     own = (own.astype(F32) + swapped(other).astype(F32)).astype(BF)
-    own = add_up(exchange(own, XY), 16)
-    own, ends, part = lax.optimization_barrier((own, hg[:2], part))
+    own, part = lax.optimization_barrier((own, part))
+    part = shifted(part, 1)
+    own = exchange(own.reshape(32, CHUNK, 128), NEAR)
+    own, part = lax.optimization_barrier((own, part))
+    own = call_fold(own, 4)
+    own, ends = lax.optimization_barrier((own, hg[:2]))
     after = shifted(ends, -1)
-    part = shifted(part, 1)
-    own = add_up(gather(own, "z", 8), 8)
-    own, after, part = lax.optimization_barrier((own, after, part))
-    own = gather(own, XY, 16)
-    clip_grad = call_clip(hg, after, taps_conv)[None]
-    own, clip_grad = lax.optimization_barrier((own, clip_grad))
-    encoded = jnp.concatenate([enc[:1] + part, enc[1:]]).astype(BF)[None]
+    own = call_fold(exchange(own, "zh"), 32)
+    own, after = lax.optimization_barrier((own, after))
+    own = exchange(own, NEAR).reshape(HALF, 128)
+    clip_grad, encoded = call_clip(hg, after, taps_conv, enc, part)
+    own, clip_grad, encoded = lax.optimization_barrier((own, clip_grad, encoded))
     scale = 1.0 / math.sqrt(lax.axis_size(DP) * frames * lax.axis_size(TM) * rows * cols)
-    conv_grad, down_grad = call_out(core, own, swapped(own), scale)
-    return (encoded, clip_grad, conv_grad.reshape(w_conv.shape), down_grad.reshape(w_down.shape))
+    begun = call_out(kernel_own, core, own, scale)
+    conv_grad, down_grad = call_out(kernel_other, core, swapped(own), scale, begun)
+    return (encoded[None], clip_grad[None], conv_grad.reshape(w_conv.shape), down_grad.reshape(w_down.shape))
 
 
 def solution(mesh):
-    fine = Mesh(mesh.devices.reshape(2, 8, 2, 4, 2), DP + TM)
-    spread_out = P(DP, TM, None, None, None)
-    in_specs = (spread_out, spread_out, P(DP), P(), P())
-    out_specs = (spread_out, spread_out, P(), P())
+    fine = Mesh(mesh.devices.reshape(2, 4, 2, 2, 4, 2), DP + TM)
+    parts = P(DP, TM, None, None, None)
+    in_specs = (parts, parts, P(DP), P(), P())
+    out_specs = (parts, parts, P(), P())
     return jax.shard_map(shards, mesh=fine, in_specs=in_specs, out_specs=out_specs, check_vma=False)

time: 135 us -> 126 us (0.933)
  waiting for transfers between devices: 53.5 us -> 36.9 us
  blocking collectives: 0 us -> 14.9 us
  starting transfers between devices: 43.1 us -> 35.2 us
  other arithmetic: 5.82 us -> 2.48 us
  Pallas kernels: 25 us -> 26.7 us
  local copies, waits for them, and re-layouts: 5.88 us -> 7.53 us
    all_to_all x3 -> x2, waiting for transfers between devices: 39.5 us -> 14.5 us  [exchange(): return lax.all_to_all(value, axes, 0, 0, tiled=True)]
    all_to_all x0 -> x1, blocking collectives: none -> 14.9 us  [exchange(): return lax.all_to_all(value, axes, 0, 0, tiled=True)]
    ppermute x4, waiting for transfers between devices: 10.2 us -> 18.5 us  [shifted(): return lax.ppermute(block, TM, route)]
    all_to_all x3 -> x2, starting transfers between devices: 23.3 us -> 16.9 us  [exchange(): return lax.all_to_all(value, axes, 0, 0, tiled=True)]
    unnamed x20 -> x18, local copies, waits for them, and re-layouts: 2.42 us -> 5.53 us
    pallas_call x1, Pallas kernels: 15.1 us -> 12.8 us  [call_grads(): pl.pallas_call(kernel_grads, out_shape=(jax.ShapeDtypeStruct((4, 16, 32,...]
    another operation x2 -> x0, local copies, waits for them, and re-layouts: 2.19 us -> none  [gather(): return exchange(jnp.tile(value, (parts, 1)), axes)]
    pallas_call x1, Pallas kernels: 0.88 us -> 3.01 us  [call_weights(): pl.pallas_call(kernel_weights, out_shape=(jax.ShapeDtypeStruct((9, 512, 2...]
  transfers between devices with their start and end apart: 9 -> 8, of which waited for: 6 -> 6; matrix products, arithmetic and copies ran while one was open for 2% -> 2% of each run, Pallas kernels for 5% -> 10%
where the time goes in v3:
time: 126 us; the launch traced here: 125 us
  waiting for transfers between devices  36.9 us (29%)
  starting transfers between devices  35.2 us (28%)
  Pallas kernels  26.7 us (21%)
  blocking collectives  14.9 us (12%)
  local copies, waits for them, and re-layouts  7.53 us (6%)
  other arithmetic  2.48 us (2%)
  between operations  1.6 us (1%)
    ppermute x4, waiting for transfers between devices, shifted(): return lax.ppermute(block, TM, route)  18.5 us
    all_to_all x2, starting transfers between devices, exchange(): return lax.all_to_all(value, axes, 0, 0, tiled=True)  16.9 us
    all_to_all x1, blocking collectives, exchange(): return lax.all_to_all(value, axes, 0, 0, tiled=True)  14.9 us
    all_to_all x2, waiting for transfers between devices, exchange(): return lax.all_to_all(value, axes, 0, 0, tiled=True)  14.5 us
    pallas_call x1, Pallas kernels, call_grads(): pl.pallas_call(kernel_grads, out_shape=(jax.ShapeDtypeStruct((4, 16, 32,...  12.8 us
    ppermute x4, starting transfers between devices, shifted(): return lax.ppermute(block, TM, route)  12.7 us
    pallas_call x1, Pallas kernels, call_clip(): pl.pallas_call(kernel_clip, out_shape=(jax.ShapeDtypeStruct((4, 16, 64, 1...  6.3 us
    unnamed x18, local copies, waits for them, and re-layouts  5.53 us
  transfers between devices with their start and end apart: 8, of which 6 were waited for; matrix products, arithmetic and copies ran while one was open for 2% of the time, Pallas kernels for 10%

profile of v3, /device:TPU:1, one launch (start us, length us, event | category | flops | bytes accessed | tf_op | source)
XLA Modules:
  0.0 125.2 jit_solution(8376974418250295501)
XLA Ops:
  1.8 5.5 %collective-permute-start = (bf16[2,16,64,128]{3,2,1,0:T(8,128)(2,1)S(1)}, bf16[2,16,64,128]{3,2,1,0:T(8,128)(2,1)S(1)}, u32[]{:S(2)}, u32[]{:S(2)}) collective-permute-start(bf16[2,16,64,128]{3,2,1,0:T(8,128)(2,1)S(1)} %slice_bitcast_fusion), channel_id=1, source_target_pairs={{0,1},{1,2},{2,3},{3,4},{4,5},{5,6},{6,7},{8,9},{9,10},{10,11},{11... | collective-permute-start | bytes 1572872 | tf_op jit(solution)/shard_map/ppermute | solution.py:368
  9.1 1.3 %collective-permute-start.1 = (bf16[1,8,32,256]{3,2,1,0:T(8,128)(2,1)S(1)}, bf16[1,8,32,256]{3,2,1,0:T(8,128)(2,1)S(1)}, u32[]{:S(2)}, u32[]{:S(2)}) collective-permute-start(bf16[1,8,32,256]{3,2,1,0:T(8,128)(2,1)S(1)} %slice.12), channel_id=1, source_target_pairs={{1,0},{2,1},{3,2},{4,3},{5,4},{6,5},{7,6},{9,8},{10,9},{11,10},{12... | collective-permute-start | bytes 393224 | tf_op jit(solution)/shard_map/ppermute | solution.py:368
  10.4 1.5 %copy-done.1 = bf16[3,3,3,128,256]{4,3,2,1,0:T(8,128)(2,1)S(1)} copy-done((bf16[3,3,3,128,256]{4,3,2,1,0:T(8,128)(2,1)S(1)}, bf16[3,3,3,128,256]{4,3,2,1,0:T(8,128)(2,1)}, u32[]{:S(2)}) %copy-start.1) | copy-done | bytes 1769496
  11.9 1.2 copy-done.3
  13.0 3.0 %shard_map.84 = (bf16[9,512,256]{2,1,0:T(8,128)(2,1)S(1)}, bf16[9,512,256]{2,1,0:T(8,128)(2,1)S(1)}, f32[2,512,256]{2,1,0:T(8,128)S(1)}) custom-call(bf16[4,16,64,128]{3,2,1,0:T(8,128)(2,1)S(1)} %bitcast.18, bf16[27,128,128]{2,1,0:T(8,128)(2,1)S(1)} %bitcast.22, bf16[9,384,256]{2,1,0:T(8,128)(2,1)S(1)} %bitcast.20), custom_call_target="tpu_custom_call" | custom-call | flops 1000000 | bytes 8000000 | tf_op jit(solution)/shard_map/pallas_call | solution.py:108
  16.0 6.6 %collective-permute-done.1.next_ref = bf16[1,8,32,256]{3,2,1,0:T(8,128)(2,1)S(1)} collective-permute-done((bf16[1,8,32,256]{3,2,1,0:T(8,128)(2,1)S(1)}, bf16[1,8,32,256]{3,2,1,0:T(8,128)(2,1)S(1)}, u32[]{:S(2)}, u32[]{:S(2)}) %collective-permute-start.1) | collective-permute-done | bytes 131104 | tf_op jit(solution)/shard_map/ppermute | solution.py:368
  22.7 12.8 %shard_map.85 = (bf16[4,16,32,256]{3,2,1,0:T(8,128)(2,1)S(1)}, bf16[5376,128]{1,0:T(8,128)(2,1)S(1)}, bf16[5376,128]{1,0:T(8,128)(2,1)S(1)}, f32[2,8,32,256]{3,2,1,0:T(8,128)S(1)}, bf16[1,8,32,256]{3,2,1,0:T(8,128)(2,1)S(1)}) custom-call(s32[1]{0:T(128)} %bitcast.core_ref, bf16[4,16,64,128]{3,2,1,0:T(8,128)(2,1)S(1)} %bitcast.19, ...), custom_call_target="tpu_custom_call" | custom-call | flops 12000000000 | bytes 10000000 | tf_op jit(solution)/shard_map/pallas_call | solution.py:222
  35.5 1.6 %collective-permute-start.2 = (bf16[5376,128]{1,0:T(8,128)(2,1)S(1)}, bf16[5376,128]{1,0:T(8,128)(2,1)S(1)}, u32[]{:S(2)}, u32[]{:S(2)}) collective-permute-start(bf16[5376,128]{1,0:T(8,128)(2,1)S(1)} %get-tuple-element.35), channel_id=1, source_target_pairs={{0,8},{8,0},{1,9},{9,1},{2,10},{10,2},{3,11},{11,3},{4,12},{12,4},... | collective-permute-start | bytes 4128776 | tf_op jit(solution)/shard_map/ppermute | solution.py:372
  37.1 2.8 %collective-permute-done.2 = bf16[5376,128]{1,0:T(8,128)(2,1)S(1)} collective-permute-done((bf16[5376,128]{1,0:T(8,128)(2,1)S(1)}, bf16[5376,128]{1,0:T(8,128)(2,1)S(1)}, u32[]{:S(2)}, u32[]{:S(2)}) %collective-permute-start.2) | collective-permute-done | bytes 1376288 | tf_op jit(solution)/shard_map/ppermute | solution.py:372
  39.9 1.4 %add_convert_fusion = bf16[5376,128]{1,0:T(8,128)(2,1)} fusion(bf16[5376,128]{1,0:T(8,128)(2,1)S(1)} %collective-permute-done.2, bf16[5376,128]{1,0:T(8,128)(2,1)S(1)} %get-tuple-element.34), kind=kLoop, calls=%fused_computation | loop fusion | flops 2752512 | bytes 4128768 | tf_op jit(solution)/shard_map/convert_element_type | solution.py:395
  41.3 8.1 %all-to-all-start = ((bf16[32,168,128]{2,1,0:T(8,128)(2,1)}), bf16[32,168,128]{2,1,0:T(8,128)(2,1)S(1)}, u32[]{:S(2)}, u32[]{:S(2)}) async-start(bf16[32,168,128]{2,1,0:T(8,128)(2,1)} %bitcast.24), calls=%async_computation | async-start | bytes 2752512 | tf_op jit(solution)/shard_map/all_to_all | solution.py:376
  49.4 4.6 %collective-permute-start.3 = (bf16[1,8,32,256]{3,2,1,0:T(8,128)(2,1)S(1)}, bf16[1,8,32,256]{3,2,1,0:T(8,128)(2,1)S(1)}, u32[]{:S(2)}, u32[]{:S(2)}) collective-permute-start(bf16[1,8,32,256]{3,2,1,0:T(8,128)(2,1)S(1)} %get-tuple-element.38), channel_id=1, source_target_pairs={{0,1},{1,2},{2,3},{3,4},{4,5},{5,6},{6,7},{8,9},{9,10},{10,11},{11... | collective-permute-start | bytes 393224 | tf_op jit(solution)/shard_map/ppermute | solution.py:368
  54.9 11.9 %collective-permute-done.3.part_ref = bf16[1,8,32,256]{3,2,1,0:T(8,128)(2,1)S(1)} collective-permute-done((bf16[1,8,32,256]{3,2,1,0:T(8,128)(2,1)S(1)}, bf16[1,8,32,256]{3,2,1,0:T(8,128)(2,1)S(1)}, u32[]{:S(2)}, u32[]{:S(2)}) %collective-permute-start.3) | collective-permute-done | bytes 131104 | tf_op jit(solution)/shard_map/ppermute | solution.py:368
  66.8 4.0 %all-to-all-done.in_ref = bf16[32,168,128]{2,1,0:T(8,128)(2,1)S(1)} async-done(((bf16[32,168,128]{2,1,0:T(8,128)(2,1)}), bf16[32,168,128]{2,1,0:T(8,128)(2,1)S(1)}, u32[]{:S(2)}, u32[]{:S(2)}) %all-to-all-start) | async-done | bytes 1376288 | tf_op jit(solution)/shard_map/all_to_all | solution.py:376
  71.0 1.3 %collective-permute-start.4 = (bf16[2,16,32,256]{3,2,1,0:T(8,128)(2,1)}, bf16[2,16,32,256]{3,2,1,0:T(8,128)(2,1)S(1)}, u32[]{:S(2)}, u32[]{:S(2)}) collective-permute-start(bf16[2,16,32,256]{3,2,1,0:T(8,128)(2,1)} %slice.11), channel_id=1, source_target_pairs={{1,0},{2,1},{3,2},{4,3},{5,4},{6,5},{7,6},{9,8},{10,9},{11,10},{12... | collective-permute-start | bytes 1572872 | tf_op jit(solution)/shard_map/ppermute | solution.py:368
  72.3 14.9 %all_to_all.15.in_ref = bf16[4,168,128]{2,1,0:T(8,128)(2,1)S(1)} all-to-all(bf16[4,168,128]{2,1,0:T(8,128)(2,1)S(1)} %shard_map.86), channel_id=1, replica_groups=mesh['xl'=2,'zh'=4,'zl'=2,'c'=2,'y'=4,'xh'=2] {'zh'}, dimensions={0} | all-to-all | bytes 344064 | tf_op jit(solution)/shard_map/all_to_all | solution.py:376
  87.2 1.2 shard_map.87
  89.1 8.8 %all-to-all-start.2 = ((bf16[32,168,128]{2,1,0:T(8,128)(2,1)}), bf16[32,168,128]{2,1,0:T(8,128)(2,1)S(1)}, u32[]{:S(2)}, u32[]{:S(2)}) async-start(bf16[32,168,128]{2,1,0:T(8,128)(2,1)} %shard_map.87), calls=%async_computation.2 | async-start | bytes 2752512 | tf_op jit(solution)/shard_map/all_to_all | solution.py:376
  100.1 6.3 %shard_map.88 = (bf16[4,16,64,128]{3,2,1,0:T(8,128)(2,1)}, bf16[2,8,32,256]{3,2,1,0:T(8,128)(2,1)}) custom-call(bf16[4,16,32,256]{3,2,1,0:T(8,128)(2,1)S(1)} %get-tuple-element.40.h_ref, bf16[2,16,32,256]{3,2,1,0:T(8,128)(2,1)S(1)} %copy-done.6, bf16[27,128,128]{2,1,0:T(8,128)(2,1)S(1)} %bitcast.23, f32[2,8,32,256]{3,2,1,0:T(8,128)S(1)} %copy-done.8, ...), custom_call_target="tpu_custom_call" | custom-call | flops 5000000000 | bytes 5000000 | tf_op jit(solution)/shard_map/pallas_call | solution.py:266
  106.4 10.4 %all-to-all-done.2 = bf16[32,168,128]{2,1,0:T(8,128)(2,1)S(1)} async-done(((bf16[32,168,128]{2,1,0:T(8,128)(2,1)}), bf16[32,168,128]{2,1,0:T(8,128)(2,1)S(1)}, u32[]{:S(2)}, u32[]{:S(2)}) %all-to-all-start.2) | async-done | bytes 1376288 | tf_op jit(solution)/shard_map/all_to_all | solution.py:376
  116.8 3.9 %collective-permute-start.5 = (bf16[5376,128]{1,0:T(8,128)(2,1)S(1)}, bf16[5376,128]{1,0:T(8,128)(2,1)S(1)}, u32[]{:S(2)}, u32[]{:S(2)}) collective-permute-start(bf16[5376,128]{1,0:T(8,128)(2,1)S(1)} %bitcast.16), channel_id=1, source_target_pairs={{0,8},{8,0},{1,9},{9,1},{2,10},{10,2},{3,11},{11,3},{4,12},{12,4},... | collective-permute-start | bytes 4128776 | tf_op jit(solution)/shard_map/ppermute | solution.py:372
  120.7 1.6 %shard_map.89 = (f32[27,128,128]{2,1,0:T(8,128)}, f32[27,128,256]{2,1,0:T(8,128)}) custom-call(s32[1]{0:T(128)} %bitcast.core_ref, bf16[5376,128]{1,0:T(8,128)(2,1)S(1)} %bitcast.17), custom_call_target="tpu_custom_call" | custom-call | flops 1000000 | bytes 4000000 | tf_op jit(solution)/shard_map/pallas_call | solution.py:326
  122.2 1.2 collective-permute-done.5.src
  123.4 1.6 %shard_map.90 = (f32[27,128,128]{2,1,0:T(8,128)}, f32[27,128,256]{2,1,0:T(8,128)}) custom-call(s32[1]{0:T(128)} %bitcast.core_ref, bf16[5376,128]{1,0:T(8,128)(2,1)S(1)} %collective-permute-done.5.src, f32[27,128,128]{2,1,0:T(8,128)} %get-tuple-element.52.conv_in, ...), custom_call_target="tpu_custom_call", output_to_operand_aliasing={{0}: (2, {}), {1}: (3, {})} | custom-call | flops 1000000 | bytes 4000000 | tf_op jit(solution)/shard_map/pallas_call | solution.py:326
  (24 shorter events, 6.2 us)
Async XLA Ops:
  0.6 9.7 %copy-start = (bf16[1,4,16,64,128]{4,3,2,1,0:T(8,128)(2,1)S(1)}, bf16[1,4,16,64,128]{4,3,2,1,0:T(8,128)(2,1)}, u32[]{:S(2)}) copy-start(bf16[1,4,16,64,128]{4,3,2,1,0:T(8,128)(2,1)} %param.5) | copy-start | bytes 3145732
  1.8 20.8 %collective-permute-start = (bf16[2,16,64,128]{3,2,1,0:T(8,128)(2,1)S(1)}, bf16[2,16,64,128]{3,2,1,0:T(8,128)(2,1)S(1)}, u32[]{:S(2)}, u32[]{:S(2)}) collective-permute-start(bf16[2,16,64,128]{3,2,1,0:T(8,128)(2,1)S(1)} %slice_bitcast_fusion), channel_id=1, source_target_pairs={{0,1},{1,2},{2,3},{3,4},{4,5},{5,6},{6,7},{8,9},{9,10},{10,11},{11... | collective-permute-start | bytes 1572872 | tf_op jit(solution)/shard_map/ppermute | solution.py:368
  9.1 13.6 %collective-permute-start.1 = (bf16[1,8,32,256]{3,2,1,0:T(8,128)(2,1)S(1)}, bf16[1,8,32,256]{3,2,1,0:T(8,128)(2,1)S(1)}, u32[]{:S(2)}, u32[]{:S(2)}) collective-permute-start(bf16[1,8,32,256]{3,2,1,0:T(8,128)(2,1)S(1)} %slice.12), channel_id=1, source_target_pairs={{1,0},{2,1},{3,2},{4,3},{5,4},{6,5},{7,6},{9,8},{10,9},{11,10},{12... | collective-permute-start | bytes 393224 | tf_op jit(solution)/shard_map/ppermute | solution.py:368
  10.4 1.5 %copy-start.1 = (bf16[3,3,3,128,256]{4,3,2,1,0:T(8,128)(2,1)S(1)}, bf16[3,3,3,128,256]{4,3,2,1,0:T(8,128)(2,1)}, u32[]{:S(2)}) copy-start(bf16[3,3,3,128,256]{4,3,2,1,0:T(8,128)(2,1)} %param.9) | copy-start | bytes 5308420
  11.9 1.2 copy-start.3
  13.0 9.6 %copy-start.2 = (bf16[3,3,3,128,256]{4,3,2,1,0:T(8,128)(2,1)S(1)}, bf16[3,3,3,128,256]{4,3,2,1,0:T(8,128)(2,1)}, u32[]{:S(2)}) copy-start(bf16[3,3,3,128,256]{4,3,2,1,0:T(8,128)(2,1)} %param.9) | copy-start | bytes 5308420
  35.5 5.8 %copy-start.7 = (f32[2,8,32,256]{3,2,1,0:T(8,128)}, f32[2,8,32,256]{3,2,1,0:T(8,128)S(1)}, u32[]{:S(2)}) copy-start(f32[2,8,32,256]{3,2,1,0:T(8,128)S(1)} %get-tuple-element.45.own_ref) | copy-start | bytes 1572868
  35.5 4.4 %collective-permute-start.2 = (bf16[5376,128]{1,0:T(8,128)(2,1)S(1)}, bf16[5376,128]{1,0:T(8,128)(2,1)S(1)}, u32[]{:S(2)}, u32[]{:S(2)}) collective-permute-start(bf16[5376,128]{1,0:T(8,128)(2,1)S(1)} %get-tuple-element.35), channel_id=1, source_target_pairs={{0,8},{8,0},{1,9},{9,1},{2,10},{10,2},{3,11},{11,3},{4,12},{12,4},... | collective-permute-start | bytes 4128776 | tf_op jit(solution)/shard_map/ppermute | solution.py:372
  41.3 29.5 %all-to-all-start = ((bf16[32,168,128]{2,1,0:T(8,128)(2,1)}), bf16[32,168,128]{2,1,0:T(8,128)(2,1)S(1)}, u32[]{:S(2)}, u32[]{:S(2)}) async-start(bf16[32,168,128]{2,1,0:T(8,128)(2,1)} %bitcast.24), calls=%async_computation | async-start | bytes 2752512 | tf_op jit(solution)/shard_map/all_to_all | solution.py:376
  49.4 17.3 %collective-permute-start.3 = (bf16[1,8,32,256]{3,2,1,0:T(8,128)(2,1)S(1)}, bf16[1,8,32,256]{3,2,1,0:T(8,128)(2,1)S(1)}, u32[]{:S(2)}, u32[]{:S(2)}) collective-permute-start(bf16[1,8,32,256]{3,2,1,0:T(8,128)(2,1)S(1)} %get-tuple-element.38), channel_id=1, source_target_pairs={{0,1},{1,2},{2,3},{3,4},{4,5},{5,6},{6,7},{8,9},{9,10},{10,11},{11... | collective-permute-start | bytes 393224 | tf_op jit(solution)/shard_map/ppermute | solution.py:368
  71.0 17.4 %collective-permute-start.4 = (bf16[2,16,32,256]{3,2,1,0:T(8,128)(2,1)}, bf16[2,16,32,256]{3,2,1,0:T(8,128)(2,1)S(1)}, u32[]{:S(2)}, u32[]{:S(2)}) collective-permute-start(bf16[2,16,32,256]{3,2,1,0:T(8,128)(2,1)} %slice.11), channel_id=1, source_target_pairs={{1,0},{2,1},{3,2},{4,3},{5,4},{6,5},{7,6},{9,8},{10,9},{11,10},{12... | collective-permute-start | bytes 1572872 | tf_op jit(solution)/shard_map/ppermute | solution.py:368
  88.3 9.6 %copy-start.4 = (bf16[3,3,3,128,128]{4,3,2,1,0:T(8,128)(2,1)S(1)}, bf16[3,3,3,128,128]{4,3,2,1,0:T(8,128)(2,1)}, u32[]{:S(2)}) copy-start(bf16[3,3,3,128,128]{4,3,2,1,0:T(8,128)(2,1)} %param.8) | copy-start | bytes 2654212
  88.3 0.8 copy-start.5
  89.1 27.7 %all-to-all-start.2 = ((bf16[32,168,128]{2,1,0:T(8,128)(2,1)}), bf16[32,168,128]{2,1,0:T(8,128)(2,1)S(1)}, u32[]{:S(2)}, u32[]{:S(2)}) async-start(bf16[32,168,128]{2,1,0:T(8,128)(2,1)} %shard_map.87), calls=%async_computation.2 | async-start | bytes 2752512 | tf_op jit(solution)/shard_map/all_to_all | solution.py:376
  98.0 1.0 copy-start.6
  99.0 1.0 copy-start.8
  116.8 6.6 %collective-permute-start.5 = (bf16[5376,128]{1,0:T(8,128)(2,1)S(1)}, bf16[5376,128]{1,0:T(8,128)(2,1)S(1)}, u32[]{:S(2)}, u32[]{:S(2)}) collective-permute-start(bf16[5376,128]{1,0:T(8,128)(2,1)S(1)} %bitcast.16), channel_id=1, source_target_pairs={{0,8},{8,0},{1,9},{9,1},{2,10},{10,2},{3,11},{11,3},{4,12},{12,4},... | collective-permute-start | bytes 4128776 | tf_op jit(solution)/shard_map/ppermute | solution.py:372

commit v4 on v3

--- a/solution.py
+++ b/solution.py
@@ -11,7 +11,7 @@
 
 TM = ("y", "xh")
 DP = ("xl", "zh", "zl", "c")
-NEAR = ("xl", "xh", "y", "zl")
+NEAR = ("zl", "y", "xl", "xh")
 
 BF = jnp.bfloat16
 F32 = jnp.float32
@@ -70,11 +70,11 @@
     dst[:, 17:18] = z
 
 
-def conv_frame(src, f, w_ref):
+def conv_frame(frames, w_ref):
     acc = None
     for k in range(3):
         for a in range(3):
-            lhs = src[f + k, a : a + 16].reshape(512, 512)
+            lhs = frames[k][a : a + 16].reshape(512, 512)
             term = dot(lhs, w_ref[3 * k + a])
             acc = term if acc is None else acc + term
     return acc
@@ -88,100 +88,144 @@
         dst[tap, 128 * r : 128 * r + 128, 128:256] = odd
 
 
-def kernel_weights(x_ref, wconv_ref, wdown_ref, wc_ref, wa_ref, late_ref, wide, xs):
+def both_weights(wc_ref, wa_ref, wconv_ref, wd_ref):
     z = jnp.zeros((256, 128), BF)
     for tap in range(9):
         pair_weights(wc_ref, tap, [wconv_ref[3 * tap + b] for b in range(3)])
-        w = [turned(wdown_ref[tap, 128 * b : 128 * b + 128]) for b in range(3)]
+        w = [turned(wd_ref[tap, 128 * b : 128 * b + 128]) for b in range(3)]
         wa_ref[tap, 0:256, 0:128] = w[1]
         wa_ref[tap, 0:256, 128:256] = w[2]
         wa_ref[tap, 256:512, 0:128] = z
         wa_ref[tap, 256:512, 128:256] = w[0]
-    clear_edges(xs, 4)
+
+
+def up_terms(ms, t, k, wa_ref):
+    here = ms[t, 0:8].reshape(256, 512)
+    below = ms[t, 1:9].reshape(256, 512)
+    even = dot(here, wa_ref[3 * k + 1])
+    odd = dot(here, wa_ref[3 * k + 2]) + dot(below, wa_ref[3 * k])
+    return even.reshape(8, 32, 256), odd.reshape(8, 32, 256)
+
+
+def spread_out(ms, t, m):
+    ms[t, 0:8, :, 0:256] = m
+    ms[t, 0:8, :, 256:512] = from_right(m.astype(F32)).astype(BF)
+    ms[t, 8:9] = jnp.zeros((1, 32, 512), BF)
+
+
+def activate(hidden, acs, f):
+    sig = 0.5 * jnp.tanh(0.5 * hidden) + 0.5
+    act = (hidden * sig).reshape(8, 2, 32, 256)
+    left = from_left(act[..., 128:256].reshape(16, 32, 128)).reshape(8, 2, 32, 128)
+    actb = act.astype(BF)
+    leftb = left.astype(BF)
+    acs[f, 0:1, 0:1] = jnp.zeros((1, 1, 32, 384), BF)
+    acs[f, 8:9, 1:2] = jnp.zeros((1, 1, 32, 384), BF)
+    acs[f, 0:8, 1, :, 128:384] = actb[:, 0]
+    acs[f, 1:9, 0, :, 128:384] = actb[:, 1]
+    acs[f, 0:8, 1, :, 0:128] = leftb[:, 0]
+    acs[f, 1:9, 0, :, 0:128] = leftb[:, 1]
+    return sig * (1.0 + hidden * (1.0 - sig))
+
+
+def tap_rows(acs, f, a):
+    rows = (acs[f, 0:8, 0], acs[f, 0:8, 1], acs[f, 1:9, 0])[a]
+    return rows.reshape(256, 384)
+
+
+def encode(pairs, wd_ref):
+    acc = None
+    for acs, f, k in pairs:
+        for a in range(3):
+            term = dot(tap_rows(acs, f, a), wd_ref[3 * k + a])
+            acc = term if acc is None else acc + term
+    return acc.reshape(8, 32, 256)
+
+
+def kernel_first(x_ref, m_ref, wconv_ref, wd_ref,
+                 wc_ref, wa_ref, xs_ref, acs_ref, slope_ref, dact_ref, mt_ref, part_ref,
+                 wide, ms):
+    both_weights(wc_ref, wa_ref, wconv_ref, wd_ref)
+    clear_edges(xs_ref, 4)
     for f in range(4):
-        spread(xs, f, *split_columns(wide.at[f % 2], x_ref[f]))
+        spread(xs_ref, f, *split_columns(wide.at[f % 2], x_ref[f]))
+    for t in range(2):
+        spread_out(ms, t, m_ref[t])
+        mt_ref[:, 256 * t : 256 * t + 256] = turned(m_ref[t].reshape(256, 256))
     for f in range(2):
-        late_ref[f] = conv_frame(xs, f, wc_ref)
-
-
-def call_weights(x, w_conv, w_down):
+        hidden = conv_frame([xs_ref.at[f + k] for k in range(3)], wc_ref)
+        slope_ref[f] = activate(hidden, acs_ref, f)
+    part_ref[0] = encode(((acs_ref, 0, 0), (acs_ref, 1, 1)), wd_ref).astype(BF)
+    even, odd = up_terms(ms, 0, 2, wa_ref)
+    even_b, odd_b = up_terms(ms, 1, 0, wa_ref)
+    dact_ref[0, :, 0] = even + even_b
+    dact_ref[0, :, 1] = odd + odd_b
+    for f, k in ((1, 1), (2, 2)):
+        even, odd = up_terms(ms, 1, k, wa_ref)
+        dact_ref[f, :, 0] = even
+        dact_ref[f, :, 1] = odd
+
+
+def call_first(x, m, w_conv, w_down):
     return pl.pallas_call(
-        kernel_weights,
-        out_shape=(jax.ShapeDtypeStruct((9, 512, 256), BF),) * 2
-        + (jax.ShapeDtypeStruct((2, 512, 256), F32),),
-        in_specs=[VMEM] * 3,
-        out_specs=(VMEM,) * 3,
+        kernel_first,
+        out_shape=(
+            jax.ShapeDtypeStruct((9, 512, 256), BF),
+            jax.ShapeDtypeStruct((9, 512, 256), BF),
+            jax.ShapeDtypeStruct((4, 18, 32, 512), BF),
+            jax.ShapeDtypeStruct((2, 9, 2, 32, 384), BF),
+            jax.ShapeDtypeStruct((2, 512, 256), F32),
+            jax.ShapeDtypeStruct((3, 8, 2, 32, 256), F32),
+            jax.ShapeDtypeStruct((256, 512), BF),
+            jax.ShapeDtypeStruct((1, 8, 32, 256), BF),
+        ),
+        in_specs=[VMEM] * 4,
+        out_specs=(VMEM,) * 8,
         scratch_shapes=[
             pltpu.VMEM((2, 16, 64, 128), F32),
-            pltpu.VMEM((4, 18, 32, 512), BF),
+            pltpu.VMEM((2, 9, 32, 512), BF),
         ],
-        compiler_params=params(16),
-        cost_estimate=cost(10**6, 8 * 10**6),
-    )(x, w_conv, w_down)
-
-
-TERMS = {0: ((0, 2), (1, 0)), 1: ((1, 1),), 2: ((1, 2), (2, 0)), 3: ((2, 1),)}
-
-
-def kernel_grads(core_ref, x_ref, before_ref, m_ref, next_ref, wc_ref, wa_ref, late_ref, wd_ref,
-                 hg_ref, own_ref, other_ref, enc_ref, part_ref,
-                 wide, xs, ms, mt, acs, hgt, dact, sums, sems):
+        compiler_params=params(12),
+        cost_estimate=cost(10**6, 10**6),
+    )(x, m, w_conv, w_down)
+
+
+def kernel_grads(core_ref, before_ref, next_ref, wc_ref, wa_ref, wd_ref, xs_ref, high_ref, slope_ref, dact_ref, mt_ref,
+                 hg_ref, own_ref, other_ref, even_ref, odd_ref,
+                 wide, ms, up, hgt, low, xb, mn, sums, sems):
     core = core_ref[0]
-    clear_edges(xs, 6)
-    for f in range(6):
-        frame = before_ref[f] if f < 2 else x_ref[f - 2]
-        spread(xs, f, *split_columns(wide.at[f % 2], frame))
-    ms[:, 8:9] = jnp.zeros((3, 1, 32, 512), BF)
-    for t in range(3):
-        m = next_ref[0] if t == 2 else m_ref[t]
-        ms[t, 0:8, :, 0:256] = m
-        ms[t, 0:8, :, 256:512] = from_right(m.astype(F32)).astype(BF)
-        mt[:, 256 * t : 256 * t + 256] = turned(m.reshape(256, 256))
-    acs[:, 0:1, 0:1] = jnp.zeros((4, 1, 1, 32, 384), BF)
-    acs[:, 8:9, 1:2] = jnp.zeros((4, 1, 1, 32, 384), BF)
     sums[0, HALF - 128 :] = jnp.zeros((128, 128), BF)
     sums[1, HALF - 256 :] = jnp.zeros((256, 128), BF)
-
-    for f in range(4):
-        even = odd = None
-        for t, k in TERMS[f]:
-            here = ms[t, 0:8].reshape(256, 512)
-            below = ms[t, 1:9].reshape(256, 512)
-            e = dot(here, wa_ref[3 * k + 1])
-            o = dot(here, wa_ref[3 * k + 2]) + dot(below, wa_ref[3 * k])
-            even = e if even is None else even + e
-            odd = o if odd is None else odd + o
-        dact[f, :, 0] = even.reshape(8, 32, 256)
-        dact[f, :, 1] = odd.reshape(8, 32, 256)
-
-    for f in range(4):
-        hidden = conv_frame(xs, f, wc_ref) if f < 2 else late_ref[f - 2]
-        sig = 1.0 / (1.0 + jnp.exp(-hidden))
-        act = (hidden * sig).reshape(8, 2, 32, 256)
-        left = from_left(act[..., 128:256].reshape(16, 32, 128)).reshape(8, 2, 32, 128)
-        actb = act.astype(BF)
-        leftb = left.astype(BF)
-        acs[f, 0:8, 1, :, 128:384] = actb[:, 0]
-        acs[f, 1:9, 0, :, 128:384] = actb[:, 1]
-        acs[f, 0:8, 1, :, 0:128] = leftb[:, 0]
-        acs[f, 1:9, 0, :, 0:128] = leftb[:, 1]
-        grad = dact[f].reshape(512, 256) * sig * (1.0 + hidden * (1.0 - sig))
+    clear_edges(xb, 2)
+    for f in range(2):
+        spread(xb, f, *split_columns(wide.at[f], before_ref[f]))
+    spread_out(ms, 0, next_ref[0])
+    mn[...] = turned(next_ref[0].reshape(256, 256))
+    for k in range(2):
+        even, odd = up_terms(ms, 0, k, wa_ref)
+        up[k, :, 0] = even
+        up[k, :, 1] = odd
+    every = [xb.at[f] for f in range(2)] + [xs_ref.at[f] for f in range(2)]
+    for f in (2, 3, 0, 1):
+        if f < 2:
+            slope = activate(conv_frame(every[f : f + 3], wc_ref), low, f)
+            grad = dact_ref[f].reshape(512, 256) * slope
+        elif f == 2:
+            grad = (dact_ref[2] + up[0]).reshape(512, 256) * slope_ref[0]
+        else:
+            grad = up[1].reshape(512, 256) * slope_ref[1]
         hg_ref[f] = grad.astype(BF).reshape(16, 32, 256)
         hgt[:, 512 * f : 512 * f + 512] = grad.T.astype(BF)
 
     def put(half, block, v):
         sums[half, 128 * block : 128 * block + 128] = v
 
-    def tap(f, a):
-        rows = (acs[f, 0:8, 0], acs[f, 0:8, 1], acs[f, 1:9, 0])[a]
-        return rows.reshape(256, 384)
-
     for k in range(3):
-        m_t = mt[:, 0:512] if k == 2 else mt[:, 256:768]
-        parity = 1 if k == 1 else 0
+        left = mt_ref[...] if k == 2 else jnp.concatenate([mt_ref[:, 256:512], mn[...]], axis=1)
+        f = 1 if k == 1 else 0
         for a in range(3):
-            right = jnp.concatenate([tap(parity, a), tap(parity + 2, a)], axis=0)
-            g = dot(m_t, right)
+            right = jnp.concatenate([tap_rows(low, f, a), tap_rows(high_ref, f, a)], axis=0)
+            g = dot(left, right)
             for b in range(3):
                 block = g[:, 128 * b : 128 * b + 128].T.astype(BF)
                 at = 9 * k + 3 * a + b
@@ -191,7 +235,10 @@
 
     for k in range(3):
         for a in range(3):
-            right = xs[k : k + 4, a : a + 16].reshape(2048, 512)
+            right = xs_ref[0 : k + 2, a : a + 16].reshape(512 * (k + 2), 512)
+            if k < 2:
+                first = xb[k:2, a : a + 16].reshape(512 * (2 - k), 512)
+                right = jnp.concatenate([first, right], axis=0)
             g = dot(hgt[...], right)
             for b in range(3):
                 u, v = (2, 0, 1)[b], (0, 1, 3)[b]
@@ -202,53 +249,45 @@
     keep = pltpu.make_async_copy(sums.at[core], own_ref, sems.at[1])
     send.start()
     keep.start()
-    for t in range(3):
-        acc = None
-        for k in range(3):
-            f = 2 * t + k - 2
-            if 0 <= f < 4:
-                for a in range(3):
-                    term = dot(tap(f, a), wd_ref[3 * k + a])
-                    acc = term if acc is None else acc + term
-        if t == 2:
-            part_ref[0] = acc.astype(BF).reshape(8, 32, 256)
-        else:
-            enc_ref[t] = acc.reshape(8, 32, 256)
+    even_ref[...] = encode(((low, 0, 2),), wd_ref)
+    pairs = ((low, 0, 0), (low, 1, 1), (high_ref, 0, 2))
+    odd_ref[...] = encode(pairs, wd_ref).astype(BF)
     send.wait()
     keep.wait()
 
 
-def call_grads(core, x, before, m, after, wc, wa, late, wd):
+def call_grads(core, before, after, wc, wa, wd, xs, high, slope, dact, mt):
     return pl.pallas_call(
         kernel_grads,
         out_shape=(
             jax.ShapeDtypeStruct((4, 16, 32, 256), BF),
             jax.ShapeDtypeStruct((HALF, 128), BF),
             jax.ShapeDtypeStruct((HALF, 128), BF),
-            jax.ShapeDtypeStruct((2, 8, 32, 256), F32),
-            jax.ShapeDtypeStruct((1, 8, 32, 256), BF),
+            jax.ShapeDtypeStruct((8, 32, 256), F32),
+            jax.ShapeDtypeStruct((8, 32, 256), BF),
         ),
-        in_specs=[SMEM] + [VMEM] * 8,
+        in_specs=[SMEM] + [VMEM] * 10,
         out_specs=(VMEM, ANY, ANY, VMEM, VMEM),
         scratch_shapes=[
             pltpu.VMEM((2, 16, 64, 128), F32),
-            pltpu.VMEM((6, 18, 32, 512), BF),
-            pltpu.VMEM((3, 9, 32, 512), BF),
-            pltpu.VMEM((256, 768), BF),
-            pltpu.VMEM((4, 9, 2, 32, 384), BF),
+            pltpu.VMEM((1, 9, 32, 512), BF),
+            pltpu.VMEM((2, 8, 2, 32, 256), F32),
             pltpu.VMEM((256, 2048), BF),
-            pltpu.VMEM((4, 8, 2, 32, 256), F32),
+            pltpu.VMEM((2, 9, 2, 32, 384), BF),
+            pltpu.VMEM((2, 18, 32, 512), BF),
+            pltpu.VMEM((256, 256), BF),
             pltpu.VMEM((2, HALF, 128), BF),
             pltpu.SemaphoreType.DMA((2,)),
         ],
-        compiler_params=params(40),
-        cost_estimate=cost(12 * 10**9, 10**7),
-    )(core, x, before, m, after, wc, wa, late, wd)
-
-
-def kernel_clip(h_ref, after_ref, w_ref, own_ref, part_ref, out_ref, enc_ref, hs, wt, wide):
-    enc_ref[0] = (own_ref[0] + part_ref[0].astype(F32)).astype(BF)
-    enc_ref[1] = own_ref[1].astype(BF)
+        compiler_params=params(24),
+        cost_estimate=cost(10**6, 10**6),
+    )(core, before, after, wc, wa, wd, xs, high, slope, dact, mt)
+
+
+def kernel_clip(h_ref, after_ref, w_ref, even_ref, odd_ref, part_ref,
+                out_ref, enc_ref, hs, wt, wide):
+    enc_ref[0] = (even_ref[...] + part_ref[0].astype(F32)).astype(BF)
+    enc_ref[1] = odd_ref[...]
     clear_edges(hs, 6)
     for tap in range(9):
         pair_weights(wt, tap, [turned(w_ref[3 * (8 - tap) + 2 - b]) for b in range(3)])
@@ -256,20 +295,20 @@
         v = (h_ref[f] if f < 4 else after_ref[f - 4]).astype(F32)
         spread(hs, f, v[:, :, 0:128], v[:, :, 128:256])
     for f in range(4):
-        v = conv_frame(hs, f, wt).reshape(16, 32, 256)
+        v = conv_frame([hs.at[f + k] for k in range(3)], wt).reshape(16, 32, 256)
         wide[f % 2, :, pl.ds(0, 32, stride=2), :] = v[:, :, 0:128]
         wide[f % 2, :, pl.ds(1, 32, stride=2), :] = v[:, :, 128:256]
         out_ref[f] = wide[f % 2].astype(BF)
 
 
-def call_clip(h, after, w, enc, part):
+def call_clip(h, after, w, even, odd, part):
     return pl.pallas_call(
         kernel_clip,
         out_shape=(
             jax.ShapeDtypeStruct((4, 16, 64, 128), BF),
             jax.ShapeDtypeStruct((2, 8, 32, 256), BF),
         ),
-        in_specs=[VMEM] * 5,
+        in_specs=[VMEM] * 6,
         out_specs=(VMEM, VMEM),
         scratch_shapes=[
             pltpu.VMEM((6, 18, 32, 512), BF),
@@ -278,7 +317,7 @@
         ],
         compiler_params=params(32),
         cost_estimate=cost(5 * 10**9, 5 * 10**6),
-    )(h, after, w, enc, part)
+    )(h, after, w, even, odd, part)
 
 
 def write_half(half, scale, src, conv_ref, down_ref, conv, down, sems):
@@ -388,9 +427,9 @@
     masked_after = shifted(masked[:1], -1)
     taps_conv = w_conv.reshape(27, 128, 128)
     taps_down = w_down.reshape(9, 384, 256)
-    wc, wa, late = call_weights(clips[0], taps_conv, taps_down)
-    hg, own, other, enc, part = call_grads(
-        core, clips[0], before, masked, masked_after, wc, wa, late, taps_down
+    wc, wa, xs, high, slope, dact, mt, part = call_first(clips[0], masked, taps_conv, taps_down)
+    hg, own, other, even, odd = call_grads(
+        core, before, masked_after, wc, wa, taps_down, xs, high, slope, dact, mt
     )
     own = (own.astype(F32) + swapped(other).astype(F32)).astype(BF)
     own, part = lax.optimization_barrier((own, part))
@@ -403,7 +442,7 @@
     own = call_fold(exchange(own, "zh"), 32)
     own, after = lax.optimization_barrier((own, after))
     own = exchange(own, NEAR).reshape(HALF, 128)
-    clip_grad, encoded = call_clip(hg, after, taps_conv, enc, part)
+    clip_grad, encoded = call_clip(hg, after, taps_conv, even, odd, part)
     own, clip_grad, encoded = lax.optimization_barrier((own, clip_grad, encoded))
     scale = 1.0 / math.sqrt(lax.axis_size(DP) * frames * lax.axis_size(TM) * rows * cols)
     begun = call_out(kernel_own, core, own, scale)

time: 126 us -> 124 us (0.984)
  waiting for transfers between devices: 36.9 us -> 31.2 us
  starting transfers between devices: 35.2 us -> 37.5 us
    all_to_all x2, waiting for transfers between devices: 14.5 us -> 10.2 us  [exchange(): return lax.all_to_all(value, axes, 0, 0, tiled=True)]
    pallas_call x1, Pallas kernels: 3.01 us -> 4.57 us  [call_first(): pl.pallas_call(kernel_first, out_shape=(jax.ShapeDtypeStruct((9, 512, 256...]
    ppermute x4, waiting for transfers between devices: 18.5 us -> 17.1 us  [shifted(): return lax.ppermute(block, TM, route)]
    ppermute x2, starting transfers between devices: 5.49 us -> 6.87 us  [swapped(): return lax.ppermute(block, 'c', [(0, 1), (1, 0)])]
    unnamed x18 -> x28, local copies, waits for them, and re-layouts: 5.53 us -> 6.11 us
  transfers between devices with their start and end apart: 8 -> 8, of which waited for: 6 -> 6; matrix products, arithmetic and copies ran while one was open for 2% -> 2% of each run, Pallas kernels for 10% -> 11%
where the time goes in v4:
time: 124 us; the launch traced here: 123 us
  starting transfers between devices  37.5 us (30%)
  waiting for transfers between devices  31.2 us (25%)
  Pallas kernels  27.2 us (22%)
  blocking collectives  15 us (12%)
  local copies, waits for them, and re-layouts  8.15 us (7%)
  other arithmetic  2.48 us (2%)
  between operations  1.65 us (1%)
    all_to_all x2, starting transfers between devices, exchange(): return lax.all_to_all(value, axes, 0, 0, tiled=True)  17.9 us
    ppermute x4, waiting for transfers between devices, shifted(): return lax.ppermute(block, TM, route)  17.1 us
    all_to_all x1, blocking collectives, exchange(): return lax.all_to_all(value, axes, 0, 0, tiled=True)  15 us
    ppermute x4, starting transfers between devices, shifted(): return lax.ppermute(block, TM, route)  12.7 us
    pallas_call x1, Pallas kernels, call_grads(): pl.pallas_call(kernel_grads, out_shape=(jax.ShapeDtypeStruct((4, 16, 32,...  11.8 us
    all_to_all x2, waiting for transfers between devices, exchange(): return lax.all_to_all(value, axes, 0, 0, tiled=True)  10.2 us
    ppermute x2, starting transfers between devices, swapped(): return lax.ppermute(block, 'c', [(0, 1), (1, 0)])  6.87 us
    pallas_call x1, Pallas kernels, call_clip(): pl.pallas_call(kernel_clip, out_shape=(jax.ShapeDtypeStruct((4, 16, 64, 1...  6.29 us
  transfers between devices with their start and end apart: 8, of which 6 were waited for; matrix products, arithmetic and copies ran while one was open for 2% of the time, Pallas kernels for 11%

profile of v4, /device:TPU:1, one launch (start us, length us, event | category | flops | bytes accessed | tf_op | source)
XLA Modules:
  0.0 123.3 jit_solution(8653090095011110450)
XLA Ops:
  0.6 1.2 slice_bitcast_fusion
  1.9 5.5 %collective-permute-start = (bf16[2,16,64,128]{3,2,1,0:T(8,128)(2,1)S(1)}, bf16[2,16,64,128]{3,2,1,0:T(8,128)(2,1)S(1)}, u32[]{:S(2)}, u32[]{:S(2)}) collective-permute-start(bf16[2,16,64,128]{3,2,1,0:T(8,128)(2,1)S(1)} %slice_bitcast_fusion), channel_id=1, source_target_pairs={{0,1},{1,2},{2,3},{3,4},{4,5},{5,6},{6,7},{8,9},{9,10},{10,11},{11... | collective-permute-start | bytes 1572872 | tf_op jit(solution)/shard_map/ppermute | solution.py:407
  9.1 1.3 %collective-permute-start.1 = (bf16[1,8,32,256]{3,2,1,0:T(8,128)(2,1)S(1)}, bf16[1,8,32,256]{3,2,1,0:T(8,128)(2,1)S(1)}, u32[]{:S(2)}, u32[]{:S(2)}) collective-permute-start(bf16[1,8,32,256]{3,2,1,0:T(8,128)(2,1)S(1)} %slice.12), channel_id=1, source_target_pairs={{1,0},{2,1},{3,2},{4,3},{5,4},{6,5},{7,6},{9,8},{10,9},{11,10},{12... | collective-permute-start | bytes 393224 | tf_op jit(solution)/shard_map/ppermute | solution.py:407
  10.4 1.2 copy-done.1
  12.8 4.6 %shard_map.84 = (bf16[9,512,256]{2,1,0:T(8,128)(2,1)S(1)}, bf16[9,512,256]{2,1,0:T(8,128)(2,1)S(1)}, bf16[4,18,32,512]{3,2,1,0:T(8,128)(2,1)S(1)}, bf16[2,9,2,32...) custom-call(bf16[4,16,64,128]{3,2,1,0:T(8,128)(2,1)S(1)} %bitcast.20, ...), custom_call_target="tpu_custom_call" | custom-call | flops 1000000 | bytes 1000000 | tf_op jit(solution)/shard_map/pallas_call | solution.py:170
  17.4 5.3 %collective-permute-done.1.next_ref = bf16[1,8,32,256]{3,2,1,0:T(8,128)(2,1)S(1)} collective-permute-done((bf16[1,8,32,256]{3,2,1,0:T(8,128)(2,1)S(1)}, bf16[1,8,32,256]{3,2,1,0:T(8,128)(2,1)S(1)}, u32[]{:S(2)}, u32[]{:S(2)}) %collective-permute-start.1) | collective-permute-done | bytes 131104 | tf_op jit(solution)/shard_map/ppermute | solution.py:407
  22.7 11.8 %shard_map.85 = (bf16[4,16,32,256]{3,2,1,0:T(8,128)(2,1)S(1)}, bf16[5376,128]{1,0:T(8,128)(2,1)S(1)}, bf16[5376,128]{1,0:T(8,128)(2,1)S(1)}, f32[8,32,256]{2,1,0:T(8,128)S(1)}, bf16[8,32,256]{2,1,0:T(8,128)(2,1)S(1)}) custom-call(s32[1]{0:T(128)} %bitcast.core_ref, bf16[2,16,64,128]{3,2,1,0:T(8,128)(2,1)S(1)} %collective-permute-done.before_ref, ...), custom_call_target="tpu_custom_call" | custom-call | flops 1000000 | bytes 1000000 | tf_op jit(solution)/shard_map/pallas_call | solution.py:260
  34.5 1.6 %collective-permute-start.2 = (bf16[5376,128]{1,0:T(8,128)(2,1)S(1)}, bf16[5376,128]{1,0:T(8,128)(2,1)S(1)}, u32[]{:S(2)}, u32[]{:S(2)}) collective-permute-start(bf16[5376,128]{1,0:T(8,128)(2,1)S(1)} %get-tuple-element.44), channel_id=1, source_target_pairs={{0,8},{8,0},{1,9},{9,1},{2,10},{10,2},{3,11},{11,3},{4,12},{12,4},... | collective-permute-start | bytes 4128776 | tf_op jit(solution)/shard_map/ppermute | solution.py:411
  36.2 2.8 %collective-permute-done.2 = bf16[5376,128]{1,0:T(8,128)(2,1)S(1)} collective-permute-done((bf16[5376,128]{1,0:T(8,128)(2,1)S(1)}, bf16[5376,128]{1,0:T(8,128)(2,1)S(1)}, u32[]{:S(2)}, u32[]{:S(2)}) %collective-permute-start.2) | collective-permute-done | bytes 1376288 | tf_op jit(solution)/shard_map/ppermute | solution.py:411
  38.9 1.4 %add_convert_fusion = bf16[5376,128]{1,0:T(8,128)(2,1)} fusion(bf16[5376,128]{1,0:T(8,128)(2,1)S(1)} %collective-permute-done.2, bf16[5376,128]{1,0:T(8,128)(2,1)S(1)} %get-tuple-element.43), kind=kLoop, calls=%fused_computation | loop fusion | flops 2752512 | bytes 4128768 | tf_op jit(solution)/shard_map/convert_element_type | solution.py:434
  40.4 8.2 %all-to-all-start = ((bf16[32,168,128]{2,1,0:T(8,128)(2,1)}), bf16[32,168,128]{2,1,0:T(8,128)(2,1)S(1)}, u32[]{:S(2)}, u32[]{:S(2)}) async-start(bf16[32,168,128]{2,1,0:T(8,128)(2,1)} %bitcast.23), calls=%async_computation | async-start | bytes 2752512 | tf_op jit(solution)/shard_map/all_to_all | solution.py:415
  48.6 4.6 %collective-permute-start.3 = (bf16[1,8,32,256]{3,2,1,0:T(8,128)(2,1)S(1)}, bf16[1,8,32,256]{3,2,1,0:T(8,128)(2,1)S(1)}, u32[]{:S(2)}, u32[]{:S(2)}) collective-permute-start(bf16[1,8,32,256]{3,2,1,0:T(8,128)(2,1)S(1)} %copy-done.11), channel_id=1, source_target_pairs={{0,1},{1,2},{2,3},{3,4},{4,5},{5,6},{6,7},{8,9},{9,10},{10,11},{11... | collective-permute-start | bytes 393224 | tf_op jit(solution)/shard_map/ppermute | solution.py:407
  54.1 11.8 %collective-permute-done.3.part_ref = bf16[1,8,32,256]{3,2,1,0:T(8,128)(2,1)S(1)} collective-permute-done((bf16[1,8,32,256]{3,2,1,0:T(8,128)(2,1)S(1)}, bf16[1,8,32,256]{3,2,1,0:T(8,128)(2,1)S(1)}, u32[]{:S(2)}, u32[]{:S(2)}) %collective-permute-start.3) | collective-permute-done | bytes 131104 | tf_op jit(solution)/shard_map/ppermute | solution.py:407
  65.9 2.7 %all-to-all-done.in_ref = bf16[32,168,128]{2,1,0:T(8,128)(2,1)S(1)} async-done(((bf16[32,168,128]{2,1,0:T(8,128)(2,1)}), bf16[32,168,128]{2,1,0:T(8,128)(2,1)S(1)}, u32[]{:S(2)}, u32[]{:S(2)}) %all-to-all-start) | async-done | bytes 1376288 | tf_op jit(solution)/shard_map/all_to_all | solution.py:415
  68.8 1.3 %collective-permute-start.4 = (bf16[2,16,32,256]{3,2,1,0:T(8,128)(2,1)}, bf16[2,16,32,256]{3,2,1,0:T(8,128)(2,1)S(1)}, u32[]{:S(2)}, u32[]{:S(2)}) collective-permute-start(bf16[2,16,32,256]{3,2,1,0:T(8,128)(2,1)} %slice.11), channel_id=1, source_target_pairs={{1,0},{2,1},{3,2},{4,3},{5,4},{6,5},{7,6},{9,8},{10,9},{11,10},{12... | collective-permute-start | bytes 1572872 | tf_op jit(solution)/shard_map/ppermute | solution.py:407
  70.1 15.0 %all_to_all.15.in_ref = bf16[4,168,128]{2,1,0:T(8,128)(2,1)S(1)} all-to-all(bf16[4,168,128]{2,1,0:T(8,128)(2,1)S(1)} %shard_map.86), channel_id=1, replica_groups=mesh['xl'=2,'zh'=4,'zl'=2,'c'=2,'y'=4,'xh'=2] {'zh'}, dimensions={0} | all-to-all | bytes 344064 | tf_op jit(solution)/shard_map/all_to_all | solution.py:415
  85.1 1.2 shard_map.87
  87.1 9.7 %all-to-all-start.2 = ((bf16[32,168,128]{2,1,0:T(8,128)(2,1)}), bf16[32,168,128]{2,1,0:T(8,128)(2,1)S(1)}, u32[]{:S(2)}, u32[]{:S(2)}) async-start(bf16[32,168,128]{2,1,0:T(8,128)(2,1)} %shard_map.87), calls=%async_computation.2 | async-start | bytes 2752512 | tf_op jit(solution)/shard_map/all_to_all | solution.py:415
  99.7 6.3 %shard_map.88 = (bf16[4,16,64,128]{3,2,1,0:T(8,128)(2,1)}, bf16[2,8,32,256]{3,2,1,0:T(8,128)(2,1)}) custom-call(bf16[4,16,32,256]{3,2,1,0:T(8,128)(2,1)S(1)} %copy-done.5, bf16[2,16,32,256]{3,2,1,0:T(8,128)(2,1)S(1)} %copy-done.7, bf16[27,128,128]{2,1,0:T(8,128)(2,1)S(1)} %bitcast.22, f32[8,32,256]{2,1,0:T(8,128)S(1)} %copy-done.9, ...), custom_call_target="tpu_custom_call" | custom-call | flops 5000000000 | bytes 5000000 | tf_op jit(solution)/shard_map/pallas_call | solution.py:305
  106.0 7.5 %all-to-all-done.2 = bf16[32,168,128]{2,1,0:T(8,128)(2,1)S(1)} async-done(((bf16[32,168,128]{2,1,0:T(8,128)(2,1)}), bf16[32,168,128]{2,1,0:T(8,128)(2,1)S(1)}, u32[]{:S(2)}, u32[]{:S(2)}) %all-to-all-start.2) | async-done | bytes 1376288 | tf_op jit(solution)/shard_map/all_to_all | solution.py:415
  113.5 5.2 %collective-permute-start.5 = (bf16[5376,128]{1,0:T(8,128)(2,1)S(1)}, bf16[5376,128]{1,0:T(8,128)(2,1)S(1)}, u32[]{:S(2)}, u32[]{:S(2)}) collective-permute-start(bf16[5376,128]{1,0:T(8,128)(2,1)S(1)} %bitcast.18), channel_id=1, source_target_pairs={{0,8},{8,0},{1,9},{9,1},{2,10},{10,2},{3,11},{11,3},{4,12},{12,4},... | collective-permute-start | bytes 4128776 | tf_op jit(solution)/shard_map/ppermute | solution.py:411
  118.8 1.6 %shard_map.89 = (f32[27,128,128]{2,1,0:T(8,128)}, f32[27,128,256]{2,1,0:T(8,128)}) custom-call(s32[1]{0:T(128)} %bitcast.core_ref, bf16[5376,128]{1,0:T(8,128)(2,1)S(1)} %bitcast.19), custom_call_target="tpu_custom_call" | custom-call | flops 1000000 | bytes 4000000 | tf_op jit(solution)/shard_map/pallas_call | solution.py:365
  120.3 1.2 collective-permute-done.5.src
  121.5 1.6 %shard_map.90 = (f32[27,128,128]{2,1,0:T(8,128)}, f32[27,128,256]{2,1,0:T(8,128)}) custom-call(s32[1]{0:T(128)} %bitcast.core_ref, bf16[5376,128]{1,0:T(8,128)(2,1)S(1)} %collective-permute-done.5.src, f32[27,128,128]{2,1,0:T(8,128)} %get-tuple-element.62.conv_in, ...), custom_call_target="tpu_custom_call", output_to_operand_aliasing={{0}: (2, {}), {1}: (3, {})} | custom-call | flops 1000000 | bytes 4000000 | tf_op jit(solution)/shard_map/pallas_call | solution.py:365
  (34 shorter events, 7.0 us)
Async XLA Ops:
  0.6 9.8 %copy-start = (bf16[3,3,3,128,256]{4,3,2,1,0:T(8,128)(2,1)S(1)}, bf16[3,3,3,128,256]{4,3,2,1,0:T(8,128)(2,1)}, u32[]{:S(2)}) copy-start(bf16[3,3,3,128,256]{4,3,2,1,0:T(8,128)(2,1)} %param.9) | copy-start | bytes 5308420
  1.9 20.8 %collective-permute-start = (bf16[2,16,64,128]{3,2,1,0:T(8,128)(2,1)S(1)}, bf16[2,16,64,128]{3,2,1,0:T(8,128)(2,1)S(1)}, u32[]{:S(2)}, u32[]{:S(2)}) collective-permute-start(bf16[2,16,64,128]{3,2,1,0:T(8,128)(2,1)S(1)} %slice_bitcast_fusion), channel_id=1, source_target_pairs={{0,1},{1,2},{2,3},{3,4},{4,5},{5,6},{6,7},{8,9},{9,10},{10,11},{11... | collective-permute-start | bytes 1572872 | tf_op jit(solution)/shard_map/ppermute | solution.py:407
  9.1 13.6 %collective-permute-start.1 = (bf16[1,8,32,256]{3,2,1,0:T(8,128)(2,1)S(1)}, bf16[1,8,32,256]{3,2,1,0:T(8,128)(2,1)S(1)}, u32[]{:S(2)}, u32[]{:S(2)}) collective-permute-start(bf16[1,8,32,256]{3,2,1,0:T(8,128)(2,1)S(1)} %slice.12), channel_id=1, source_target_pairs={{1,0},{2,1},{3,2},{4,3},{5,4},{6,5},{7,6},{9,8},{10,9},{11,10},{12... | collective-permute-start | bytes 393224 | tf_op jit(solution)/shard_map/ppermute | solution.py:407
  10.4 1.2 copy-start.1
  11.6 1.2 copy-start.2
  17.4 17.1 %copy-start.10 = (bf16[1,8,32,256]{3,2,1,0:T(8,128)(2,1)}, bf16[1,8,32,256]{3,2,1,0:T(8,128)(2,1)S(1)}, u32[]{:S(2)}) copy-start(bf16[1,8,32,256]{3,2,1,0:T(8,128)(2,1)S(1)} %get-tuple-element.47) | copy-start | bytes 393220
  34.5 5.9 %copy-start.4 = (bf16[4,16,32,256]{3,2,1,0:T(8,128)(2,1)}, bf16[4,16,32,256]{3,2,1,0:T(8,128)(2,1)S(1)}, u32[]{:S(2)}) copy-start(bf16[4,16,32,256]{3,2,1,0:T(8,128)(2,1)S(1)} %get-tuple-element.49.h_ref) | copy-start | bytes 3145732
  34.5 5.8 %copy-start.8 = (f32[8,32,256]{2,1,0:T(8,128)}, f32[8,32,256]{2,1,0:T(8,128)S(1)}, u32[]{:S(2)}) copy-start(f32[8,32,256]{2,1,0:T(8,128)S(1)} %get-tuple-element.54.even_ref) | copy-start | bytes 786436
  34.5 4.4 %collective-permute-start.2 = (bf16[5376,128]{1,0:T(8,128)(2,1)S(1)}, bf16[5376,128]{1,0:T(8,128)(2,1)S(1)}, u32[]{:S(2)}, u32[]{:S(2)}) collective-permute-start(bf16[5376,128]{1,0:T(8,128)(2,1)S(1)} %get-tuple-element.44), channel_id=1, source_target_pairs={{0,8},{8,0},{1,9},{9,1},{2,10},{10,2},{3,11},{11,3},{4,12},{12,4},... | collective-permute-start | bytes 4128776 | tf_op jit(solution)/shard_map/ppermute | solution.py:411
  40.4 8.3 %copy-start.11 = (bf16[1,8,32,256]{3,2,1,0:T(8,128)(2,1)S(1)}, bf16[1,8,32,256]{3,2,1,0:T(8,128)(2,1)}, u32[]{:S(2)}) copy-start(bf16[1,8,32,256]{3,2,1,0:T(8,128)(2,1)} %copy-done.10) | copy-start | bytes 393220
  40.4 12.9 %copy-start.5 = (bf16[4,16,32,256]{3,2,1,0:T(8,128)(2,1)S(1)}, bf16[4,16,32,256]{3,2,1,0:T(8,128)(2,1)}, u32[]{:S(2)}) copy-start(bf16[4,16,32,256]{3,2,1,0:T(8,128)(2,1)} %copy-done.4) | copy-start | bytes 3145732
  40.4 28.2 %all-to-all-start = ((bf16[32,168,128]{2,1,0:T(8,128)(2,1)}), bf16[32,168,128]{2,1,0:T(8,128)(2,1)S(1)}, u32[]{:S(2)}, u32[]{:S(2)}) async-start(bf16[32,168,128]{2,1,0:T(8,128)(2,1)} %bitcast.23), calls=%async_computation | async-start | bytes 2752512 | tf_op jit(solution)/shard_map/all_to_all | solution.py:415
  48.6 17.3 %collective-permute-start.3 = (bf16[1,8,32,256]{3,2,1,0:T(8,128)(2,1)S(1)}, bf16[1,8,32,256]{3,2,1,0:T(8,128)(2,1)S(1)}, u32[]{:S(2)}, u32[]{:S(2)}) collective-permute-start(bf16[1,8,32,256]{3,2,1,0:T(8,128)(2,1)S(1)} %copy-done.11), channel_id=1, source_target_pairs={{0,1},{1,2},{2,3},{3,4},{4,5},{5,6},{6,7},{8,9},{9,10},{10,11},{11... | collective-permute-start | bytes 393224 | tf_op jit(solution)/shard_map/ppermute | solution.py:407
  65.9 19.2 %copy-start.12 = (bf16[1,8,32,256]{3,2,1,0:T(8,128)(2,1)}, bf16[1,8,32,256]{3,2,1,0:T(8,128)(2,1)S(1)}, u32[]{:S(2)}) copy-start(bf16[1,8,32,256]{3,2,1,0:T(8,128)(2,1)S(1)} %collective-permute-done.3.part_ref) | copy-start | bytes 393220
  68.8 17.5 %collective-permute-start.4 = (bf16[2,16,32,256]{3,2,1,0:T(8,128)(2,1)}, bf16[2,16,32,256]{3,2,1,0:T(8,128)(2,1)S(1)}, u32[]{:S(2)}, u32[]{:S(2)}) collective-permute-start(bf16[2,16,32,256]{3,2,1,0:T(8,128)(2,1)} %slice.11), channel_id=1, source_target_pairs={{1,0},{2,1},{3,2},{4,3},{5,4},{6,5},{7,6},{9,8},{10,9},{11,10},{12... | collective-permute-start | bytes 1572872 | tf_op jit(solution)/shard_map/ppermute | solution.py:407
  86.3 10.5 %copy-start.3 = (bf16[3,3,3,128,128]{4,3,2,1,0:T(8,128)(2,1)S(1)}, bf16[3,3,3,128,128]{4,3,2,1,0:T(8,128)(2,1)}, u32[]{:S(2)}) copy-start(bf16[3,3,3,128,128]{4,3,2,1,0:T(8,128)(2,1)} %param.8) | copy-start | bytes 2654212
  86.3 0.8 copy-start.6
  87.1 26.4 %all-to-all-start.2 = ((bf16[32,168,128]{2,1,0:T(8,128)(2,1)}), bf16[32,168,128]{2,1,0:T(8,128)(2,1)S(1)}, u32[]{:S(2)}, u32[]{:S(2)}) async-start(bf16[32,168,128]{2,1,0:T(8,128)(2,1)} %shard_map.87), calls=%async_computation.2 | async-start | bytes 2752512 | tf_op jit(solution)/shard_map/all_to_all | solution.py:415
  96.8 1.0 copy-start.7
  97.9 0.9 copy-start.9
  98.8 0.9 copy-start.13
  113.5 8.0 %collective-permute-start.5 = (bf16[5376,128]{1,0:T(8,128)(2,1)S(1)}, bf16[5376,128]{1,0:T(8,128)(2,1)S(1)}, u32[]{:S(2)}, u32[]{:S(2)}) collective-permute-start(bf16[5376,128]{1,0:T(8,128)(2,1)S(1)} %bitcast.18), channel_id=1, source_target_pairs={{0,8},{8,0},{1,9},{9,1},{2,10},{10,2},{3,11},{11,3},{4,12},{12,4},... | collective-permute-start | bytes 4128776 | tf_op jit(solution)/shard_map/ppermute | solution.py:411

commit v5 on v4

--- a/solution.py
+++ b/solution.py
@@ -19,7 +19,7 @@
 SMEM = pl.BlockSpec(memory_space=pltpu.SMEM)
 ANY = pl.BlockSpec(memory_space=pl.ANY)
 HBM = pl.BlockSpec(memory_space=pltpu.HBM)
-HALF = 42 * 128
+HALF = 44 * 128
 EARLY = 7
 
 
@@ -194,8 +194,8 @@
                  hg_ref, own_ref, other_ref, even_ref, odd_ref,
                  wide, ms, up, hgt, low, xb, mn, sums, sems):
     core = core_ref[0]
-    sums[0, HALF - 128 :] = jnp.zeros((128, 128), BF)
-    sums[1, HALF - 256 :] = jnp.zeros((256, 128), BF)
+    sums[0, 41 * 128 :] = jnp.zeros((HALF - 41 * 128, 128), BF)
+    sums[1, 40 * 128 :] = jnp.zeros((HALF - 40 * 128, 128), BF)
     clear_edges(xb, 2)
     for f in range(2):
         spread(xb, f, *split_columns(wide.at[f], before_ref[f]))

time: 124 us -> 126 us (1.016)
  waiting for transfers between devices: 31.2 us -> 32.9 us
where the time goes in v5:
time: 126 us; the launch traced here: 125 us
  starting transfers between devices  37.8 us (30%)
  waiting for transfers between devices  32.9 us (26%)
  Pallas kernels  27.4 us (22%)
  blocking collectives  14.9 us (12%)
  local copies, waits for them, and re-layouts  8.15 us (6%)
  other arithmetic  2.52 us (2%)
  between operations  1.65 us (1%)
    all_to_all x2, starting transfers between devices, exchange(): return lax.all_to_all(value, axes, 0, 0, tiled=True)  18.1 us
    ppermute x4, waiting for transfers between devices, shifted(): return lax.ppermute(block, TM, route)  17.7 us
    all_to_all x1, blocking collectives, exchange(): return lax.all_to_all(value, axes, 0, 0, tiled=True)  14.9 us
    ppermute x4, starting transfers between devices, shifted(): return lax.ppermute(block, TM, route)  12.7 us
    pallas_call x1, Pallas kernels, call_grads(): pl.pallas_call(kernel_grads, out_shape=(jax.ShapeDtypeStruct((4, 16, 32,...  12 us
    all_to_all x2, waiting for transfers between devices, exchange(): return lax.all_to_all(value, axes, 0, 0, tiled=True)  11 us
    ppermute x2, starting transfers between devices, swapped(): return lax.ppermute(block, 'c', [(0, 1), (1, 0)])  6.93 us
    pallas_call x1, Pallas kernels, call_clip(): pl.pallas_call(kernel_clip, out_shape=(jax.ShapeDtypeStruct((4, 16, 64, 1...  6.29 us
  transfers between devices with their start and end apart: 8, of which 6 were waited for; matrix products, arithmetic and copies ran while one was open for 2% of the time, Pallas kernels for 11%

profile of v5, /device:TPU:1, one launch (start us, length us, event | category | flops | bytes accessed | tf_op | source)
XLA Modules:
  0.0 125.3 jit_solution(539371653967102766)
XLA Ops:
  0.6 1.2 slice_bitcast_fusion
  1.9 5.5 %collective-permute-start = (bf16[2,16,64,128]{3,2,1,0:T(8,128)(2,1)S(1)}, bf16[2,16,64,128]{3,2,1,0:T(8,128)(2,1)S(1)}, u32[]{:S(2)}, u32[]{:S(2)}) collective-permute-start(bf16[2,16,64,128]{3,2,1,0:T(8,128)(2,1)S(1)} %slice_bitcast_fusion), channel_id=1, source_target_pairs={{0,1},{1,2},{2,3},{3,4},{4,5},{5,6},{6,7},{8,9},{9,10},{10,11},{11... | collective-permute-start | bytes 1572872 | tf_op jit(solution)/shard_map/ppermute | solution.py:407
  9.1 1.3 %collective-permute-start.1 = (bf16[1,8,32,256]{3,2,1,0:T(8,128)(2,1)S(1)}, bf16[1,8,32,256]{3,2,1,0:T(8,128)(2,1)S(1)}, u32[]{:S(2)}, u32[]{:S(2)}) collective-permute-start(bf16[1,8,32,256]{3,2,1,0:T(8,128)(2,1)S(1)} %slice.12), channel_id=1, source_target_pairs={{1,0},{2,1},{3,2},{4,3},{5,4},{6,5},{7,6},{9,8},{10,9},{11,10},{12... | collective-permute-start | bytes 393224 | tf_op jit(solution)/shard_map/ppermute | solution.py:407
  10.4 1.2 copy-done.1
  12.8 4.6 %shard_map.84 = (bf16[9,512,256]{2,1,0:T(8,128)(2,1)S(1)}, bf16[9,512,256]{2,1,0:T(8,128)(2,1)S(1)}, bf16[4,18,32,512]{3,2,1,0:T(8,128)(2,1)S(1)}, bf16[2,9,2,32...) custom-call(bf16[4,16,64,128]{3,2,1,0:T(8,128)(2,1)S(1)} %bitcast.20, ...), custom_call_target="tpu_custom_call" | custom-call | flops 1000000 | bytes 1000000 | tf_op jit(solution)/shard_map/pallas_call | solution.py:170
  17.4 5.3 %collective-permute-done.1.next_ref = bf16[1,8,32,256]{3,2,1,0:T(8,128)(2,1)S(1)} collective-permute-done((bf16[1,8,32,256]{3,2,1,0:T(8,128)(2,1)S(1)}, bf16[1,8,32,256]{3,2,1,0:T(8,128)(2,1)S(1)}, u32[]{:S(2)}, u32[]{:S(2)}) %collective-permute-start.1) | collective-permute-done | bytes 131104 | tf_op jit(solution)/shard_map/ppermute | solution.py:407
  22.7 12.0 %shard_map.85 = (bf16[4,16,32,256]{3,2,1,0:T(8,128)(2,1)S(1)}, bf16[5632,128]{1,0:T(8,128)(2,1)S(1)}, bf16[5632,128]{1,0:T(8,128)(2,1)S(1)}, f32[8,32,256]{2,1,0:T(8,128)S(1)}, bf16[8,32,256]{2,1,0:T(8,128)(2,1)S(1)}) custom-call(s32[1]{0:T(128)} %bitcast.core_ref, bf16[2,16,64,128]{3,2,1,0:T(8,128)(2,1)S(1)} %collective-permute-done.before_ref, ...), custom_call_target="tpu_custom_call" | custom-call | flops 1000000 | bytes 1000000 | tf_op jit(solution)/shard_map/pallas_call | solution.py:260
  34.7 1.6 %collective-permute-start.2 = (bf16[5632,128]{1,0:T(8,128)(2,1)S(1)}, bf16[5632,128]{1,0:T(8,128)(2,1)S(1)}, u32[]{:S(2)}, u32[]{:S(2)}) collective-permute-start(bf16[5632,128]{1,0:T(8,128)(2,1)S(1)} %get-tuple-element.44), channel_id=1, source_target_pairs={{0,8},{8,0},{1,9},{9,1},{2,10},{10,2},{3,11},{11,3},{4,12},{12,4},... | collective-permute-start | bytes 4325384 | tf_op jit(solution)/shard_map/ppermute | solution.py:411
  36.3 2.8 %collective-permute-done.2 = bf16[5632,128]{1,0:T(8,128)(2,1)S(1)} collective-permute-done((bf16[5632,128]{1,0:T(8,128)(2,1)S(1)}, bf16[5632,128]{1,0:T(8,128)(2,1)S(1)}, u32[]{:S(2)}, u32[]{:S(2)}) %collective-permute-start.2) | collective-permute-done | bytes 1441824 | tf_op jit(solution)/shard_map/ppermute | solution.py:411
  39.2 1.5 %add_convert_fusion = bf16[5632,128]{1,0:T(8,128)(2,1)} fusion(bf16[5632,128]{1,0:T(8,128)(2,1)S(1)} %collective-permute-done.2, bf16[5632,128]{1,0:T(8,128)(2,1)S(1)} %get-tuple-element.43), kind=kLoop, calls=%fused_computation | loop fusion | flops 2883584 | bytes 4325376 | tf_op jit(solution)/shard_map/convert_element_type | solution.py:434
  40.7 8.2 %all-to-all-start = ((bf16[32,176,128]{2,1,0:T(8,128)(2,1)}), bf16[32,176,128]{2,1,0:T(8,128)(2,1)S(1)}, u32[]{:S(2)}, u32[]{:S(2)}) async-start(bf16[32,176,128]{2,1,0:T(8,128)(2,1)} %bitcast.23), calls=%async_computation | async-start | bytes 2883584 | tf_op jit(solution)/shard_map/all_to_all | solution.py:415
  48.9 4.6 %collective-permute-start.3 = (bf16[1,8,32,256]{3,2,1,0:T(8,128)(2,1)S(1)}, bf16[1,8,32,256]{3,2,1,0:T(8,128)(2,1)S(1)}, u32[]{:S(2)}, u32[]{:S(2)}) collective-permute-start(bf16[1,8,32,256]{3,2,1,0:T(8,128)(2,1)S(1)} %copy-done.11), channel_id=1, source_target_pairs={{0,1},{1,2},{2,3},{3,4},{4,5},{5,6},{6,7},{8,9},{9,10},{10,11},{11... | collective-permute-start | bytes 393224 | tf_op jit(solution)/shard_map/ppermute | solution.py:407
  54.4 12.4 %collective-permute-done.3.part_ref = bf16[1,8,32,256]{3,2,1,0:T(8,128)(2,1)S(1)} collective-permute-done((bf16[1,8,32,256]{3,2,1,0:T(8,128)(2,1)S(1)}, bf16[1,8,32,256]{3,2,1,0:T(8,128)(2,1)S(1)}, u32[]{:S(2)}, u32[]{:S(2)}) %collective-permute-start.3) | collective-permute-done | bytes 131104 | tf_op jit(solution)/shard_map/ppermute | solution.py:407
  66.9 2.8 %all-to-all-done.in_ref = bf16[32,176,128]{2,1,0:T(8,128)(2,1)S(1)} async-done(((bf16[32,176,128]{2,1,0:T(8,128)(2,1)}), bf16[32,176,128]{2,1,0:T(8,128)(2,1)S(1)}, u32[]{:S(2)}, u32[]{:S(2)}) %all-to-all-start) | async-done | bytes 1441824 | tf_op jit(solution)/shard_map/all_to_all | solution.py:415
  69.9 1.3 %collective-permute-start.4 = (bf16[2,16,32,256]{3,2,1,0:T(8,128)(2,1)}, bf16[2,16,32,256]{3,2,1,0:T(8,128)(2,1)S(1)}, u32[]{:S(2)}, u32[]{:S(2)}) collective-permute-start(bf16[2,16,32,256]{3,2,1,0:T(8,128)(2,1)} %slice.11), channel_id=1, source_target_pairs={{1,0},{2,1},{3,2},{4,3},{5,4},{6,5},{7,6},{9,8},{10,9},{11,10},{12... | collective-permute-start | bytes 1572872 | tf_op jit(solution)/shard_map/ppermute | solution.py:407
  71.2 14.9 %all_to_all.15.in_ref = bf16[4,176,128]{2,1,0:T(8,128)(2,1)S(1)} all-to-all(bf16[4,176,128]{2,1,0:T(8,128)(2,1)S(1)} %shard_map.86), channel_id=1, replica_groups=mesh['xl'=2,'zh'=4,'zl'=2,'c'=2,'y'=4,'xh'=2] {'zh'}, dimensions={0} | all-to-all | bytes 360448 | tf_op jit(solution)/shard_map/all_to_all | solution.py:415
  86.1 1.2 shard_map.87
  88.1 9.8 %all-to-all-start.2 = ((bf16[32,176,128]{2,1,0:T(8,128)(2,1)}), bf16[32,176,128]{2,1,0:T(8,128)(2,1)S(1)}, u32[]{:S(2)}, u32[]{:S(2)}) async-start(bf16[32,176,128]{2,1,0:T(8,128)(2,1)} %shard_map.87), calls=%async_computation.2 | async-start | bytes 2883584 | tf_op jit(solution)/shard_map/all_to_all | solution.py:415
  100.9 6.3 %shard_map.88 = (bf16[4,16,64,128]{3,2,1,0:T(8,128)(2,1)}, bf16[2,8,32,256]{3,2,1,0:T(8,128)(2,1)}) custom-call(bf16[4,16,32,256]{3,2,1,0:T(8,128)(2,1)S(1)} %copy-done.5, bf16[2,16,32,256]{3,2,1,0:T(8,128)(2,1)S(1)} %copy-done.7, bf16[27,128,128]{2,1,0:T(8,128)(2,1)S(1)} %bitcast.22, f32[8,32,256]{2,1,0:T(8,128)S(1)} %copy-done.9, ...), custom_call_target="tpu_custom_call" | custom-call | flops 5000000000 | bytes 5000000 | tf_op jit(solution)/shard_map/pallas_call | solution.py:305
  107.2 8.2 %all-to-all-done.2 = bf16[32,176,128]{2,1,0:T(8,128)(2,1)S(1)} async-done(((bf16[32,176,128]{2,1,0:T(8,128)(2,1)}), bf16[32,176,128]{2,1,0:T(8,128)(2,1)S(1)}, u32[]{:S(2)}, u32[]{:S(2)}) %all-to-all-start.2) | async-done | bytes 1441824 | tf_op jit(solution)/shard_map/all_to_all | solution.py:415
  115.4 5.3 %collective-permute-start.5 = (bf16[5632,128]{1,0:T(8,128)(2,1)S(1)}, bf16[5632,128]{1,0:T(8,128)(2,1)S(1)}, u32[]{:S(2)}, u32[]{:S(2)}) collective-permute-start(bf16[5632,128]{1,0:T(8,128)(2,1)S(1)} %bitcast.18), channel_id=1, source_target_pairs={{0,8},{8,0},{1,9},{9,1},{2,10},{10,2},{3,11},{11,3},{4,12},{12,4},... | collective-permute-start | bytes 4325384 | tf_op jit(solution)/shard_map/ppermute | solution.py:411
  120.7 1.6 %shard_map.89 = (f32[27,128,128]{2,1,0:T(8,128)}, f32[27,128,256]{2,1,0:T(8,128)}) custom-call(s32[1]{0:T(128)} %bitcast.core_ref, bf16[5632,128]{1,0:T(8,128)(2,1)S(1)} %bitcast.19), custom_call_target="tpu_custom_call" | custom-call | flops 1000000 | bytes 4000000 | tf_op jit(solution)/shard_map/pallas_call | solution.py:365
  122.2 1.3 %collective-permute-done.5.src = bf16[5632,128]{1,0:T(8,128)(2,1)S(1)} collective-permute-done((bf16[5632,128]{1,0:T(8,128)(2,1)S(1)}, bf16[5632,128]{1,0:T(8,128)(2,1)S(1)}, u32[]{:S(2)}, u32[]{:S(2)}) %collective-permute-start.5) | collective-permute-done | bytes 1441824 | tf_op jit(solution)/shard_map/ppermute | solution.py:411
  123.5 1.6 %shard_map.90 = (f32[27,128,128]{2,1,0:T(8,128)}, f32[27,128,256]{2,1,0:T(8,128)}) custom-call(s32[1]{0:T(128)} %bitcast.core_ref, bf16[5632,128]{1,0:T(8,128)(2,1)S(1)} %collective-permute-done.5.src, f32[27,128,128]{2,1,0:T(8,128)} %get-tuple-element.62.conv_in, ...), custom_call_target="tpu_custom_call", output_to_operand_aliasing={{0}: (2, {}), {1}: (3, {})} | custom-call | flops 1000000 | bytes 4000000 | tf_op jit(solution)/shard_map/pallas_call | solution.py:365
  (34 shorter events, 7.0 us)
Async XLA Ops:
  0.6 9.8 %copy-start = (bf16[3,3,3,128,256]{4,3,2,1,0:T(8,128)(2,1)S(1)}, bf16[3,3,3,128,256]{4,3,2,1,0:T(8,128)(2,1)}, u32[]{:S(2)}) copy-start(bf16[3,3,3,128,256]{4,3,2,1,0:T(8,128)(2,1)} %param.9) | copy-start | bytes 5308420
  1.9 20.8 %collective-permute-start = (bf16[2,16,64,128]{3,2,1,0:T(8,128)(2,1)S(1)}, bf16[2,16,64,128]{3,2,1,0:T(8,128)(2,1)S(1)}, u32[]{:S(2)}, u32[]{:S(2)}) collective-permute-start(bf16[2,16,64,128]{3,2,1,0:T(8,128)(2,1)S(1)} %slice_bitcast_fusion), channel_id=1, source_target_pairs={{0,1},{1,2},{2,3},{3,4},{4,5},{5,6},{6,7},{8,9},{9,10},{10,11},{11... | collective-permute-start | bytes 1572872 | tf_op jit(solution)/shard_map/ppermute | solution.py:407
  9.1 13.6 %collective-permute-start.1 = (bf16[1,8,32,256]{3,2,1,0:T(8,128)(2,1)S(1)}, bf16[1,8,32,256]{3,2,1,0:T(8,128)(2,1)S(1)}, u32[]{:S(2)}, u32[]{:S(2)}) collective-permute-start(bf16[1,8,32,256]{3,2,1,0:T(8,128)(2,1)S(1)} %slice.12), channel_id=1, source_target_pairs={{1,0},{2,1},{3,2},{4,3},{5,4},{6,5},{7,6},{9,8},{10,9},{11,10},{12... | collective-permute-start | bytes 393224 | tf_op jit(solution)/shard_map/ppermute | solution.py:407
  10.4 1.2 copy-start.1
  11.6 1.2 copy-start.2
  17.4 17.3 %copy-start.10 = (bf16[1,8,32,256]{3,2,1,0:T(8,128)(2,1)}, bf16[1,8,32,256]{3,2,1,0:T(8,128)(2,1)S(1)}, u32[]{:S(2)}) copy-start(bf16[1,8,32,256]{3,2,1,0:T(8,128)(2,1)S(1)} %get-tuple-element.47) | copy-start | bytes 393220
  34.7 6.0 %copy-start.4 = (bf16[4,16,32,256]{3,2,1,0:T(8,128)(2,1)}, bf16[4,16,32,256]{3,2,1,0:T(8,128)(2,1)S(1)}, u32[]{:S(2)}) copy-start(bf16[4,16,32,256]{3,2,1,0:T(8,128)(2,1)S(1)} %get-tuple-element.49.h_ref) | copy-start | bytes 3145732
  34.7 6.0 %copy-start.8 = (f32[8,32,256]{2,1,0:T(8,128)}, f32[8,32,256]{2,1,0:T(8,128)S(1)}, u32[]{:S(2)}) copy-start(f32[8,32,256]{2,1,0:T(8,128)S(1)} %get-tuple-element.54.even_ref) | copy-start | bytes 786436
  34.7 4.5 %collective-permute-start.2 = (bf16[5632,128]{1,0:T(8,128)(2,1)S(1)}, bf16[5632,128]{1,0:T(8,128)(2,1)S(1)}, u32[]{:S(2)}, u32[]{:S(2)}) collective-permute-start(bf16[5632,128]{1,0:T(8,128)(2,1)S(1)} %get-tuple-element.44), channel_id=1, source_target_pairs={{0,8},{8,0},{1,9},{9,1},{2,10},{10,2},{3,11},{11,3},{4,12},{12,4},... | collective-permute-start | bytes 4325384 | tf_op jit(solution)/shard_map/ppermute | solution.py:411
  40.7 8.3 %copy-start.11 = (bf16[1,8,32,256]{3,2,1,0:T(8,128)(2,1)S(1)}, bf16[1,8,32,256]{3,2,1,0:T(8,128)(2,1)}, u32[]{:S(2)}) copy-start(bf16[1,8,32,256]{3,2,1,0:T(8,128)(2,1)} %copy-done.10) | copy-start | bytes 393220
  40.7 12.9 %copy-start.5 = (bf16[4,16,32,256]{3,2,1,0:T(8,128)(2,1)S(1)}, bf16[4,16,32,256]{3,2,1,0:T(8,128)(2,1)}, u32[]{:S(2)}) copy-start(bf16[4,16,32,256]{3,2,1,0:T(8,128)(2,1)} %copy-done.4) | copy-start | bytes 3145732
  40.7 29.0 %all-to-all-start = ((bf16[32,176,128]{2,1,0:T(8,128)(2,1)}), bf16[32,176,128]{2,1,0:T(8,128)(2,1)S(1)}, u32[]{:S(2)}, u32[]{:S(2)}) async-start(bf16[32,176,128]{2,1,0:T(8,128)(2,1)} %bitcast.23), calls=%async_computation | async-start | bytes 2883584 | tf_op jit(solution)/shard_map/all_to_all | solution.py:415
  48.9 17.9 %collective-permute-start.3 = (bf16[1,8,32,256]{3,2,1,0:T(8,128)(2,1)S(1)}, bf16[1,8,32,256]{3,2,1,0:T(8,128)(2,1)S(1)}, u32[]{:S(2)}, u32[]{:S(2)}) collective-permute-start(bf16[1,8,32,256]{3,2,1,0:T(8,128)(2,1)S(1)} %copy-done.11), channel_id=1, source_target_pairs={{0,1},{1,2},{2,3},{3,4},{4,5},{5,6},{6,7},{8,9},{9,10},{10,11},{11... | collective-permute-start | bytes 393224 | tf_op jit(solution)/shard_map/ppermute | solution.py:407
  66.9 19.2 %copy-start.12 = (bf16[1,8,32,256]{3,2,1,0:T(8,128)(2,1)}, bf16[1,8,32,256]{3,2,1,0:T(8,128)(2,1)S(1)}, u32[]{:S(2)}) copy-start(bf16[1,8,32,256]{3,2,1,0:T(8,128)(2,1)S(1)} %collective-permute-done.3.part_ref) | copy-start | bytes 393220
  69.9 17.4 %collective-permute-start.4 = (bf16[2,16,32,256]{3,2,1,0:T(8,128)(2,1)}, bf16[2,16,32,256]{3,2,1,0:T(8,128)(2,1)S(1)}, u32[]{:S(2)}, u32[]{:S(2)}) collective-permute-start(bf16[2,16,32,256]{3,2,1,0:T(8,128)(2,1)} %slice.11), channel_id=1, source_target_pairs={{1,0},{2,1},{3,2},{4,3},{5,4},{6,5},{7,6},{9,8},{10,9},{11,10},{12... | collective-permute-start | bytes 1572872 | tf_op jit(solution)/shard_map/ppermute | solution.py:407
  87.3 10.6 %copy-start.3 = (bf16[3,3,3,128,128]{4,3,2,1,0:T(8,128)(2,1)S(1)}, bf16[3,3,3,128,128]{4,3,2,1,0:T(8,128)(2,1)}, u32[]{:S(2)}) copy-start(bf16[3,3,3,128,128]{4,3,2,1,0:T(8,128)(2,1)} %param.8) | copy-start | bytes 2654212
  87.3 0.8 copy-start.6
  88.1 27.2 %all-to-all-start.2 = ((bf16[32,176,128]{2,1,0:T(8,128)(2,1)}), bf16[32,176,128]{2,1,0:T(8,128)(2,1)S(1)}, u32[]{:S(2)}, u32[]{:S(2)}) async-start(bf16[32,176,128]{2,1,0:T(8,128)(2,1)} %shard_map.87), calls=%async_computation.2 | async-start | bytes 2883584 | tf_op jit(solution)/shard_map/all_to_all | solution.py:415
  98.0 1.0 copy-start.7
  99.0 0.9 copy-start.9
  100.0 0.9 copy-start.13
  115.4 8.2 %collective-permute-start.5 = (bf16[5632,128]{1,0:T(8,128)(2,1)S(1)}, bf16[5632,128]{1,0:T(8,128)(2,1)S(1)}, u32[]{:S(2)}, u32[]{:S(2)}) collective-permute-start(bf16[5632,128]{1,0:T(8,128)(2,1)S(1)} %bitcast.18), channel_id=1, source_target_pairs={{0,8},{8,0},{1,9},{9,1},{2,10},{10,2},{3,11},{11,3},{4,12},{12,4},... | collective-permute-start | bytes 4325384 | tf_op jit(solution)/shard_map/ppermute | solution.py:411

commit v6 on v4

--- a/solution.py
+++ b/solution.py
@@ -11,7 +11,7 @@
 
 TM = ("y", "xh")
 DP = ("xl", "zh", "zl", "c")
-NEAR = ("zl", "y", "xl", "xh")
+NEAR = ("zl", "xl", "xh", "y")
 
 BF = jnp.bfloat16
 F32 = jnp.float32

time: 124 us -> 124 us (level)
  starting transfers between devices: 37.5 us -> 39.7 us
  waiting for transfers between devices: 31.2 us -> 29.3 us
    all_to_all x2, starting transfers between devices: 17.9 us -> 20.9 us  [exchange(): return lax.all_to_all(value, axes, 0, 0, tiled=True)]
    all_to_all x2, waiting for transfers between devices: 10.2 us -> 8.18 us  [exchange(): return lax.all_to_all(value, axes, 0, 0, tiled=True)]
where the time goes in v6:
time: 124 us; the launch traced here: 123 us
  starting transfers between devices  39.7 us (32%)
  waiting for transfers between devices  29.3 us (24%)
  Pallas kernels  27.2 us (22%)
  blocking collectives  14.9 us (12%)
  local copies, waits for them, and re-layouts  8.15 us (7%)
  other arithmetic  2.48 us (2%)
  between operations  1.65 us (1%)
    all_to_all x2, starting transfers between devices, exchange(): return lax.all_to_all(value, axes, 0, 0, tiled=True)  20.9 us
    ppermute x4, waiting for transfers between devices, shifted(): return lax.ppermute(block, TM, route)  17.1 us
    all_to_all x1, blocking collectives, exchange(): return lax.all_to_all(value, axes, 0, 0, tiled=True)  14.9 us
    ppermute x4, starting transfers between devices, shifted(): return lax.ppermute(block, TM, route)  12.7 us
    pallas_call x1, Pallas kernels, call_grads(): pl.pallas_call(kernel_grads, out_shape=(jax.ShapeDtypeStruct((4, 16, 32,...  11.8 us
    all_to_all x2, waiting for transfers between devices, exchange(): return lax.all_to_all(value, axes, 0, 0, tiled=True)  8.18 us
    pallas_call x1, Pallas kernels, call_clip(): pl.pallas_call(kernel_clip, out_shape=(jax.ShapeDtypeStruct((4, 16, 64, 1...  6.28 us
    unnamed x28, local copies, waits for them, and re-layouts  6.11 us
  transfers between devices with their start and end apart: 8, of which 6 were waited for; matrix products, arithmetic and copies ran while one was open for 2% of the time, Pallas kernels for 11%

profile of v6, /device:TPU:1, one launch (start us, length us, event | category | flops | bytes accessed | tf_op | source)
XLA Modules:
  0.0 123.3 jit_solution(2376626897719066)
XLA Ops:
  0.6 1.2 slice_bitcast_fusion
  1.9 5.5 %collective-permute-start = (bf16[2,16,64,128]{3,2,1,0:T(8,128)(2,1)S(1)}, bf16[2,16,64,128]{3,2,1,0:T(8,128)(2,1)S(1)}, u32[]{:S(2)}, u32[]{:S(2)}) collective-permute-start(bf16[2,16,64,128]{3,2,1,0:T(8,128)(2,1)S(1)} %slice_bitcast_fusion), channel_id=1, source_target_pairs={{0,1},{1,2},{2,3},{3,4},{4,5},{5,6},{6,7},{8,9},{9,10},{10,11},{11... | collective-permute-start | bytes 1572872 | tf_op jit(solution)/shard_map/ppermute | solution.py:407
  9.1 1.3 %collective-permute-start.1 = (bf16[1,8,32,256]{3,2,1,0:T(8,128)(2,1)S(1)}, bf16[1,8,32,256]{3,2,1,0:T(8,128)(2,1)S(1)}, u32[]{:S(2)}, u32[]{:S(2)}) collective-permute-start(bf16[1,8,32,256]{3,2,1,0:T(8,128)(2,1)S(1)} %slice.12), channel_id=1, source_target_pairs={{1,0},{2,1},{3,2},{4,3},{5,4},{6,5},{7,6},{9,8},{10,9},{11,10},{12... | collective-permute-start | bytes 393224 | tf_op jit(solution)/shard_map/ppermute | solution.py:407
  10.4 1.2 copy-done.1
  11.6 1.2 copy-done.2
  12.8 4.6 %shard_map.84 = (bf16[9,512,256]{2,1,0:T(8,128)(2,1)S(1)}, bf16[9,512,256]{2,1,0:T(8,128)(2,1)S(1)}, bf16[4,18,32,512]{3,2,1,0:T(8,128)(2,1)S(1)}, bf16[2,9,2,32...) custom-call(bf16[4,16,64,128]{3,2,1,0:T(8,128)(2,1)S(1)} %bitcast.20, ...), custom_call_target="tpu_custom_call" | custom-call | flops 1000000 | bytes 1000000 | tf_op jit(solution)/shard_map/pallas_call | solution.py:170
  17.4 5.3 %collective-permute-done.1.next_ref = bf16[1,8,32,256]{3,2,1,0:T(8,128)(2,1)S(1)} collective-permute-done((bf16[1,8,32,256]{3,2,1,0:T(8,128)(2,1)S(1)}, bf16[1,8,32,256]{3,2,1,0:T(8,128)(2,1)S(1)}, u32[]{:S(2)}, u32[]{:S(2)}) %collective-permute-start.1) | collective-permute-done | bytes 131104 | tf_op jit(solution)/shard_map/ppermute | solution.py:407
  22.7 11.8 %shard_map.85 = (bf16[4,16,32,256]{3,2,1,0:T(8,128)(2,1)S(1)}, bf16[5376,128]{1,0:T(8,128)(2,1)S(1)}, bf16[5376,128]{1,0:T(8,128)(2,1)S(1)}, f32[8,32,256]{2,1,0:T(8,128)S(1)}, bf16[8,32,256]{2,1,0:T(8,128)(2,1)S(1)}) custom-call(s32[1]{0:T(128)} %bitcast.core_ref, bf16[2,16,64,128]{3,2,1,0:T(8,128)(2,1)S(1)} %collective-permute-done.before_ref, ...), custom_call_target="tpu_custom_call" | custom-call | flops 1000000 | bytes 1000000 | tf_op jit(solution)/shard_map/pallas_call | solution.py:260
  34.5 1.6 %collective-permute-start.2 = (bf16[5376,128]{1,0:T(8,128)(2,1)S(1)}, bf16[5376,128]{1,0:T(8,128)(2,1)S(1)}, u32[]{:S(2)}, u32[]{:S(2)}) collective-permute-start(bf16[5376,128]{1,0:T(8,128)(2,1)S(1)} %get-tuple-element.44), channel_id=1, source_target_pairs={{0,8},{8,0},{1,9},{9,1},{2,10},{10,2},{3,11},{11,3},{4,12},{12,4},... | collective-permute-start | bytes 4128776 | tf_op jit(solution)/shard_map/ppermute | solution.py:411
  36.2 2.8 %collective-permute-done.2 = bf16[5376,128]{1,0:T(8,128)(2,1)S(1)} collective-permute-done((bf16[5376,128]{1,0:T(8,128)(2,1)S(1)}, bf16[5376,128]{1,0:T(8,128)(2,1)S(1)}, u32[]{:S(2)}, u32[]{:S(2)}) %collective-permute-start.2) | collective-permute-done | bytes 1376288 | tf_op jit(solution)/shard_map/ppermute | solution.py:411
  38.9 1.4 %add_convert_fusion = bf16[5376,128]{1,0:T(8,128)(2,1)} fusion(bf16[5376,128]{1,0:T(8,128)(2,1)S(1)} %collective-permute-done.2, bf16[5376,128]{1,0:T(8,128)(2,1)S(1)} %get-tuple-element.43), kind=kLoop, calls=%fused_computation | loop fusion | flops 2752512 | bytes 4128768 | tf_op jit(solution)/shard_map/convert_element_type | solution.py:434
  40.4 8.2 %all-to-all-start = ((bf16[32,168,128]{2,1,0:T(8,128)(2,1)}), bf16[32,168,128]{2,1,0:T(8,128)(2,1)S(1)}, u32[]{:S(2)}, u32[]{:S(2)}) async-start(bf16[32,168,128]{2,1,0:T(8,128)(2,1)} %bitcast.23), calls=%async_computation | async-start | bytes 2752512 | tf_op jit(solution)/shard_map/all_to_all | solution.py:415
  48.6 4.6 %collective-permute-start.3 = (bf16[1,8,32,256]{3,2,1,0:T(8,128)(2,1)S(1)}, bf16[1,8,32,256]{3,2,1,0:T(8,128)(2,1)S(1)}, u32[]{:S(2)}, u32[]{:S(2)}) collective-permute-start(bf16[1,8,32,256]{3,2,1,0:T(8,128)(2,1)S(1)} %copy-done.11), channel_id=1, source_target_pairs={{0,1},{1,2},{2,3},{3,4},{4,5},{5,6},{6,7},{8,9},{9,10},{10,11},{11... | collective-permute-start | bytes 393224 | tf_op jit(solution)/shard_map/ppermute | solution.py:407
  54.1 11.8 %collective-permute-done.3.part_ref = bf16[1,8,32,256]{3,2,1,0:T(8,128)(2,1)S(1)} collective-permute-done((bf16[1,8,32,256]{3,2,1,0:T(8,128)(2,1)S(1)}, bf16[1,8,32,256]{3,2,1,0:T(8,128)(2,1)S(1)}, u32[]{:S(2)}, u32[]{:S(2)}) %collective-permute-start.3) | collective-permute-done | bytes 131104 | tf_op jit(solution)/shard_map/ppermute | solution.py:407
  67.2 1.3 %collective-permute-start.4 = (bf16[2,16,32,256]{3,2,1,0:T(8,128)(2,1)}, bf16[2,16,32,256]{3,2,1,0:T(8,128)(2,1)S(1)}, u32[]{:S(2)}, u32[]{:S(2)}) collective-permute-start(bf16[2,16,32,256]{3,2,1,0:T(8,128)(2,1)} %slice.11), channel_id=1, source_target_pairs={{1,0},{2,1},{3,2},{4,3},{5,4},{6,5},{7,6},{9,8},{10,9},{11,10},{12... | collective-permute-start | bytes 1572872 | tf_op jit(solution)/shard_map/ppermute | solution.py:407
  68.5 14.9 %all_to_all.15.in_ref = bf16[4,168,128]{2,1,0:T(8,128)(2,1)S(1)} all-to-all(bf16[4,168,128]{2,1,0:T(8,128)(2,1)S(1)} %shard_map.86), channel_id=1, replica_groups=mesh['xl'=2,'zh'=4,'zl'=2,'c'=2,'y'=4,'xh'=2] {'zh'}, dimensions={0} | all-to-all | bytes 344064 | tf_op jit(solution)/shard_map/all_to_all | solution.py:415
  83.4 1.2 shard_map.87
  85.3 12.6 %all-to-all-start.2 = ((bf16[32,168,128]{2,1,0:T(8,128)(2,1)}), bf16[32,168,128]{2,1,0:T(8,128)(2,1)S(1)}, u32[]{:S(2)}, u32[]{:S(2)}) async-start(bf16[32,168,128]{2,1,0:T(8,128)(2,1)} %shard_map.87), calls=%async_computation.2 | async-start | bytes 2752512 | tf_op jit(solution)/shard_map/all_to_all | solution.py:415
  100.9 6.3 %shard_map.88 = (bf16[4,16,64,128]{3,2,1,0:T(8,128)(2,1)}, bf16[2,8,32,256]{3,2,1,0:T(8,128)(2,1)}) custom-call(bf16[4,16,32,256]{3,2,1,0:T(8,128)(2,1)S(1)} %copy-done.5, bf16[2,16,32,256]{3,2,1,0:T(8,128)(2,1)S(1)} %copy-done.7, bf16[27,128,128]{2,1,0:T(8,128)(2,1)S(1)} %bitcast.22, f32[8,32,256]{2,1,0:T(8,128)S(1)} %copy-done.9, ...), custom_call_target="tpu_custom_call" | custom-call | flops 5000000000 | bytes 5000000 | tf_op jit(solution)/shard_map/pallas_call | solution.py:305
  107.2 7.2 %all-to-all-done.2 = bf16[32,168,128]{2,1,0:T(8,128)(2,1)S(1)} async-done(((bf16[32,168,128]{2,1,0:T(8,128)(2,1)}), bf16[32,168,128]{2,1,0:T(8,128)(2,1)S(1)}, u32[]{:S(2)}, u32[]{:S(2)}) %all-to-all-start.2) | async-done | bytes 1376288 | tf_op jit(solution)/shard_map/all_to_all | solution.py:415
  114.3 4.4 %collective-permute-start.5 = (bf16[5376,128]{1,0:T(8,128)(2,1)S(1)}, bf16[5376,128]{1,0:T(8,128)(2,1)S(1)}, u32[]{:S(2)}, u32[]{:S(2)}) collective-permute-start(bf16[5376,128]{1,0:T(8,128)(2,1)S(1)} %bitcast.18), channel_id=1, source_target_pairs={{0,8},{8,0},{1,9},{9,1},{2,10},{10,2},{3,11},{11,3},{4,12},{12,4},... | collective-permute-start | bytes 4128776 | tf_op jit(solution)/shard_map/ppermute | solution.py:411
  118.8 1.6 %shard_map.89 = (f32[27,128,128]{2,1,0:T(8,128)}, f32[27,128,256]{2,1,0:T(8,128)}) custom-call(s32[1]{0:T(128)} %bitcast.core_ref, bf16[5376,128]{1,0:T(8,128)(2,1)S(1)} %bitcast.19), custom_call_target="tpu_custom_call" | custom-call | flops 1000000 | bytes 4000000 | tf_op jit(solution)/shard_map/pallas_call | solution.py:365
  120.4 1.2 collective-permute-done.5.src
  121.5 1.6 %shard_map.90 = (f32[27,128,128]{2,1,0:T(8,128)}, f32[27,128,256]{2,1,0:T(8,128)}) custom-call(s32[1]{0:T(128)} %bitcast.core_ref, bf16[5376,128]{1,0:T(8,128)(2,1)S(1)} %collective-permute-done.5.src, f32[27,128,128]{2,1,0:T(8,128)} %get-tuple-element.62.conv_in, ...), custom_call_target="tpu_custom_call", output_to_operand_aliasing={{0}: (2, {}), {1}: (3, {})} | custom-call | flops 1000000 | bytes 4000000 | tf_op jit(solution)/shard_map/pallas_call | solution.py:365
  (34 shorter events, 6.8 us)
Async XLA Ops:
  0.6 9.8 %copy-start = (bf16[3,3,3,128,256]{4,3,2,1,0:T(8,128)(2,1)S(1)}, bf16[3,3,3,128,256]{4,3,2,1,0:T(8,128)(2,1)}, u32[]{:S(2)}) copy-start(bf16[3,3,3,128,256]{4,3,2,1,0:T(8,128)(2,1)} %param.9) | copy-start | bytes 5308420
  1.9 20.8 %collective-permute-start = (bf16[2,16,64,128]{3,2,1,0:T(8,128)(2,1)S(1)}, bf16[2,16,64,128]{3,2,1,0:T(8,128)(2,1)S(1)}, u32[]{:S(2)}, u32[]{:S(2)}) collective-permute-start(bf16[2,16,64,128]{3,2,1,0:T(8,128)(2,1)S(1)} %slice_bitcast_fusion), channel_id=1, source_target_pairs={{0,1},{1,2},{2,3},{3,4},{4,5},{5,6},{6,7},{8,9},{9,10},{10,11},{11... | collective-permute-start | bytes 1572872 | tf_op jit(solution)/shard_map/ppermute | solution.py:407
  9.1 13.6 %collective-permute-start.1 = (bf16[1,8,32,256]{3,2,1,0:T(8,128)(2,1)S(1)}, bf16[1,8,32,256]{3,2,1,0:T(8,128)(2,1)S(1)}, u32[]{:S(2)}, u32[]{:S(2)}) collective-permute-start(bf16[1,8,32,256]{3,2,1,0:T(8,128)(2,1)S(1)} %slice.12), channel_id=1, source_target_pairs={{1,0},{2,1},{3,2},{4,3},{5,4},{6,5},{7,6},{9,8},{10,9},{11,10},{12... | collective-permute-start | bytes 393224 | tf_op jit(solution)/shard_map/ppermute | solution.py:407
  10.4 1.2 copy-start.1
  11.6 1.2 copy-start.2
  17.4 17.1 %copy-start.10 = (bf16[1,8,32,256]{3,2,1,0:T(8,128)(2,1)}, bf16[1,8,32,256]{3,2,1,0:T(8,128)(2,1)S(1)}, u32[]{:S(2)}) copy-start(bf16[1,8,32,256]{3,2,1,0:T(8,128)(2,1)S(1)} %get-tuple-element.47) | copy-start | bytes 393220
  34.5 5.9 %copy-start.4 = (bf16[4,16,32,256]{3,2,1,0:T(8,128)(2,1)}, bf16[4,16,32,256]{3,2,1,0:T(8,128)(2,1)S(1)}, u32[]{:S(2)}) copy-start(bf16[4,16,32,256]{3,2,1,0:T(8,128)(2,1)S(1)} %get-tuple-element.49.h_ref) | copy-start | bytes 3145732
  34.5 5.8 %copy-start.8 = (f32[8,32,256]{2,1,0:T(8,128)}, f32[8,32,256]{2,1,0:T(8,128)S(1)}, u32[]{:S(2)}) copy-start(f32[8,32,256]{2,1,0:T(8,128)S(1)} %get-tuple-element.54.even_ref) | copy-start | bytes 786436
  34.5 4.4 %collective-permute-start.2 = (bf16[5376,128]{1,0:T(8,128)(2,1)S(1)}, bf16[5376,128]{1,0:T(8,128)(2,1)S(1)}, u32[]{:S(2)}, u32[]{:S(2)}) collective-permute-start(bf16[5376,128]{1,0:T(8,128)(2,1)S(1)} %get-tuple-element.44), channel_id=1, source_target_pairs={{0,8},{8,0},{1,9},{9,1},{2,10},{10,2},{3,11},{11,3},{4,12},{12,4},... | collective-permute-start | bytes 4128776 | tf_op jit(solution)/shard_map/ppermute | solution.py:411
  40.4 8.3 %copy-start.11 = (bf16[1,8,32,256]{3,2,1,0:T(8,128)(2,1)S(1)}, bf16[1,8,32,256]{3,2,1,0:T(8,128)(2,1)}, u32[]{:S(2)}) copy-start(bf16[1,8,32,256]{3,2,1,0:T(8,128)(2,1)} %copy-done.10) | copy-start | bytes 393220
  40.4 12.9 %copy-start.5 = (bf16[4,16,32,256]{3,2,1,0:T(8,128)(2,1)S(1)}, bf16[4,16,32,256]{3,2,1,0:T(8,128)(2,1)}, u32[]{:S(2)}) copy-start(bf16[4,16,32,256]{3,2,1,0:T(8,128)(2,1)} %copy-done.4) | copy-start | bytes 3145732
  40.4 26.6 %all-to-all-start = ((bf16[32,168,128]{2,1,0:T(8,128)(2,1)}), bf16[32,168,128]{2,1,0:T(8,128)(2,1)S(1)}, u32[]{:S(2)}, u32[]{:S(2)}) async-start(bf16[32,168,128]{2,1,0:T(8,128)(2,1)} %bitcast.23), calls=%async_computation | async-start | bytes 2752512 | tf_op jit(solution)/shard_map/all_to_all | solution.py:415
  48.6 17.3 %collective-permute-start.3 = (bf16[1,8,32,256]{3,2,1,0:T(8,128)(2,1)S(1)}, bf16[1,8,32,256]{3,2,1,0:T(8,128)(2,1)S(1)}, u32[]{:S(2)}, u32[]{:S(2)}) collective-permute-start(bf16[1,8,32,256]{3,2,1,0:T(8,128)(2,1)S(1)} %copy-done.11), channel_id=1, source_target_pairs={{0,1},{1,2},{2,3},{3,4},{4,5},{5,6},{6,7},{8,9},{9,10},{10,11},{11... | collective-permute-start | bytes 393224 | tf_op jit(solution)/shard_map/ppermute | solution.py:407
  66.0 17.4 %copy-start.12 = (bf16[1,8,32,256]{3,2,1,0:T(8,128)(2,1)}, bf16[1,8,32,256]{3,2,1,0:T(8,128)(2,1)S(1)}, u32[]{:S(2)}) copy-start(bf16[1,8,32,256]{3,2,1,0:T(8,128)(2,1)S(1)} %collective-permute-done.3.part_ref) | copy-start | bytes 393220
  67.2 17.4 %collective-permute-start.4 = (bf16[2,16,32,256]{3,2,1,0:T(8,128)(2,1)}, bf16[2,16,32,256]{3,2,1,0:T(8,128)(2,1)S(1)}, u32[]{:S(2)}, u32[]{:S(2)}) collective-permute-start(bf16[2,16,32,256]{3,2,1,0:T(8,128)(2,1)} %slice.11), channel_id=1, source_target_pairs={{1,0},{2,1},{3,2},{4,3},{5,4},{6,5},{7,6},{9,8},{10,9},{11,10},{12... | collective-permute-start | bytes 1572872 | tf_op jit(solution)/shard_map/ppermute | solution.py:407
  84.5 13.4 %copy-start.3 = (bf16[3,3,3,128,128]{4,3,2,1,0:T(8,128)(2,1)S(1)}, bf16[3,3,3,128,128]{4,3,2,1,0:T(8,128)(2,1)}, u32[]{:S(2)}) copy-start(bf16[3,3,3,128,128]{4,3,2,1,0:T(8,128)(2,1)} %param.8) | copy-start | bytes 2654212
  84.5 0.8 copy-start.6
  85.3 29.0 %all-to-all-start.2 = ((bf16[32,168,128]{2,1,0:T(8,128)(2,1)}), bf16[32,168,128]{2,1,0:T(8,128)(2,1)S(1)}, u32[]{:S(2)}, u32[]{:S(2)}) async-start(bf16[32,168,128]{2,1,0:T(8,128)(2,1)} %shard_map.87), calls=%async_computation.2 | async-start | bytes 2752512 | tf_op jit(solution)/shard_map/all_to_all | solution.py:415
  98.0 1.0 copy-start.7
  99.0 0.9 copy-start.9
  100.0 0.9 copy-start.13
  114.3 7.2 %collective-permute-start.5 = (bf16[5376,128]{1,0:T(8,128)(2,1)S(1)}, bf16[5376,128]{1,0:T(8,128)(2,1)S(1)}, u32[]{:S(2)}, u32[]{:S(2)}) collective-permute-start(bf16[5376,128]{1,0:T(8,128)(2,1)S(1)} %bitcast.18), channel_id=1, source_target_pairs={{0,8},{8,0},{1,9},{9,1},{2,10},{10,2},{3,11},{11,3},{4,12},{12,4},... | collective-permute-start | bytes 4128776 | tf_op jit(solution)/shard_map/ppermute | solution.py:411
